TPU v7x, 256 devices: a whole 4x4x8 slice. The times are simulated.
256 devices in a mesh: row: 16 (over z, x_lo), col: 16 (over x_hi, y, core).
Axes of the slice: x: 4 (x_hi: 2, x_lo: 2; x = x_hi * 2 + x_lo), y: 4, z: 8, core: 2. Of those that a mesh axis runs over, the one named last changes fastest.
Arguments:
- cotangent: bfloat16 [2048, 8192], P('col', 'row'), may hold values from -6 to 6
- activations: bfloat16 [2048, 16384], P('row', 'col'), may hold values from -0.125 to 0.125
- down_weight: bfloat16 [16384, 8192], P('col', 'row'), may hold values from -0.046875 to 0.046875
- left_stats: float32 [16, 8192, 1024], P('col', 'row'), may hold values from -6 to 6
- right_stats: float32 [16, 8192, 1024], P('col', 'row'), may hold values from -6 to 6
- left_root: bfloat16 [16, 8192, 1024], P('col', 'row'), may hold values from -0.1875 to 0.1875
- right_root: bfloat16 [16, 1024, 8192], P('col', None, 'row'), may hold values from -0.1875 to 0.1875
Outputs:
- input_grad: bfloat16 [2048, 16384], P('row', 'col')
- update: bfloat16 [16384, 8192], P('col', 'row')
- left_new: float32 [16, 8192, 1024], P('col', 'row')
- right_new: float32 [16, 8192, 1024], P('col', 'row')
All inputs are finite; a program needn't handle non-finite values.
Results may differ from a plain program's by a relative error of at most 0.0057.
Values may be sent and summed in bfloat16 or wider, within the bound.
No kernel may reach another device: no remote copies, remote signals or barrier semaphores. Data moves between devices by JAX's collectives and lax.ppermute only.
A program may use at most 128 MiB of HBM per device.

v0:
```python
import jax
import jax.numpy as jnp
from jax import lax
from jax.sharding import PartitionSpec as P


def from_partner(array, axis, distance):
    return lax.ppermute(array, axis, [(i, i ^ 1 << distance) for i in range(lax.axis_size(axis))])


def join_halves(own_part, partner, high_half, join_axis):
    low_part = jnp.where(high_half, partner, own_part)
    high_part = jnp.where(high_half, own_part, partner)
    return jnp.concatenate([low_part, high_part], axis=join_axis)


def local(cotangent, activations, down_weight, left_stats, right_stats, left_root, right_root):
    ff_dev, d_dev = down_weight.shape
    block_size = left_root.shape[2]
    n_blocks = ff_dev // block_size
    pair_size = block_size // d_dev
    row_index = lax.axis_index("row")
    tok_all = lax.all_gather(cotangent, "col", axis=0, tiled=True)
    tok_rows = tok_all
    weight_grad = lax.dot_general(
        lax.all_gather(activations, "row", axis=0, tiled=True),
        tok_rows,
        (((0,), (0,)), ((), ())),
        preferred_element_type=jnp.float32,
    )
    gradient = weight_grad.astype(jnp.bfloat16)
    tok_rows = tok_all
    input_grad = lax.psum_scatter(
        lax.dot_general(
            tok_rows, down_weight, (((1,), (1,)), ((), ())), preferred_element_type=jnp.float32
        ),
        "row",
        scatter_dimension=0,
        tiled=True,
    ).astype(jnp.bfloat16)
    own_cols = gradient.reshape(n_blocks, block_size, d_dev)
    full_block = own_cols
    bit_level = 0
    high_half = row_index // (1 << bit_level) % 2 == 1
    partner = from_partner(full_block, "row", bit_level)
    full_block = join_halves(full_block, partner, high_half, 2)
    offset = row_index % pair_size * d_dev
    own_rows = lax.dynamic_slice_in_dim(full_block, offset, d_dev, 1)
    left_gram = (
        jnp.einsum("frk,fck->frc", own_rows, full_block, preferred_element_type=jnp.float32)
        / block_size
    )
    left_new = left_stats + left_gram
    right_gram = (
        jnp.einsum("fkr,fkc->frc", own_cols, full_block, preferred_element_type=jnp.float32)
        / block_size
    )
    right_new = right_stats + right_gram
    conditioned = jnp.einsum(
        "frk,fkc->frc", left_root, full_block, preferred_element_type=jnp.float32
    ).astype(jnp.bfloat16)
    bit_level = 0
    high_half = row_index // (1 << bit_level) % 2 == 1
    partner = from_partner(conditioned, "row", bit_level)
    conditioned = join_halves(conditioned, partner, high_half, 1)
    update = jnp.einsum(
        "frk,fkc->frc", conditioned, right_root, preferred_element_type=jnp.float32
    ).astype(jnp.bfloat16)
    return (input_grad, update.reshape(ff_dev, d_dev), left_new, right_new)


def solution(mesh):
    in_specs = (
        P("col", "row"),
        P("row", "col"),
        P("col", "row"),
        P("col", "row", None),
        P("col", "row", None),
        P("col", "row", None),
        P("col", None, "row"),
    )
    out_specs = (P("row", "col"), P("col", "row"), P("col", "row", None), P("col", "row", None))
    return jax.shard_map(local, mesh=mesh, in_specs=in_specs, out_specs=out_specs, check_vma=False)
```

profile of v0, /device:TPU:2, one launch (start us, length us, event | category | flops | bytes accessed | tf_op | source)
XLA Modules:
  0.0 395.3 jit_solution(6226253543873577438)
XLA Ops:
  7.2 0.0 copy-start
  7.2 0.0 all-gather.3.cloned.1.call-start
  7.2 0.7 all-gather.3.cloned.1.call-update
  7.9 0.0 all-gather.5.cloned.1.call-start
  8.0 0.7 all-gather.5.cloned.1.call-update
  8.7 0.0 reduce-scatter.2.cloned.1.call-start
  8.7 56.7 %all-gather.3.cloned.1.call-done = bf16[2048,512]{1,0:T(8,128)(2,1)} async-done(((bf16[128,512]{1,0:T(8,128)(2,1)}), bf16[2048,512]{1,0:T(8,128)(2,1)}) %all-gather.3.cloned.1.call-update) | async-done | bytes 2097168 | tf_op jit(solution)/shard_map/all_gather | solution.py:23
  65.4 7.2 %fusion.19 = f32[2048,1024]{1,0:T(8,128)} fusion(bf16[2048,512]{1,0:T(8,128)(2,1)} %all-gather.3.cloned.1.call-done, bf16[1024,512]{1,0:T(8,128)(2,1)S(1)} %copy-done), kind=kOutput, calls=%fused_computation.27 | convolution fusion | flops 2147483648 | bytes 11534336 | tf_op jit(solution)/shard_map/dot_general | solution.py:34
  72.6 0.0 reduce-scatter.2.cloned.1.call-update
  72.7 92.8 %all-gather.5.cloned.1.call-done = bf16[2048,1024]{1,0:T(8,128)(2,1)} async-done(((bf16[128,1024]{1,0:T(8,128)(2,1)}), bf16[2048,1024]{1,0:T(8,128)(2,1)}) %all-gather.5.cloned.1.call-update) | async-done | bytes 4194320 | tf_op jit(solution)/shard_map/all_gather | solution.py:26
  165.5 5.2 %convolution_convert_fusion.1 = bf16[1024,512]{0,1:T(8,128)(2,1)S(1)} fusion(bf16[2048,1024]{1,0:T(8,128)(2,1)} %all-gather.5.cloned.1.call-done, bf16[2048,512]{1,0:T(8,128)(2,1)} %all-gather.3.cloned.1.call-done), kind=kOutput, calls=%fused_computation.12 | convolution fusion | flops 2148007936 | bytes 7340032 | tf_op jit(solution)/shard_map/dot_general | solution.py:25
  170.7 1.2 collective-permute-start
  172.0 59.8 %collective-permute-done = bf16[1,1024,512]{1,2,0:T(8,128)(2,1)S(1)} collective-permute-done((bf16[1,1024,512]{1,2,0:T(8,128)(2,1)S(1)}, bf16[1,1024,512]{1,2,0:T(8,128)(2,1)S(1)}, u32[]{:S(2)}, u32[]{:S(2)}) %collective-permute-start) | collective-permute-done | bytes 1048608 | tf_op jit(solution)/shard_map/ppermute | solution.py:8
  231.8 0.1 broadcast_select_fusion.1
  231.9 0.0 copy-start.3
  231.9 1.3 fusion.5
  233.3 0.1 collective-permute-start.1
  233.4 5.0 %bitcast_add_fusion = f32[1,512,1024]{2,1,0:T(8,128)} fusion(f32[1,512,1024]{2,1,0:T(8,128)} %param.11, bf16[1024,512]{0,1:T(8,128)(2,1)S(1)} %convolution_convert_fusion.1, bf16[1,1024,512]{1,2,0:T(8,128)(2,1)} %copy-done.3, bf16[1,1024,512]{1,2,0:T(8,128)(2,1)} %copy-done.1), kind=kOutput, calls=%fused_computation.8 | convolution fusion | flops 1078984704 | bytes 7340032 | tf_op jit(solution)/shard_map/fkr,fkc->frc/dot_general | solution.py:55
  238.5 2.6 bitcast_add_fusion.1
  241.1 61.0 %collective-permute-done.1 = bf16[1,512,1024]{2,1,0:T(8,128)(2,1)} collective-permute-done((bf16[1,512,1024]{2,1,0:T(8,128)(2,1)S(1)}, bf16[1,512,1024]{2,1,0:T(8,128)(2,1)}, u32[]{:S(2)}, u32[]{:S(2)}) %collective-permute-start.1) | collective-permute-done | bytes 1048608 | tf_op jit(solution)/shard_map/ppermute | solution.py:8
  302.1 1.4 broadcast_select_fusion.3
  303.5 2.2 fusion.4
  305.7 81.3 %reduce-scatter.2.cloned.1.call-done = f32[128,1024]{1,0:T(8,128)} async-done(((f32[2048,1024]{1,0:T(8,128)}), f32[128,1024]{1,0:T(8,128)}) %reduce-scatter.2.cloned.1.call-update) | async-done | bytes 524304 | tf_op jit(solution)/shard_map/reduce_scatter | solution.py:33
  387.0 1.8 convert_element_type.19
  (14 shorter events, 0.0 us)
Async XLA Ops:
  7.2 58.3 %copy-start = (bf16[1024,512]{1,0:T(8,128)(2,1)S(1)}, bf16[1024,512]{1,0:T(8,128)(2,1)}, u32[]{:S(2)}) copy-start(bf16[1024,512]{1,0:T(8,128)(2,1)} %param.9) | copy-start | bytes 3145732
  7.2 58.2 %all-gather.3.cloned.1.call-start = ((), (), s32[]{:S(2)}) async-start(), calls=%async_computation.1 | async-start | bytes 2228224 | tf_op jit(solution)/shard_map/all_gather | solution.py:23
  7.9 157.6 %all-gather.5.cloned.1.call-start = ((), (), s32[]{:S(2)}) async-start(), calls=%async_computation.3 | async-start | bytes 4456448 | tf_op jit(solution)/shard_map/all_gather | solution.py:26
  8.7 378.3 %reduce-scatter.2.cloned.1.call-start = ((), (), s32[]{:S(2)}) async-start(), calls=%async_computation.2 | async-start | bytes 8912896 | tf_op jit(solution)/shard_map/reduce_scatter | solution.py:33
  170.7 61.0 %collective-permute-start = (bf16[1,1024,512]{1,2,0:T(8,128)(2,1)S(1)}, bf16[1,1024,512]{1,2,0:T(8,128)(2,1)S(1)}, u32[]{:S(2)}, u32[]{:S(2)}) collective-permute-start(bf16[1,1024,512]{1,2,0:T(8,128)(2,1)S(1)} %bitcast.35), channel_id=1, source_target_pairs={{0,16},{16,0},{32,48},{48,32},{64,80},{80,64},{96,112},{112,96},{1... | collective-permute-start | bytes 3145736 | tf_op jit(solution)/shard_map/ppermute | solution.py:8
  172.0 60.0 %copy-start.6 = (bf16[1,512,1024]{2,1,0:T(8,128)(2,1)S(1)}, bf16[1,512,1024]{2,1,0:T(8,128)(2,1)}, u32[]{:S(2)}) copy-start(bf16[1,512,1024]{2,1,0:T(8,128)(2,1)} %param.12) | copy-start | bytes 3145732
  231.9 1.3 copy-start.1
  231.9 1.3 copy-start.3
  233.3 68.8 %collective-permute-start.1 = (bf16[1,512,1024]{2,1,0:T(8,128)(2,1)S(1)}, bf16[1,512,1024]{2,1,0:T(8,128)(2,1)}, u32[]{:S(2)}, u32[]{:S(2)}) collective-permute-start(bf16[1,512,1024]{2,1,0:T(8,128)(2,1)S(1)} %fusion.5), channel_id=1, source_target_pairs={{0,16},{16,0},{32,48},{48,32},{64,80},{80,64},{96,112},{112,96},{1... | collective-permute-start | bytes 3145736 | tf_op jit(solution)/shard_map/ppermute | solution.py:8
  233.4 5.1 %copy-start.2 = (bf16[1,1024,512]{1,2,0:T(8,128)(2,1)S(1)}, bf16[1,1024,512]{1,2,0:T(8,128)(2,1)}, u32[]{:S(2)}) copy-start(bf16[1,1024,512]{1,2,0:T(8,128)(2,1)} %copy-done.1) | copy-start | bytes 3145732
  233.4 5.1 %copy-start.4 = (bf16[1,1024,512]{1,2,0:T(8,128)(2,1)S(1)}, bf16[1,1024,512]{1,2,0:T(8,128)(2,1)}, u32[]{:S(2)}) copy-start(bf16[1,1024,512]{1,2,0:T(8,128)(2,1)} %copy-done.3) | copy-start | bytes 3145732
  233.4 5.1 %copy-start.5 = (f32[1,512,1024]{2,1,0:T(8,128)S(1)}, f32[1,512,1024]{2,1,0:T(8,128)}, u32[]{:S(2)}) copy-start(f32[1,512,1024]{2,1,0:T(8,128)} %param.10) | copy-start | bytes 6291460
  241.1 62.4 %copy-start.7 = (bf16[1,1024,512]{2,1,0:T(8,128)(2,1)S(1)}, bf16[1,1024,512]{2,1,0:T(8,128)(2,1)}, u32[]{:S(2)}) copy-start(bf16[1,1024,512]{2,1,0:T(8,128)(2,1)} %param.13) | copy-start | bytes 3145732
Sparse Core Ops, SparseCore 0:
  10.8 54.6 all-gather.2
  67.2 98.2 all-gather.4
  168.0 218.9 reduce-scatter.1
where the time goes:
time: 397 us; the launch traced here: 395 us
  waiting for transfers between devices  353 us (89%)
  matrix products  23.6 us (6%)
  between operations  13.9 us (4%)
    ppermute x2, waiting for transfers between devices, from_partner(): lax.ppermute(array, axis, [(i, i ^ 1 << distance) for i in range(lax.axis...  121 us
    all_gather x1, waiting for transfers between devices, local(): lax.all_gather(activations, 'row', axis=0, tiled=True)  92.8 us
    reduce_scatter x1, waiting for transfers between devices, local(): lax.psum_scatter(lax.dot_general(tok_rows, down_weight, (((1,), (1,)), ((...  81.3 us
    all_gather x1, waiting for transfers between devices, local(): tok_all = lax.all_gather(cotangent, 'col', axis=0, tiled=True)  56.7 us
  transfers between devices with their start and end apart: 5, of which 5 were waited for; matrix products, arithmetic and copies ran while one was open for 6% of the time, Pallas kernels for 0%

commit v1 on v0

v1 whole, which is shorter than its diff:
```python
import jax
import jax.numpy as jnp
from jax import lax
from jax.sharding import Mesh, PartitionSpec as P

F32 = jnp.float32
BF16 = jnp.bfloat16


def after(value, *others):
    return lax.optimization_barrier((value, *others))[0]


def swap(value, axis):
    return lax.ppermute(value, axis, [(0, 1), (1, 0)])


def shift(value, axis, distance):
    n = lax.axis_size(axis)
    return lax.ppermute(value, axis, [(i, (i + distance) % n) for i in range(n)])


def cross(value):
    return lax.ppermute(value, ("xl", "xh"), [(0, 3), (3, 0), (1, 2), (2, 1)])


def half(value, index, dim):
    size = value.shape[dim] // 2
    return lax.dynamic_slice_in_dim(value, index * size, size, dim)


def dot(a, b, contract):
    return lax.dot_general(a, b, ((contract[:1], contract[1:]), ((), ())), preferred_element_type=F32)


def order(h, own, other, dim):
    low = jnp.where(h == 0, own, other)
    high = jnp.where(h == 0, other, own)
    return jnp.concatenate([low, high], axis=dim)


def gather_z(block):
    n = lax.axis_size("z")
    z = lax.axis_index("z")
    out = jnp.zeros((n, *block.shape), block.dtype)
    out = lax.dynamic_update_index_in_dim(out, block, z, 0)
    up = down = block
    for step in range(1, n // 2 + 1):
        up = shift(up, "z", 1)
        out = lax.dynamic_update_index_in_dim(out, up, (z - step) % n, 0)
        if step < n // 2:
            down = shift(down, "z", -1)
            out = lax.dynamic_update_index_in_dim(out, down, (z + step) % n, 0)
    return out


def scatter_z(parts):
    n = lax.axis_size("z")
    z = lax.axis_index("z")
    rows = parts.shape[1]
    far = n // 2

    def part(k):
        return lax.dynamic_index_in_dim(parts, (z + k) % n, 0, keepdims=False)

    opposite = part(far)
    up = shift(opposite[: rows // 2].astype(BF16), "z", 1)
    down = shift(opposite[rows // 2 :].astype(BF16), "z", -1)
    up = jnp.pad(up, ((0, rows // 2), (0, 0)))
    down = jnp.pad(down, ((rows // 2, 0), (0, 0)))
    for k in range(far - 1, 0, -1):
        up = shift((part(k) + up.astype(F32)).astype(BF16), "z", 1)
        down = shift((part(-k) + down.astype(F32)).astype(BF16), "z", -1)
    return part(0) + up.astype(F32) + down.astype(F32)


def local(cotangent, activations, down_weight, left_stats, right_stats, left_root, right_root):
    h = lax.axis_index("xl")
    xh = lax.axis_index("xh")
    y = lax.axis_index("y")
    core = lax.axis_index("core")
    tok, d = cotangent.shape
    block = left_root.shape[2]
    left_stats, right_stats, left_root, right_root = (
        v[0] for v in (left_stats, right_stats, left_root, right_root)
    )

    act_other = swap(half(activations, 1 - h, 1), "xl")
    cot_pair = swap(cotangent, "xl")
    cot_cross = cross(cotangent)
    cot_far = swap(cotangent, "xh")
    act_two = order(h, half(activations, h, 1), act_other, 0)
    near = order(h, cotangent, cot_pair, 1)
    far = order(h, cot_far, cot_cross, 1)
    cot_x = jnp.stack([jnp.where(xh == 0, near, far), jnp.where(xh == 0, far, near)])

    act_all = gather_z(act_two).reshape(-1, d)
    y_up = shift(cot_x, "y", 1)
    y_down = shift(cot_x, "y", -1)
    y_far_0 = shift(y_up[0], "y", 1)
    y_far_1 = shift(y_down[1], "y", -1)
    cot_y = jnp.zeros((2, 4, tok, 2 * d), BF16)
    for k, v in ((0, cot_x), (-1, y_up), (1, y_down), (2, jnp.stack([y_far_0, y_far_1]))):
        cot_y = lax.dynamic_update_index_in_dim(cot_y, v, (y + k) % 4, 1)
    cot_c = swap(cot_y, "core")
    cot_all = jnp.stack(
        [jnp.where(core == 0, cot_y, cot_c), jnp.where(core == 0, cot_c, cot_y)], axis=2
    ).reshape(-1, 2 * d)

    weight_other = swap(half(down_weight, 1 - h, 0), "xl")
    weight = order(h, half(down_weight, h, 0), weight_other, 1)
    root_other = swap(left_root, "xl")

    grad = dot(act_all, cot_all, (0, 0)).astype(BF16)
    grad_other = swap(grad, "xl")

    parts = dot(cot_all, weight, (1, 1)).reshape(-1, 2 * tok, d)
    total = scatter_z(parts)
    keep = half(total, h, 0).astype(BF16)
    other = swap(half(total, 1 - h, 0).astype(BF16), "xl")
    input_grad = order(h, keep, other, 1)

    scale = 1.0 / block
    left_gram = order(h, dot(grad, grad, (1, 1)), dot(grad, grad_other, (1, 1)), 1)
    left_new = left_stats + left_gram * scale
    right_gram = dot(half(grad, h, 1), grad, (0, 0)) + dot(half(grad_other, h, 1), grad_other, (0, 0))
    right_new = right_stats + right_gram * scale

    m_own = dot(grad, right_root, (1, 0)).astype(BF16)
    m_other = dot(grad_other, right_root, (1, 0)).astype(BF16)
    m = order(h, m_own, m_other, 0)
    up_own = dot(left_root, m, (1, 0)).astype(BF16)
    up_other = dot(root_other, m, (1, 0)).astype(BF16)
    update = order(h, up_own, up_other, 0)
    return input_grad, update, left_new[None], right_new[None]


def solution(mesh):
    fine = Mesh(mesh.devices.reshape(8, 2, 2, 4, 2), ("z", "xl", "xh", "y", "core"))
    row, col = ("z", "xl"), ("xh", "y", "core")
    in_specs = (
        P(col, row),
        P(row, col),
        P(col, row),
        P(col, row, None),
        P(col, row, None),
        P(col, row, None),
        P(col, None, row),
    )
    out_specs = (P(row, col), P(col, row), P(col, row, None), P(col, row, None))
    return jax.shard_map(local, mesh=fine, in_specs=in_specs, out_specs=out_specs, check_vma=False)
```

time: 397 us -> 137 us (0.35)
  waiting for transfers between devices: 353 us -> 55.2 us
  starting transfers between devices: 1.45 us -> 46.8 us
  between operations: 13.9 us -> 1.1 us
  local copies, waits for them, and re-layouts: 0.05 us -> 9.35 us
  matrix products: 23.6 us -> 14.5 us
  other arithmetic: 3.3 us -> 9.5 us
    all_gather x2 -> x0, waiting for transfers between devices: 150 us -> none  [the longest x1 92.8 us: local(): lax.all_gather(activations, 'row', axis=0, tiled=True)]
    reduce_scatter x1 -> x0, waiting for transfers between devices: 81.3 us -> none  [local(): lax.psum_scatter(lax.dot_general(tok_rows, down_weight, (((1,), (1,)), ((...]
    ppermute x2 -> x28, waiting for transfers between devices: 121 us -> 55.2 us  [the longest x19 45.3 us: shift(): lax.ppermute(value, axis, [(i, (i + distance) % n) for i in range(n)])]
    ppermute x2 -> x28, starting transfers between devices: 1.34 us -> 46.8 us  [the longest x19 34.7 us: shift(): lax.ppermute(value, axis, [(i, (i + distance) % n) for i in range(n)])]
    dot_general x6 -> x10, matrix products: 23.6 us -> 14.5 us  [dot(): lax.dot_general(a, b, ((contract[:1], contract[1:]), ((), ())), preferred...]
  transfers between devices with their start and end apart: 5 -> 28, of which waited for: 5 -> 13; matrix products, arithmetic and copies ran while one was open for 6% -> 23% of each run, Pallas kernels for 0% -> 0%
where the time goes in v1:
time: 137 us; the launch traced here: 136 us
  waiting for transfers between devices  55.2 us (40%)
  starting transfers between devices  46.8 us (34%)
  matrix products  14.5 us (11%)
  other arithmetic  9.5 us (7%)
  local copies, waits for them, and re-layouts  9.35 us (7%)
    ppermute x19, waiting for transfers between devices, shift(): lax.ppermute(value, axis, [(i, (i + distance) % n) for i in range(n)])  45.3 us
    ppermute x19, starting transfers between devices, shift(): lax.ppermute(value, axis, [(i, (i + distance) % n) for i in range(n)])  34.7 us
    dot_general x10, matrix products, dot(): lax.dot_general(a, b, ((contract[:1], contract[1:]), ((), ())), preferred...  14.5 us
    ppermute x8, starting transfers between devices, swap(): return lax.ppermute(value, axis, [(0, 1), (1, 0)])  11.3 us
    ppermute x8, waiting for transfers between devices, swap(): return lax.ppermute(value, axis, [(0, 1), (1, 0)])  9.64 us
    unnamed x21, local copies, waits for them, and re-layouts  2.93 us
  transfers between devices with their start and end apart: 28, of which 13 were waited for; matrix products, arithmetic and copies ran while one was open for 23% of the time, Pallas kernels for 0%

profile of v1, /device:TPU:2, one launch (start us, length us, event | category | flops | bytes accessed | tf_op | source)
XLA Modules:
  0.0 136.5 jit_solution(18255267717891539664)
XLA Ops:
  0.7 2.4 %collective-permute-start = (bf16[128,512]{1,0:T(8,128)(2,1)}, bf16[128,512]{1,0:T(8,128)(2,1)S(1)}, u32[]{:S(2)}, u32[]{:S(2)}) collective-permute-start(bf16[128,512]{1,0:T(8,128)(2,1)} %param.7), channel_id=1, source_target_pairs={{0,16},{16,0},{1,17},{17,1},{2,18},{18,2},{3,19},{19,3},{4,20},{20... | collective-permute-start | bytes 393224 | tf_op jit(solution)/shard_map/ppermute | solution.py:15
  5.5 3.2 %collective-permute-start.18 = (bf16[128,512]{1,0:T(8,128)(2,1)S(1)}, bf16[128,512]{1,0:T(8,128)(2,1)S(1)}, u32[]{:S(2)}, u32[]{:S(2)}) collective-permute-start(bf16[128,512]{1,0:T(8,128)(2,1)S(1)} %constant_dynamic-slice_fusion), channel_id=1, source_target_pairs={{0,16},{16,0},{1,17},{17,1},{2,18},{18,2},{3,19},{19,3},{4,20},{20... | collective-permute-start | bytes 393224 | tf_op jit(solution)/shard_map/ppermute | solution.py:15
  12.4 3.0 %collective-permute-start.4 = (bf16[2,128,1024]{2,1,0:T(8,128)(2,1)}, bf16[2,128,1024]{2,1,0:T(8,128)(2,1)}, u32[]{:S(2)}, u32[]{:S(2)}) collective-permute-start(bf16[2,128,1024]{2,1,0:T(8,128)(2,1)} %pad_maximum_fusion.5), channel_id=1, source_target_pairs={{0,6},{2,0},{4,2},{6,4},{1,7},{3,1},{5,3},{7,5},{8,14},{10,8},{12,... | collective-permute-start | bytes 1572872 | tf_op jit(solution)/shard_map/ppermute | solution.py:20
  18.2 4.0 %collective-permute-start.20 = (bf16[256,512]{1,0:T(8,128)(2,1)}, bf16[256,512]{1,0:T(8,128)(2,1)}, u32[]{:S(2)}, u32[]{:S(2)}) collective-permute-start(bf16[256,512]{1,0:T(8,128)(2,1)} %pad_maximum_fusion.9), channel_id=1, source_target_pairs={{0,224},{32,0},{64,32},{96,64},{128,96},{160,128},{192,160},{224,1... | collective-permute-start | bytes 786440 | tf_op jit(solution)/shard_map/ppermute | solution.py:20
  23.2 2.3 %collective-permute-done.4 = bf16[2,128,1024]{2,1,0:T(8,128)(2,1)} collective-permute-done((bf16[2,128,1024]{2,1,0:T(8,128)(2,1)}, bf16[2,128,1024]{2,1,0:T(8,128)(2,1)}, u32[]{:S(2)}, u32[]{:S(2)}) %collective-permute-start.4) | collective-permute-done | bytes 524320 | tf_op jit(solution)/shard_map/ppermute | solution.py:20
  26.5 3.8 %collective-permute-start.6 = (bf16[128,1024]{1,0:T(8,128)(2,1)S(1)}, bf16[128,1024]{1,0:T(8,128)(2,1)S(1)}, u32[]{:S(2)}, u32[]{:S(2)}) collective-permute-start(bf16[128,1024]{1,0:T(8,128)(2,1)S(1)} %slice_bitcast_fusion), channel_id=1, source_target_pairs={{0,6},{2,0},{4,2},{6,4},{1,7},{3,1},{5,3},{7,5},{8,14},{10,8},{12,... | collective-permute-start | bytes 786440 | tf_op jit(solution)/shard_map/ppermute | solution.py:20
  31.5 2.6 %collective-permute-done.6 = bf16[128,1024]{1,0:T(8,128)(2,1)S(1)} collective-permute-done((bf16[128,1024]{1,0:T(8,128)(2,1)S(1)}, bf16[128,1024]{1,0:T(8,128)(2,1)S(1)}, u32[]{:S(2)}, u32[]{:S(2)}) %collective-permute-start.6) | collective-permute-done | bytes 262176 | tf_op jit(solution)/shard_map/ppermute | solution.py:20
  34.1 3.8 %collective-permute-done.5 = bf16[128,1024]{1,0:T(8,128)(2,1)S(1)} collective-permute-done((bf16[128,1024]{1,0:T(8,128)(2,1)S(1)}, bf16[128,1024]{1,0:T(8,128)(2,1)S(1)}, u32[]{:S(2)}, u32[]{:S(2)}) %collective-permute-start.5) | collective-permute-done | bytes 262176 | tf_op jit(solution)/shard_map/ppermute | solution.py:20
  38.9 3.4 %collective-permute-start.8 = (bf16[512,512]{1,0:T(8,128)(2,1)}, bf16[512,512]{1,0:T(8,128)(2,1)}, u32[]{:S(2)}, u32[]{:S(2)}) collective-permute-start(bf16[512,512]{1,0:T(8,128)(2,1)} %constant_dynamic-slice_fusion.1), channel_id=1, source_target_pairs={{0,16},{16,0},{1,17},{17,1},{2,18},{18,2},{3,19},{19,3},{4,20},{20... | collective-permute-start | bytes 1572872 | tf_op jit(solution)/shard_map/ppermute | solution.py:15
  44.6 4.0 %collective-permute-start.22 = (bf16[256,512]{1,0:T(8,128)(2,1)}, bf16[256,512]{1,0:T(8,128)(2,1)S(1)}, u32[]{:S(2)}, u32[]{:S(2)}) collective-permute-start(bf16[256,512]{1,0:T(8,128)(2,1)} %collective-permute-done.20), channel_id=1, source_target_pairs={{0,224},{32,0},{64,32},{96,64},{128,96},{160,128},{192,160},{224,1... | collective-permute-start | bytes 786440 | tf_op jit(solution)/shard_map/ppermute | solution.py:20
  50.6 4.8 %collective-permute-done.8 = bf16[512,512]{1,0:T(8,128)(2,1)} collective-permute-done((bf16[512,512]{1,0:T(8,128)(2,1)}, bf16[512,512]{1,0:T(8,128)(2,1)}, u32[]{:S(2)}, u32[]{:S(2)}) %collective-permute-start.8) | collective-permute-done | bytes 524320 | tf_op jit(solution)/shard_map/ppermute | solution.py:15
  56.7 2.2 %collective-permute-start.23 = (bf16[256,512]{1,0:T(8,128)(2,1)S(1)}, bf16[256,512]{1,0:T(8,128)(2,1)S(1)}, u32[]{:S(2)}, u32[]{:S(2)}) collective-permute-start(bf16[256,512]{1,0:T(8,128)(2,1)S(1)} %collective-permute-done.21), channel_id=1, source_target_pairs={{0,32},{32,64},{64,96},{96,128},{128,160},{160,192},{192,224},{224... | collective-permute-start | bytes 786440 | tf_op jit(solution)/shard_map/ppermute | solution.py:20
  58.8 4.0 %collective-permute-start.24 = (bf16[256,512]{1,0:T(8,128)(2,1)S(1)}, bf16[256,512]{1,0:T(8,128)(2,1)S(1)}, u32[]{:S(2)}, u32[]{:S(2)}) collective-permute-start(bf16[256,512]{1,0:T(8,128)(2,1)S(1)} %collective-permute-done.22), channel_id=1, source_target_pairs={{0,224},{32,0},{64,32},{96,64},{128,96},{160,128},{192,160},{224,1... | collective-permute-start | bytes 786440 | tf_op jit(solution)/shard_map/ppermute | solution.py:20
  62.9 6.0 %collective-permute-done.23 = bf16[256,512]{1,0:T(8,128)(2,1)S(1)} collective-permute-done((bf16[256,512]{1,0:T(8,128)(2,1)S(1)}, bf16[256,512]{1,0:T(8,128)(2,1)S(1)}, u32[]{:S(2)}, u32[]{:S(2)}) %collective-permute-start.23) | collective-permute-done | bytes 262176 | tf_op jit(solution)/shard_map/ppermute | solution.py:20
  69.0 8.5 %collective-permute-done.25 = bf16[256,512]{1,0:T(8,128)(2,1)S(1)} collective-permute-done((bf16[256,512]{1,0:T(8,128)(2,1)S(1)}, bf16[256,512]{1,0:T(8,128)(2,1)S(1)}, u32[]{:S(2)}, u32[]{:S(2)}) %collective-permute-start.25) | collective-permute-done | bytes 262176 | tf_op jit(solution)/shard_map/ppermute | solution.py:20
  79.8 2.4 %fusion.2 = f32[8,256,512]{2,1,0:T(8,128)S(1)} fusion(bf16[8,256,1024]{2,1,0:T(8,128)(2,1)S(1)} %bitcast.128, bf16[512,512]{1,0:T(8,128)(2,1)S(1)} %get-tuple-element.15, bf16[512,512]{1,0:T(8,128)(2,1)S(1)} %get-tuple-element.14), kind=kOutput, calls=%fused_computation.13 | convolution fusion | flops 2149580800 | bytes 9437184 | tf_op jit(solution)/shard_map/dot_general | solution.py:33
  82.4 3.2 %collective-permute-start.13 = (bf16[128,512]{1,0:T(8,128)(2,1)S(1)}, bf16[128,512]{1,0:T(8,128)(2,1)S(1)}, u32[]{:S(2)}, u32[]{:S(2)}) collective-permute-start(bf16[128,512]{1,0:T(8,128)(2,1)S(1)} %get-tuple-element.27), channel_id=1, source_target_pairs={{0,224},{32,0},{64,32},{96,64},{128,96},{160,128},{192,160},{224,1... | collective-permute-start | bytes 393224 | tf_op jit(solution)/shard_map/ppermute | solution.py:20
  85.6 2.3 %convolution_convert_fusion = bf16[512,1024]{1,0:T(8,128)(2,1)S(1)} fusion(bf16[2048,512]{1,0:T(8,128)(2,1)S(1)} %bitcast.130, bf16[2048,1024]{1,0:T(8,128)(2,1)S(1)} %bitcast.129), kind=kOutput, calls=%fused_computation.7 | convolution fusion | flops 2148007936 | bytes 7340032 | tf_op jit(solution)/shard_map/dot_general | solution.py:33
  90.0 7.1 %collective-permute-done.10 = bf16[256,512]{1,0:T(8,128)(2,1)S(1)} collective-permute-done((bf16[256,512]{1,0:T(8,128)(2,1)S(1)}, bf16[256,512]{1,0:T(8,128)(2,1)S(1)}, u32[]{:S(2)}, u32[]{:S(2)}) %collective-permute-start.10) | collective-permute-done | bytes 262176 | tf_op jit(solution)/shard_map/ppermute | solution.py:20
  98.0 7.0 %collective-permute-done.11 = bf16[256,512]{1,0:T(8,128)(2,1)S(1)} collective-permute-done((bf16[256,512]{1,0:T(8,128)(2,1)S(1)}, bf16[256,512]{1,0:T(8,128)(2,1)S(1)}, u32[]{:S(2)}, u32[]{:S(2)}) %collective-permute-start.11) | collective-permute-done | bytes 262176 | tf_op jit(solution)/shard_map/ppermute | solution.py:20
  108.3 5.5 %collective-permute-done.14 = bf16[256,512]{1,0:T(8,128)(2,1)S(1)} collective-permute-done((bf16[256,512]{1,0:T(8,128)(2,1)S(1)}, bf16[256,512]{1,0:T(8,128)(2,1)S(1)}, u32[]{:S(2)}, u32[]{:S(2)}) %collective-permute-start.14) | collective-permute-done | bytes 262176 | tf_op jit(solution)/shard_map/ppermute | solution.py:20
  119.8 2.1 %fusion.1 = f32[1,512,1024]{2,1,0:T(8,128)} fusion(f32[1,512,1024]{2,1,0:T(8,128)S(1)} %copy-done.4, f32[512,1024]{1,0:T(8,128)S(1)} %fusion.16, bf16[512,1024]{1,0:T(8,128)(2,1)S(1)} %collective-permute-done.26, s32[]{:T(128)S(6)} %select_n.272), kind=kOutput, calls=%fused_computation.4 | convolution fusion | flops 538443776 | bytes 7864324 | tf_op jit(solution)/shard_map/dot_general | solution.py:33
  128.0 2.5 %collective-permute-done.16 = bf16[256,512]{1,0:T(8,128)(2,1)S(1)} collective-permute-done((bf16[256,512]{1,0:T(8,128)(2,1)S(1)}, bf16[256,512]{1,0:T(8,128)(2,1)S(1)}, u32[]{:S(2)}, u32[]{:S(2)}) %collective-permute-start.16) | collective-permute-done | bytes 262176 | tf_op jit(solution)/shard_map/ppermute | solution.py:20
  132.4 3.3 %collective-permute-done.17 = bf16[128,512]{1,0:T(8,128)(2,1)S(1)} collective-permute-done((bf16[128,512]{1,0:T(8,128)(2,1)S(1)}, bf16[128,512]{1,0:T(8,128)(2,1)S(1)}, u32[]{:S(2)}, u32[]{:S(2)}) %collective-permute-start.17) | collective-permute-done | bytes 131104 | tf_op jit(solution)/shard_map/ppermute | solution.py:15
  (103 shorter events, 41.9 us)
Async XLA Ops:
  0.7 8.1 %collective-permute-start = (bf16[128,512]{1,0:T(8,128)(2,1)}, bf16[128,512]{1,0:T(8,128)(2,1)S(1)}, u32[]{:S(2)}, u32[]{:S(2)}) collective-permute-start(bf16[128,512]{1,0:T(8,128)(2,1)} %param.7), channel_id=1, source_target_pairs={{0,16},{16,0},{1,17},{17,1},{2,18},{18,2},{3,19},{19,3},{4,20},{20... | collective-permute-start | bytes 393224 | tf_op jit(solution)/shard_map/ppermute | solution.py:15
  3.0 8.2 %collective-permute-start.1 = (bf16[128,512]{1,0:T(8,128)(2,1)}, bf16[128,512]{1,0:T(8,128)(2,1)S(1)}, u32[]{:S(2)}, u32[]{:S(2)}) collective-permute-start(bf16[128,512]{1,0:T(8,128)(2,1)} %param.7), channel_id=1, source_target_pairs={{0,8},{8,0},{1,9},{9,1},{2,10},{10,2},{3,11},{11,3},{4,12},{12,4},... | collective-permute-start | bytes 393224 | tf_op jit(solution)/shard_map/ppermute | solution.py:15
  3.7 7.7 %collective-permute-start.2 = (bf16[128,512]{1,0:T(8,128)(2,1)}, bf16[128,512]{1,0:T(8,128)(2,1)S(1)}, u32[]{:S(2)}, u32[]{:S(2)}) collective-permute-start(bf16[128,512]{1,0:T(8,128)(2,1)} %param.7), channel_id=1, source_target_pairs={{0,24},{24,0},{8,16},{16,8},{1,25},{25,1},{9,17},{17,9},{2,26},{26... | collective-permute-start | bytes 393224 | tf_op jit(solution)/shard_map/ppermute | solution.py:24
  5.5 9.9 %collective-permute-start.18 = (bf16[128,512]{1,0:T(8,128)(2,1)S(1)}, bf16[128,512]{1,0:T(8,128)(2,1)S(1)}, u32[]{:S(2)}, u32[]{:S(2)}) collective-permute-start(bf16[128,512]{1,0:T(8,128)(2,1)S(1)} %constant_dynamic-slice_fusion), channel_id=1, source_target_pairs={{0,16},{16,0},{1,17},{17,1},{2,18},{18,2},{3,19},{19,3},{4,20},{20... | collective-permute-start | bytes 393224 | tf_op jit(solution)/shard_map/ppermute | solution.py:15
  12.4 13.1 %collective-permute-start.4 = (bf16[2,128,1024]{2,1,0:T(8,128)(2,1)}, bf16[2,128,1024]{2,1,0:T(8,128)(2,1)}, u32[]{:S(2)}, u32[]{:S(2)}) collective-permute-start(bf16[2,128,1024]{2,1,0:T(8,128)(2,1)} %pad_maximum_fusion.5), channel_id=1, source_target_pairs={{0,6},{2,0},{4,2},{6,4},{1,7},{3,1},{5,3},{7,5},{8,14},{10,8},{12,... | collective-permute-start | bytes 1572872 | tf_op jit(solution)/shard_map/ppermute | solution.py:20
  15.4 14.8 %collective-permute-start.3 = (bf16[2,128,1024]{2,1,0:T(8,128)(2,1)}, bf16[2,128,1024]{2,1,0:T(8,128)(2,1)S(1)}, u32[]{:S(2)}, u32[]{:S(2)}) collective-permute-start(bf16[2,128,1024]{2,1,0:T(8,128)(2,1)} %pad_maximum_fusion.5), channel_id=1, source_target_pairs={{0,2},{2,4},{4,6},{6,0},{1,3},{3,5},{5,7},{7,1},{8,10},{10,12},{12... | collective-permute-start | bytes 1572872 | tf_op jit(solution)/shard_map/ppermute | solution.py:20
  16.3 26.3 %collective-permute-start.19 = (bf16[256,512]{1,0:T(8,128)(2,1)}, bf16[256,512]{1,0:T(8,128)(2,1)}, u32[]{:S(2)}, u32[]{:S(2)}) collective-permute-start(bf16[256,512]{1,0:T(8,128)(2,1)} %pad_maximum_fusion.9), channel_id=1, source_target_pairs={{0,32},{32,64},{64,96},{96,128},{128,160},{160,192},{192,224},{224... | collective-permute-start | bytes 786440 | tf_op jit(solution)/shard_map/ppermute | solution.py:20
  18.2 26.4 %collective-permute-start.20 = (bf16[256,512]{1,0:T(8,128)(2,1)}, bf16[256,512]{1,0:T(8,128)(2,1)}, u32[]{:S(2)}, u32[]{:S(2)}) collective-permute-start(bf16[256,512]{1,0:T(8,128)(2,1)} %pad_maximum_fusion.9), channel_id=1, source_target_pairs={{0,224},{32,0},{64,32},{96,64},{128,96},{160,128},{192,160},{224,1... | collective-permute-start | bytes 786440 | tf_op jit(solution)/shard_map/ppermute | solution.py:20
  26.5 7.7 %collective-permute-start.6 = (bf16[128,1024]{1,0:T(8,128)(2,1)S(1)}, bf16[128,1024]{1,0:T(8,128)(2,1)S(1)}, u32[]{:S(2)}, u32[]{:S(2)}) collective-permute-start(bf16[128,1024]{1,0:T(8,128)(2,1)S(1)} %slice_bitcast_fusion), channel_id=1, source_target_pairs={{0,6},{2,0},{4,2},{6,4},{1,7},{3,1},{5,3},{7,5},{8,14},{10,8},{12,... | collective-permute-start | bytes 786440 | tf_op jit(solution)/shard_map/ppermute | solution.py:20
  38.0 39.5 %collective-permute-start.7 = (bf16[2,4,128,1024]{3,2,1,0:T(8,128)(2,1)S(1)}, bf16[2,4,128,1024]{3,2,1,0:T(8,128)(2,1)}, u32[]{:S(2)}, u32[]{:S(2)}) collective-permute-start(bf16[2,4,128,1024]{3,2,1,0:T(8,128)(2,1)S(1)} %fusion.7), channel_id=1, source_target_pairs={{0,1},{1,0},{2,3},{3,2},{4,5},{5,4},{6,7},{7,6},{8,9},{9,8},{10,11... | collective-permute-start | bytes 6291464 | tf_op jit(solution)/shard_map/ppermute | solution.py:15
  38.9 16.5 %collective-permute-start.8 = (bf16[512,512]{1,0:T(8,128)(2,1)}, bf16[512,512]{1,0:T(8,128)(2,1)}, u32[]{:S(2)}, u32[]{:S(2)}) collective-permute-start(bf16[512,512]{1,0:T(8,128)(2,1)} %constant_dynamic-slice_fusion.1), channel_id=1, source_target_pairs={{0,16},{16,0},{1,17},{17,1},{2,18},{18,2},{3,19},{19,3},{4,20},{20... | collective-permute-start | bytes 1572872 | tf_op jit(solution)/shard_map/ppermute | solution.py:15
  42.3 83.6 %collective-permute-start.27 = (bf16[512,1024]{1,0:T(8,128)(2,1)}, bf16[512,1024]{1,0:T(8,128)(2,1)}, u32[]{:S(2)}, u32[]{:S(2)}) collective-permute-start(bf16[512,1024]{1,0:T(8,128)(2,1)} %bitcast.41), channel_id=1, source_target_pairs={{0,16},{16,0},{1,17},{17,1},{2,18},{18,2},{3,19},{19,3},{4,20},{20... | collective-permute-start | bytes 3145736 | tf_op jit(solution)/shard_map/ppermute | solution.py:15
  42.6 14.1 %collective-permute-start.21 = (bf16[256,512]{1,0:T(8,128)(2,1)}, bf16[256,512]{1,0:T(8,128)(2,1)S(1)}, u32[]{:S(2)}, u32[]{:S(2)}) collective-permute-start(bf16[256,512]{1,0:T(8,128)(2,1)} %collective-permute-done.19), channel_id=1, source_target_pairs={{0,32},{32,64},{64,96},{96,128},{128,160},{160,192},{192,224},{224... | collective-permute-start | bytes 786440 | tf_op jit(solution)/shard_map/ppermute | solution.py:20
  44.6 14.3 %collective-permute-start.22 = (bf16[256,512]{1,0:T(8,128)(2,1)}, bf16[256,512]{1,0:T(8,128)(2,1)S(1)}, u32[]{:S(2)}, u32[]{:S(2)}) collective-permute-start(bf16[256,512]{1,0:T(8,128)(2,1)} %collective-permute-done.20), channel_id=1, source_target_pairs={{0,224},{32,0},{64,32},{96,64},{128,96},{160,128},{192,160},{224,1... | collective-permute-start | bytes 786440 | tf_op jit(solution)/shard_map/ppermute | solution.py:20
  56.7 12.3 %collective-permute-start.23 = (bf16[256,512]{1,0:T(8,128)(2,1)S(1)}, bf16[256,512]{1,0:T(8,128)(2,1)S(1)}, u32[]{:S(2)}, u32[]{:S(2)}) collective-permute-start(bf16[256,512]{1,0:T(8,128)(2,1)S(1)} %collective-permute-done.21), channel_id=1, source_target_pairs={{0,32},{32,64},{64,96},{96,128},{128,160},{160,192},{192,224},{224... | collective-permute-start | bytes 786440 | tf_op jit(solution)/shard_map/ppermute | solution.py:20
  58.8 10.1 %collective-permute-start.24 = (bf16[256,512]{1,0:T(8,128)(2,1)S(1)}, bf16[256,512]{1,0:T(8,128)(2,1)S(1)}, u32[]{:S(2)}, u32[]{:S(2)}) collective-permute-start(bf16[256,512]{1,0:T(8,128)(2,1)S(1)} %collective-permute-done.22), channel_id=1, source_target_pairs={{0,224},{32,0},{64,32},{96,64},{128,96},{160,128},{192,160},{224,1... | collective-permute-start | bytes 786440 | tf_op jit(solution)/shard_map/ppermute | solution.py:20
  68.9 8.5 %collective-permute-start.25 = (bf16[256,512]{1,0:T(8,128)(2,1)S(1)}, bf16[256,512]{1,0:T(8,128)(2,1)S(1)}, u32[]{:S(2)}, u32[]{:S(2)}) collective-permute-start(bf16[256,512]{1,0:T(8,128)(2,1)S(1)} %collective-permute-done.23), channel_id=1, source_target_pairs={{0,32},{32,64},{64,96},{96,128},{128,160},{160,192},{192,224},{224... | collective-permute-start | bytes 786440 | tf_op jit(solution)/shard_map/ppermute | solution.py:20
  82.4 15.6 %collective-permute-start.13 = (bf16[128,512]{1,0:T(8,128)(2,1)S(1)}, bf16[128,512]{1,0:T(8,128)(2,1)S(1)}, u32[]{:S(2)}, u32[]{:S(2)}) collective-permute-start(bf16[128,512]{1,0:T(8,128)(2,1)S(1)} %get-tuple-element.27), channel_id=1, source_target_pairs={{0,224},{32,0},{64,32},{96,64},{128,96},{160,128},{192,160},{224,1... | collective-permute-start | bytes 393224 | tf_op jit(solution)/shard_map/ppermute | solution.py:20
  88.0 27.8 %collective-permute-start.26 = (bf16[512,1024]{1,0:T(8,128)(2,1)S(1)}, bf16[512,1024]{1,0:T(8,128)(2,1)S(1)}, u32[]{:S(2)}, u32[]{:S(2)}) collective-permute-start(bf16[512,1024]{1,0:T(8,128)(2,1)S(1)} %convolution_convert_fusion), channel_id=1, source_target_pairs={{0,16},{16,0},{1,17},{17,1},{2,18},{18,2},{3,19},{19,3},{4,20},{20... | collective-permute-start | bytes 3145736 | tf_op jit(solution)/shard_map/ppermute | solution.py:15
  89.2 7.9 %collective-permute-start.10 = (bf16[256,512]{1,0:T(8,128)(2,1)S(1)}, bf16[256,512]{1,0:T(8,128)(2,1)S(1)}, u32[]{:S(2)}, u32[]{:S(2)}) collective-permute-start(bf16[256,512]{1,0:T(8,128)(2,1)S(1)} %fusion.11), channel_id=1, source_target_pairs={{0,32},{32,64},{64,96},{96,128},{128,160},{160,192},{192,224},{224... | collective-permute-start | bytes 786440 | tf_op jit(solution)/shard_map/ppermute | solution.py:20
  97.1 7.9 %collective-permute-start.11 = (bf16[256,512]{1,0:T(8,128)(2,1)S(1)}, bf16[256,512]{1,0:T(8,128)(2,1)S(1)}, u32[]{:S(2)}, u32[]{:S(2)}) collective-permute-start(bf16[256,512]{1,0:T(8,128)(2,1)S(1)} %fusion.12), channel_id=1, source_target_pairs={{0,32},{32,64},{64,96},{96,128},{128,160},{160,192},{192,224},{224... | collective-permute-start | bytes 786440 | tf_op jit(solution)/shard_map/ppermute | solution.py:20
  105.1 8.7 %collective-permute-start.14 = (bf16[256,512]{1,0:T(8,128)(2,1)S(1)}, bf16[256,512]{1,0:T(8,128)(2,1)S(1)}, u32[]{:S(2)}, u32[]{:S(2)}) collective-permute-start(bf16[256,512]{1,0:T(8,128)(2,1)S(1)} %get-tuple-element.9), channel_id=1, source_target_pairs={{0,224},{32,0},{64,32},{96,64},{128,96},{160,128},{192,160},{224,1... | collective-permute-start | bytes 786440 | tf_op jit(solution)/shard_map/ppermute | solution.py:20
  106.2 21.8 %collective-permute-start.12 = (bf16[256,512]{1,0:T(8,128)(2,1)S(1)}, bf16[256,512]{1,0:T(8,128)(2,1)S(1)}, u32[]{:S(2)}, u32[]{:S(2)}) collective-permute-start(bf16[256,512]{1,0:T(8,128)(2,1)S(1)} %get-tuple-element.8), channel_id=1, source_target_pairs={{0,32},{32,64},{64,96},{96,128},{128,160},{160,192},{192,224},{224... | collective-permute-start | bytes 786440 | tf_op jit(solution)/shard_map/ppermute | solution.py:20
  113.9 10.0 %collective-permute-start.15 = (bf16[256,512]{1,0:T(8,128)(2,1)S(1)}, bf16[256,512]{1,0:T(8,128)(2,1)S(1)}, u32[]{:S(2)}, u32[]{:S(2)}) collective-permute-start(bf16[256,512]{1,0:T(8,128)(2,1)S(1)} %fusion.9), channel_id=1, source_target_pairs={{0,224},{32,0},{64,32},{96,64},{128,96},{160,128},{192,160},{224,1... | collective-permute-start | bytes 786440 | tf_op jit(solution)/shard_map/ppermute | solution.py:20
  (14 other events, 192.6 us)

commit v2 on v1

v2 whole, which is shorter than its diff:
```python
import jax
import jax.numpy as jnp
from jax import lax
from jax.experimental import pallas as pl
from jax.experimental.pallas import tpu as pltpu
from jax.sharding import Mesh, PartitionSpec as P

F32 = jnp.float32
BF16 = jnp.bfloat16
VMEM = pl.BlockSpec(memory_space=pltpu.VMEM)
SMEM = pl.BlockSpec(memory_space=pltpu.SMEM)
ANY = pl.BlockSpec(memory_space=pl.ANY)
PARAMS = pltpu.CompilerParams(vmem_limit_bytes=28 * 1024 * 1024)


def after(value, *others):
    return lax.optimization_barrier((value, *others))[0]


def swap(value, axis):
    return lax.ppermute(value, axis, [(0, 1), (1, 0)])


def step(value, axis):
    n = lax.axis_size(axis)
    pairs = [(2 * i + c, (i + 1 - 2 * c) % n * 2 + c) for i in range(n) for c in range(2)]
    return lax.ppermute(value, (axis, "core"), pairs)


def cross(value):
    return lax.ppermute(value, ("xl", "xh"), [(0, 3), (3, 0), (1, 2), (2, 1)])


def half(value, index, dim):
    size = value.shape[dim] // 2
    return lax.dynamic_slice_in_dim(value, index * size, size, dim)


def dot(a, b, contract):
    return lax.dot_general(a, b, ((contract[:1], contract[1:]), ((), ())), preferred_element_type=F32)


def order(h, own, other, dim):
    low = jnp.where(h == 0, own, other)
    high = jnp.where(h == 0, other, own)
    return jnp.concatenate([low, high], axis=dim)


def call(kernel, shapes, *args, specs=None, outs=None, scratch=()):
    return pl.pallas_call(
        kernel,
        out_shape=[jax.ShapeDtypeStruct(s, t) for s, t in shapes],
        in_specs=[SMEM] + (specs or [VMEM] * (len(args) - 1)),
        out_specs=outs or [VMEM] * len(shapes),
        scratch_shapes=list(scratch),
        compiler_params=PARAMS,
        cost_estimate=pl.CostEstimate(flops=0, bytes_accessed=0, transcendentals=0),
    )(*args)


def fetch(y_at, x_at, pieces, tokens, sems):
    tok = pieces[0].shape[1]
    for k in range(4):

        @pl.when(y_at == k)
        def _(k=k):
            for side in range(2):
                target = tokens.at[pl.ds(side * tok, tok)]
                pltpu.make_async_copy(pieces[2 * k + side].at[x_at], target, sems.at[side]).start()


def fetched(pieces, tokens, sems):
    tok = pieces[0].shape[1]
    for side in range(2):
        target = tokens.at[pl.ds(side * tok, tok)]
        pltpu.make_async_copy(pieces[side].at[0], target, sems.at[side]).wait()


def far_kernel(index, *refs):
    pieces, (weight, out, tokens, sems) = refs[:8], refs[8:]
    fetch(index[0], index[1], pieces, tokens, sems)
    fetched(pieces, tokens, sems)
    out[...] = dot(tokens[...], weight[...], (1, 1)).astype(BF16)


def part_kernel(index, *refs):
    pieces, (weight, sibling, *outs), (tokens, sems) = refs[:8], refs[8:14], refs[14:]
    for k in range(4):
        fetch(index[2 * k], index[2 * k + 1], pieces, tokens.at[k], sems.at[k])
    for k, out in enumerate(outs):
        fetched(pieces, tokens.at[k], sems.at[k])
        out[0] = dot(tokens[k], weight[...], (1, 1))
        if k < 3:
            out[1] = dot(tokens[k], sibling[...], (1, 1))


PICKS = (None, 0, 0, 0, 1, 1, 1, None)


def grad_kernel(index, *refs):
    acts, pieces = refs[:8], refs[8:16]
    out, rows, tokens, total, row_sems, sems = refs[16:]
    copies = []
    for k, pick in enumerate(PICKS):
        source = acts[k] if pick is None else acts[k].at[pick]
        copies.append(pltpu.make_async_copy(source, rows.at[k], row_sems.at[k]))
        copies[k].start()
        fetch(index[2 * k], index[2 * k + 1], pieces, tokens.at[k], sems.at[k])
    for k in range(8):
        copies[k].wait()
        fetched(pieces, tokens.at[k], sems.at[k])
        product = dot(rows[k], tokens[k], (0, 0))
        if k == 0:
            total[...] = product
        elif k < 7:
            total[...] += product
        else:
            out[...] = (total[...] + product).astype(BF16)


def own_kernel(index, grad, right_root, left_root, left_root_other, left_out, right_out, up_out):
    h = index[0]
    d = grad.shape[0]
    scale = 1.0 / (2 * d)
    at = pl.ds(pl.multiple_of(h * d, d), d)
    there = pl.ds(pl.multiple_of((1 - h) * d, d), d)
    left_out[...] = dot(grad[...], grad[...], (1, 1)) * scale
    right_out[...] = dot(grad[:, :d], grad[...], (0, 0)) * scale
    m = (dot(grad[:, :d], right_root[at], (1, 0)) + dot(grad[:, d:], right_root[there], (1, 0))).astype(BF16)
    up_out[:d] = dot(left_root[:, at], m, (1, 0))
    up_out[d:] = dot(left_root_other[:, at], m, (1, 0))


def other_kernel(index, *refs):
    (grad, other, right_root, left_root, left_root_other, left_own, right_own, up_own) = refs[:8]
    left_stats, right_stats, left_new, right_new, update = refs[8:13]
    left_in, right_in, left_buf, right_buf, up_buf, sems = refs[13:]
    h = index[0]
    d = grad.shape[0]
    scale = 1.0 / (2 * d)
    at = pl.ds(pl.multiple_of(h * d, d), d)
    there = pl.ds(pl.multiple_of((1 - h) * d, d), d)
    copy = pltpu.make_async_copy
    ins = [copy(left_stats, left_in, sems.at[0]), copy(right_stats, right_in, sems.at[1])]
    outs = [
        copy(up_buf, update, sems.at[2]),
        copy(left_buf, left_new, sems.at[3]),
        copy(right_buf, right_new, sems.at[4]),
    ]
    for c in ins:
        c.start()
    m = dot(other[:, d:], right_root[at], (1, 0)) + dot(other[:, :d], right_root[there], (1, 0))
    m = m.astype(BF16)
    up_buf[at] = (up_own[:d] + dot(left_root[:, there], m, (1, 0))).astype(BF16)
    up_buf[there] = (up_own[d:] + dot(left_root_other[:, there], m, (1, 0))).astype(BF16)
    outs[0].start()
    gram = dot(grad[:, :d], other[:, d:], (1, 1)) + dot(grad[:, d:], other[:, :d], (1, 1))
    ins[0].wait()
    left_buf[:, at] = left_in[:, at] + left_own[...]
    left_buf[:, there] = left_in[:, there] + gram * scale
    outs[1].start()
    mine = other[:, d:]
    gram = dot(mine, other[:, d:], (0, 0))
    ins[1].wait()
    right_buf[:, at] = right_in[:, at] + right_own[:, :d] + gram * scale
    gram = dot(mine, other[:, :d], (0, 0))
    right_buf[:, there] = right_in[:, there] + right_own[:, d:] + gram * scale
    outs[2].start()
    for c in outs:
        c.wait()


def cot_kernel(index, own, pair, far, cross_block, out):
    tok, d = own.shape
    out[0, :, :d] = own[...]
    out[0, :, d:] = pair[tok:]
    out[1, :, :d] = far[...]
    out[1, :, d:] = cross_block[...]


def send_kernel(index, act, own, out, sems):
    tok, d = own.shape
    at = pl.ds(pl.multiple_of(index[0] * d, d), d)
    copies = [
        pltpu.make_async_copy(act.at[:, at], out.at[pl.ds(0, tok)], sems.at[0]),
        pltpu.make_async_copy(own, out.at[pl.ds(tok, tok)], sems.at[1]),
    ]
    for c in copies:
        c.start()
    for c in copies:
        c.wait()


def add_kernel(index, part, arrived, out):
    if len(arrived.shape) == 2:
        out[0] = (part[0] + arrived[...].astype(F32)).astype(BF16)
        out[1] = part[1].astype(BF16)
    else:
        out[...] = (part[...] + arrived[...].astype(F32)).astype(BF16)


def last_kernel(index, part, arrived, sibling, keep, send):
    h = index[0]
    rows = keep.shape[0]

    def total(k):
        at = pl.ds(pl.multiple_of(k * rows, rows), rows)
        there = pl.ds(pl.multiple_of((1 - k) * rows, rows), rows)
        return part[0, at] + arrived[0, at].astype(F32) + sibling[1, there].astype(F32)

    keep[...] = total(h).astype(BF16)
    send[...] = total(1 - h).astype(BF16)


def local(cotangent, activations, down_weight, left_stats, right_stats, left_root, right_root):
    z = lax.axis_index("z")
    h = lax.axis_index("xl")
    xh = lax.axis_index("xh")
    y = lax.axis_index("y")
    core = lax.axis_index("core")
    sign = 1 - 2 * core
    tok, d = cotangent.shape
    block = left_root.shape[2]
    left_stats, right_stats, left_root, right_root = (
        v[0] for v in (left_stats, right_stats, left_root, right_root)
    )

    nothing = jnp.zeros((1,), jnp.int32)

    both = call(
        send_kernel,
        [((2 * tok, d), BF16)],
        (1 - h)[None],
        activations,
        cotangent,
        specs=[ANY] * 2,
        scratch=[pltpu.SemaphoreType.DMA((2,))],
    )[0]
    both = swap(both, "xl")
    cot_cross = cross(cotangent)
    cot_far = swap(cotangent, "xh")
    act = order(h ^ core, half(activations, h, 1), both[:tok], 0)
    cot = call(cot_kernel, [((2, tok, 2 * d), BF16)], nothing, cotangent, both, cot_far, cot_cross)[0]

    cot_s = swap(cot, "core")
    y_a = step(cot, "y")
    y_b = step(cot_s, "y")
    z_0 = jnp.stack([act, swap(act, "core")])
    z_1 = step(z_0, "z")
    z_2 = step(z_1, "z")
    z_3 = step(z_2, "z")
    z_4 = step(z_3[0], "z")
    s_1, s_2, s_3 = (swap(v, "core") for v in (z_1, z_2, z_3))

    weight_other = swap(half(down_weight, 1 - h, 0), "xl")
    weight = jnp.concatenate([half(down_weight, h, 0), weight_other], 1)
    weight_s = swap(weight, "core")
    root_after = after(left_root, weight_other)
    root_a = swap(root_after[: d // 2], "xl")
    root_b = swap(root_after[d // 2 :], "xl")

    y_c = step(y_a, "y")
    t_a, t_b, t_c = (swap(v, "core") for v in (y_a, y_b, y_c))
    pieces = (cot, cot_s, y_a, y_b, t_b, t_a, y_c, t_c)

    def place(k):
        target = (z + k * sign) % 8
        offset = (target % 4 - y) * sign % 4
        y_at = jnp.where(offset == 0, 0, jnp.where(offset == 3, 1, jnp.where(offset == 1, 2, 3)))
        return jnp.stack([y_at, xh ^ (target // 4)])

    def places(*ks):
        return jnp.concatenate([place(k) for k in ks])

    sem = pltpu.SemaphoreType.DMA
    grad = call(
        grad_kernel,
        [((d, 2 * d), BF16)],
        after(places(0, -1, -2, -3, 1, 2, 3, 4), root_b),
        act, z_1, z_2, z_3, s_1, s_2, s_3, z_4,
        *pieces,
        specs=[ANY] * 16,
        scratch=[
            pltpu.VMEM((8, 2 * tok, d), BF16),
            pltpu.VMEM((8, 2 * tok, 2 * d), BF16),
            pltpu.VMEM((d, 2 * d), F32),
            sem((8,)),
            sem((8, 2)),
        ],
    )[0]
    other = swap(grad, "xl")

    flow = call(
        far_kernel,
        [((2 * tok, d), BF16)],
        after(place(4), root_a),
        *pieces,
        weight,
        specs=[ANY] * 8 + [VMEM],
        scratch=[pltpu.VMEM((2 * tok, 2 * d), BF16), sem((2,))],
    )[0]
    flow = step(flow, "z")
    *parts, part_0 = call(
        part_kernel,
        [((2, 2 * tok, d), F32)] * 3 + [((1, 2 * tok, d), F32)],
        places(3, 2, 1, 0),
        *pieces,
        weight,
        weight_s,
        specs=[ANY] * 8 + [VMEM] * 2,
        scratch=[pltpu.VMEM((4, 2 * tok, 2 * d), BF16), sem((4, 2))],
    )
    for k, part in enumerate(parts):
        flow = call(add_kernel, [((2, 2 * tok, d), BF16)], nothing, part, flow)[0]
        if k < 2:
            flow = step(flow, "z")
    flow = step(flow, "z")
    keep, send = call(
        last_kernel, [((tok, d), BF16)] * 2, (h ^ core)[None], part_0, flow, swap(flow, "core")
    )
    input_grad = order(h, keep, swap(send, "xl"), 1)

    root_other = jnp.concatenate([root_a, root_b], 0)
    left_own, right_own, up_own = call(
        own_kernel,
        [((d, d), F32), ((d, 2 * d), F32), ((2 * d, d), F32)],
        h[None],
        grad,
        right_root,
        left_root,
        root_other,
    )
    stats = ((d, 2 * d), F32)
    left_new, right_new, update = call(
        other_kernel,
        [stats, stats, ((2 * d, d), BF16)],
        h[None],
        grad,
        other,
        right_root,
        left_root,
        root_other,
        left_own,
        right_own,
        up_own,
        left_stats,
        right_stats,
        specs=[VMEM] * 8 + [ANY] * 2,
        outs=[ANY] * 3,
        scratch=[pltpu.VMEM((d, 2 * d), F32)] * 4 + [pltpu.VMEM((2 * d, d), BF16), sem((5,))],
    )
    return input_grad, update, left_new[None], right_new[None]


def solution(mesh):
    fine = Mesh(mesh.devices.reshape(8, 2, 2, 4, 2), ("z", "xl", "xh", "y", "core"))
    row, col = ("z", "xl"), ("xh", "y", "core")
    in_specs = (
        P(col, row),
        P(row, col),
        P(col, row),
        P(col, row, None),
        P(col, row, None),
        P(col, row, None),
        P(col, None, row),
    )
    out_specs = (P(row, col), P(col, row), P(col, row, None), P(col, row, None))
    return jax.shard_map(local, mesh=fine, in_specs=in_specs, out_specs=out_specs, check_vma=False)
```

time: 137 us -> 143 us (1.044)
  waiting for transfers between devices: 55.2 us -> 80.2 us
  Pallas kernels: 0 us -> 24.4 us
  starting transfers between devices: 46.8 us -> 22.6 us
  matrix products: 14.5 us -> 0 us
  other arithmetic: 9.5 us -> 3.08 us
  local copies, waits for them, and re-layouts: 9.35 us -> 11.1 us
    ppermute x8 -> x17, waiting for transfers between devices: 9.64 us -> 35.7 us  [swap(): return lax.ppermute(value, axis, [(0, 1), (1, 0)])]
    ppermute x19 -> x11, starting transfers between devices: 34.7 us -> 8.72 us  [step(): return lax.ppermute(value, (axis, 'core'), pairs)]
    pallas_call x0 -> x11, Pallas kernels: none -> 24.4 us  [call(): pl.pallas_call(kernel, out_shape=[jax.ShapeDtypeStruct(s, t) for s, t in...]
    dot_general x10 -> x0, matrix products: 14.5 us -> none  [dot(): lax.dot_general(a, b, ((contract[:1], contract[1:]), ((), ())), preferred...]
    dynamic_update_slice x9 -> x0, local copies, waits for them, and re-layouts: 3.18 us -> none  [the longest x2 1.13 us: local(): cot_y = lax.dynamic_update_index_in_dim(cot_y, v, (y + k) % 4, 1)]
    unnamed x21 -> x29, local copies, waits for them, and re-layouts: 2.93 us -> 5.82 us
    another operation x3, other arithmetic: 3.13 us -> 0.95 us  [the longest x2 0.88 us: local(): z_0 = jnp.stack([act, swap(act, 'core')])]
    add x2 -> x0, other arithmetic: 1.87 us -> none  [the longest x1 1.75 us: local(): left_new = left_stats + left_gram * scale]
  transfers between devices with their start and end apart: 28 -> 29, of which waited for: 13 -> 13; matrix products, arithmetic and copies ran while one was open for 23% -> 4% of each run, Pallas kernels for 0% -> 17%
where the time goes in v2:
time: 143 us; the launch traced here: 142 us
  waiting for transfers between devices  80.2 us (56%)
  Pallas kernels  24.4 us (17%)
  starting transfers between devices  22.6 us (16%)
  local copies, waits for them, and re-layouts  11.1 us (8%)
  other arithmetic  3.08 us (2%)
    ppermute x11, waiting for transfers between devices, step(): return lax.ppermute(value, (axis, 'core'), pairs)  44.4 us
    ppermute x17, waiting for transfers between devices, swap(): return lax.ppermute(value, axis, [(0, 1), (1, 0)])  35.7 us
    pallas_call x11, Pallas kernels, call(): pl.pallas_call(kernel, out_shape=[jax.ShapeDtypeStruct(s, t) for s, t in...  24.4 us
    ppermute x17, starting transfers between devices, swap(): return lax.ppermute(value, axis, [(0, 1), (1, 0)])  12.3 us
    ppermute x11, starting transfers between devices, step(): return lax.ppermute(value, (axis, 'core'), pairs)  8.72 us
    unnamed x29, local copies, waits for them, and re-layouts  5.82 us
  transfers between devices with their start and end apart: 29, of which 13 were waited for; matrix products, arithmetic and copies ran while one was open for 4% of the time, Pallas kernels for 17%

profile of v2, /device:TPU:2, one launch (start us, length us, event | category | flops | bytes accessed | tf_op | source)
XLA Modules:
  0.0 142.2 jit_solution(2430131462503990038)
XLA Ops:
  0.7 2.3 %constant_dynamic-slice_fusion.1 = (bf16[512,512]{1,0:T(8,128)(2,1)}, bf16[512,512]{1,0:T(8,128)(2,1)}) fusion(bf16[1024,512]{1,0:T(8,128)(2,1)} %param.9, s32[]{:T(128)S(6)} %select_n.306, s32[]{:T(128)S(6)} %select_n.307), kind=kLoop, calls=%fused_computation.12 | loop fusion | bytes 2097160 | tf_op jit(solution)/shard_map/dynamic_slice | solution.py:36
  3.0 2.3 %collective-permute-start.10 = (bf16[512,512]{1,0:T(8,128)(2,1)}, bf16[512,512]{1,0:T(8,128)(2,1)S(1)}, u32[]{:S(2)}, u32[]{:S(2)}) collective-permute-start(bf16[512,512]{1,0:T(8,128)(2,1)} %get-tuple-element.37), channel_id=1, source_target_pairs={{0,16},{16,0},{1,17},{17,1},{2,18},{18,2},{3,19},{19,3},{4,20},{20... | collective-permute-start | bytes 1572872 | tf_op jit(solution)/shard_map/ppermute | solution.py:21
  9.1 17.2 %collective-permute-done.1.far = bf16[128,512]{1,0:T(8,128)(2,1)S(1)} collective-permute-done((bf16[128,512]{1,0:T(8,128)(2,1)S(1)}, bf16[128,512]{1,0:T(8,128)(2,1)S(1)}, u32[]{:S(2)}, u32[]{:S(2)}) %collective-permute-start.1) | collective-permute-done | bytes 131104 | tf_op jit(solution)/shard_map/ppermute | solution.py:21
  30.9 5.9 %collective-permute-done.4.refs_2_.refs_10_ = bf16[2,128,1024]{2,1,0:T(8,128)(2,1)S(1)} collective-permute-done((bf16[2,128,1024]{2,1,0:T(8,128)(2,1)S(1)}, bf16[2,128,1024]{2,1,0:T(8,128)(2,1)S(1)}, u32[]{:S(2)}, u32[]{:S(2)}) %collective-permute-start.4) | collective-permute-done | bytes 524320 | tf_op jit(solution)/shard_map/ppermute | solution.py:27
  40.9 6.3 %collective-permute-done.8.refs_6_.refs_14_ = bf16[2,128,1024]{2,1,0:T(8,128)(2,1)} collective-permute-done((bf16[2,128,1024]{2,1,0:T(8,128)(2,1)S(1)}, bf16[2,128,1024]{2,1,0:T(8,128)(2,1)}, u32[]{:S(2)}, u32[]{:S(2)}) %collective-permute-start.8) | collective-permute-done | bytes 524320 | tf_op jit(solution)/shard_map/ppermute | solution.py:27
  47.3 5.6 %collective-permute-done.5.refs_3_.refs_11_ = bf16[2,128,1024]{2,1,0:T(8,128)(2,1)} collective-permute-done((bf16[2,128,1024]{2,1,0:T(8,128)(2,1)}, bf16[2,128,1024]{2,1,0:T(8,128)(2,1)}, u32[]{:S(2)}, u32[]{:S(2)}) %collective-permute-start.5) | collective-permute-done | bytes 524320 | tf_op jit(solution)/shard_map/ppermute | solution.py:27
  53.7 1.9 %collective-permute-start.21 = (bf16[2,256,512]{2,1,0:T(8,128)(2,1)}, bf16[2,256,512]{2,1,0:T(8,128)(2,1)}, u32[]{:S(2)}, u32[]{:S(2)}) collective-permute-start(bf16[2,256,512]{2,1,0:T(8,128)(2,1)} %pad_maximum_fusion.1), channel_id=1, source_target_pairs={{0,32},{1,225},{32,64},{33,1},{64,96},{65,33},{96,128},{97,65},{12... | collective-permute-start | bytes 1572872 | tf_op jit(solution)/shard_map/ppermute | solution.py:27
  55.7 2.7 %shard_map.105 = bf16[256,512]{1,0:T(8,128)(2,1)} custom-call(s32[2]{0:T(128)S(1)} %pad_add_fusion.index, bf16[2,128,1024]{2,1,0:T(8,128)(2,1)S(1)} %shard_map.103.refs_0_.refs_8_, bf16[2,128,1024]{2,1,0:T(8,128)(2,1)} %collective-permute-done.3.refs_1_.refs_9_, bf16[2,128,1024]{2,1,0:T(8,128)(2,1)S(1)} %collective-permute-done.4.refs_2_.refs_10_, ...), custom_call_target="tpu_custom_call" | custom-call | tf_op jit(solution)/shard_map/pallas_call | solution.py:50
  58.4 2.1 %collective-permute-start.13 = (bf16[256,512]{1,0:T(8,128)(2,1)}, bf16[256,512]{1,0:T(8,128)(2,1)}, u32[]{:S(2)}, u32[]{:S(2)}) collective-permute-start(bf16[256,512]{1,0:T(8,128)(2,1)} %shard_map.105), channel_id=1, source_target_pairs={{0,32},{1,225},{32,64},{33,1},{64,96},{65,33},{96,128},{97,65},{12... | collective-permute-start | bytes 786440 | tf_op jit(solution)/shard_map/ppermute | solution.py:27
  60.5 6.5 %collective-permute-done.21.refs_1_ = bf16[2,256,512]{2,1,0:T(8,128)(2,1)} collective-permute-done((bf16[2,256,512]{2,1,0:T(8,128)(2,1)}, bf16[2,256,512]{2,1,0:T(8,128)(2,1)}, u32[]{:S(2)}, u32[]{:S(2)}) %collective-permute-start.21) | collective-permute-done | bytes 524320 | tf_op jit(solution)/shard_map/ppermute | solution.py:27
  67.1 5.0 %shard_map.104 = (f32[2,256,512]{2,1,0:T(8,128)S(1)}, f32[2,256,512]{2,1,0:T(8,128)S(1)}, f32[2,256,512]{2,1,0:T(8,128)S(1)}, f32[1,256,512]{2,1,0:T(8,128)S(1)}) custom-call(s32[8]{0:T(128)S(1)} %concatenate.18.index, bf16[2,128,1024]{2,1,0:T(8,128)(2,1)S(1)} %shard_map.103.refs_0_.refs_8_, bf16[2,128,1024]{2,1,0:T(8,128)(2,1)} %collective-permute-done.3.refs_1_.refs_9_, ...), custom_call_target="tpu_custom_call" | custom-call | tf_op jit(solution)/shard_map/pallas_call | solution.py:50
  74.1 3.6 %collective-permute-done.22.refs_2_ = bf16[2,256,512]{2,1,0:T(8,128)(2,1)} collective-permute-done((bf16[2,256,512]{2,1,0:T(8,128)(2,1)}, bf16[2,256,512]{2,1,0:T(8,128)(2,1)}, u32[]{:S(2)}, u32[]{:S(2)}) %collective-permute-start.22) | collective-permute-done | bytes 524320 | tf_op jit(solution)/shard_map/ppermute | solution.py:27
  77.8 6.8 %collective-permute-done.14.arrived = bf16[2,256,512]{2,1,0:T(8,128)(2,1)S(1)} collective-permute-done((bf16[2,256,512]{2,1,0:T(8,128)(2,1)S(1)}, bf16[2,256,512]{2,1,0:T(8,128)(2,1)S(1)}, u32[]{:S(2)}, u32[]{:S(2)}) %collective-permute-start.14) | collective-permute-done | bytes 524320 | tf_op jit(solution)/shard_map/ppermute | solution.py:27
  84.8 1.9 %collective-permute-start.19 = (bf16[256,1024]{1,0:T(8,128)(2,1)S(1)}, bf16[256,1024]{1,0:T(8,128)(2,1)}, u32[]{:S(2)}, u32[]{:S(2)}) collective-permute-start(bf16[256,1024]{1,0:T(8,128)(2,1)S(1)} %copy-done.12), channel_id=1, source_target_pairs={{0,16},{16,0},{1,17},{17,1},{2,18},{18,2},{3,19},{19,3},{4,20},{20... | collective-permute-start | bytes 1572872 | tf_op jit(solution)/shard_map/ppermute | solution.py:21
  87.3 2.8 %collective-permute-done.23.refs_3_ = bf16[2,256,512]{2,1,0:T(8,128)(2,1)S(1)} collective-permute-done((bf16[2,256,512]{2,1,0:T(8,128)(2,1)}, bf16[2,256,512]{2,1,0:T(8,128)(2,1)S(1)}, u32[]{:S(2)}, u32[]{:S(2)}) %collective-permute-start.23) | collective-permute-done | bytes 524320 | tf_op jit(solution)/shard_map/ppermute | solution.py:27
  91.2 4.6 %collective-permute-done.15.arrived = bf16[2,256,512]{2,1,0:T(8,128)(2,1)S(1)} collective-permute-done((bf16[2,256,512]{2,1,0:T(8,128)(2,1)S(1)}, bf16[2,256,512]{2,1,0:T(8,128)(2,1)S(1)}, u32[]{:S(2)}, u32[]{:S(2)}) %collective-permute-start.15) | collective-permute-done | bytes 524320 | tf_op jit(solution)/shard_map/ppermute | solution.py:27
  96.7 3.0 %collective-permute-done.19 = bf16[256,1024]{1,0:T(8,128)(2,1)} collective-permute-done((bf16[256,1024]{1,0:T(8,128)(2,1)S(1)}, bf16[256,1024]{1,0:T(8,128)(2,1)}, u32[]{:S(2)}, u32[]{:S(2)}) %collective-permute-start.19) | collective-permute-done | bytes 524320 | tf_op jit(solution)/shard_map/ppermute | solution.py:21
  101.5 2.1 %collective-permute-done.27.refs_7_ = bf16[256,512]{1,0:T(8,128)(2,1)} collective-permute-done((bf16[256,512]{1,0:T(8,128)(2,1)}, bf16[256,512]{1,0:T(8,128)(2,1)}, u32[]{:S(2)}, u32[]{:S(2)}) %collective-permute-start.27) | collective-permute-done | bytes 262176 | tf_op jit(solution)/shard_map/ppermute | solution.py:27
  105.8 4.6 %shard_map.110.grad.refs_0_ = bf16[512,1024]{1,0:T(8,128)(2,1)S(1)} custom-call(s32[16]{0:T(128)S(1)} %concatenate.21.index, bf16[256,512]{1,0:T(8,128)(2,1)S(1)} %get-tuple-element.41.refs_0_, bf16[2,256,512]{2,1,0:T(8,128)(2,1)} %collective-permute-done.21.refs_1_, bf16[2,256,512]{2,1,0:T(8,128)(2,1)} %collective-permute-done.22.refs_2_, ...), custom_call_target="tpu_custom_call" | custom-call | tf_op jit(solution)/shard_map/pallas_call | solution.py:50
  110.4 1.9 %collective-permute-start.28 = (bf16[512,1024]{1,0:T(8,128)(2,1)S(1)}, bf16[512,1024]{1,0:T(8,128)(2,1)}, u32[]{:S(2)}, u32[]{:S(2)}) collective-permute-start(bf16[512,1024]{1,0:T(8,128)(2,1)S(1)} %shard_map.110.grad.refs_0_), channel_id=1, source_target_pairs={{0,16},{16,0},{1,17},{17,1},{2,18},{18,2},{3,19},{19,3},{4,20},{20... | collective-permute-start | bytes 3145736 | tf_op jit(solution)/shard_map/ppermute | solution.py:21
  112.3 2.2 %collective-permute-done.17.sibling = bf16[2,256,512]{2,1,0:T(8,128)(2,1)} collective-permute-done((bf16[2,256,512]{2,1,0:T(8,128)(2,1)}, bf16[2,256,512]{2,1,0:T(8,128)(2,1)}, u32[]{:S(2)}, u32[]{:S(2)}) %collective-permute-start.17) | collective-permute-done | bytes 524320 | tf_op jit(solution)/shard_map/ppermute | solution.py:21
  119.6 2.4 %shard_map.111 = (f32[512,512]{1,0:T(8,128)S(1)}, f32[512,1024]{1,0:T(8,128)S(1)}, f32[1024,512]{1,0:T(8,128)S(1)}) custom-call(s32[1]{0:T(128)} %bitcast.13.index, bf16[512,1024]{1,0:T(8,128)(2,1)S(1)} %shard_map.110.grad.refs_0_, bf16[1024,512]{1,0:T(8,128)(2,1)S(1)} %bitcast.33, bf16[512,1024]{1,0:T(8,128)(2,1)S(1)} %bitcast.31, ...), custom_call_target="tpu_custom_call" | custom-call | tf_op jit(solution)/shard_map/pallas_call | solution.py:50
  122.1 13.3 %collective-permute-done.28.refs_1_ = bf16[512,1024]{1,0:T(8,128)(2,1)} collective-permute-done((bf16[512,1024]{1,0:T(8,128)(2,1)S(1)}, bf16[512,1024]{1,0:T(8,128)(2,1)}, u32[]{:S(2)}, u32[]{:S(2)}) %collective-permute-start.28) | collective-permute-done | bytes 1048608 | tf_op jit(solution)/shard_map/ppermute | solution.py:21
  135.4 6.1 %shard_map.112 = (f32[512,1024]{1,0:T(8,128)}, f32[512,1024]{1,0:T(8,128)}, bf16[1024,512]{1,0:T(8,128)(2,1)}) custom-call(s32[1]{0:T(128)} %bitcast.13.index, bf16[512,1024]{1,0:T(8,128)(2,1)S(1)} %shard_map.110.grad.refs_0_, bf16[512,1024]{1,0:T(8,128)(2,1)} %collective-permute-done.28.refs_1_, bf16[1024,512]{1,0:T(8,128)(2,1)S(1)} %bitcast.34, ...), custom_call_target="tpu_custom_call" | custom-call | tf_op jit(solution)/shard_map/pallas_call | solution.py:50
  (87 shorter events, 28.0 us)
Async XLA Ops:
  3.0 25.1 %collective-permute-start.10 = (bf16[512,512]{1,0:T(8,128)(2,1)}, bf16[512,512]{1,0:T(8,128)(2,1)S(1)}, u32[]{:S(2)}, u32[]{:S(2)}) collective-permute-start(bf16[512,512]{1,0:T(8,128)(2,1)} %get-tuple-element.37), channel_id=1, source_target_pairs={{0,16},{16,0},{1,17},{17,1},{2,18},{18,2},{3,19},{19,3},{4,20},{20... | collective-permute-start | bytes 1572872 | tf_op jit(solution)/shard_map/ppermute | solution.py:21
  5.5 20.7 %collective-permute-start = (bf16[256,512]{1,0:T(8,128)(2,1)S(1)}, bf16[256,512]{1,0:T(8,128)(2,1)S(1)}, u32[]{:S(2)}, u32[]{:S(2)}) collective-permute-start(bf16[256,512]{1,0:T(8,128)(2,1)S(1)} %shard_map.102), channel_id=1, source_target_pairs={{0,16},{16,0},{1,17},{17,1},{2,18},{18,2},{3,19},{19,3},{4,20},{20... | collective-permute-start | bytes 786440 | tf_op jit(solution)/shard_map/ppermute | solution.py:21
  5.6 20.6 %collective-permute-start.1 = (bf16[128,512]{1,0:T(8,128)(2,1)S(1)}, bf16[128,512]{1,0:T(8,128)(2,1)S(1)}, u32[]{:S(2)}, u32[]{:S(2)}) collective-permute-start(bf16[128,512]{1,0:T(8,128)(2,1)S(1)} %copy-done.11), channel_id=1, source_target_pairs={{0,8},{8,0},{1,9},{9,1},{2,10},{10,2},{3,11},{11,3},{4,12},{12,4},... | collective-permute-start | bytes 393224 | tf_op jit(solution)/shard_map/ppermute | solution.py:21
  7.5 18.8 %collective-permute-start.2 = (bf16[128,512]{1,0:T(8,128)(2,1)S(1)}, bf16[128,512]{1,0:T(8,128)(2,1)S(1)}, u32[]{:S(2)}, u32[]{:S(2)}) collective-permute-start(bf16[128,512]{1,0:T(8,128)(2,1)S(1)} %copy-done.11), channel_id=1, source_target_pairs={{0,24},{24,0},{8,16},{16,8},{1,25},{25,1},{9,17},{17,9},{2,26},{26... | collective-permute-start | bytes 393224 | tf_op jit(solution)/shard_map/ppermute | solution.py:31
  26.3 10.5 %collective-permute-start.4 = (bf16[2,128,1024]{2,1,0:T(8,128)(2,1)S(1)}, bf16[2,128,1024]{2,1,0:T(8,128)(2,1)S(1)}, u32[]{:S(2)}, u32[]{:S(2)}) collective-permute-start(bf16[2,128,1024]{2,1,0:T(8,128)(2,1)S(1)} %shard_map.103.refs_0_.refs_8_), channel_id=1, source_target_pairs={{0,2},{1,7},{2,4},{3,1},{4,6},{5,3},{6,0},{7,5},{8,10},{9,15},{10,... | collective-permute-start | bytes 1572872 | tf_op jit(solution)/shard_map/ppermute | solution.py:27
  27.9 9.2 %collective-permute-start.3 = (bf16[2,128,1024]{2,1,0:T(8,128)(2,1)S(1)}, bf16[2,128,1024]{2,1,0:T(8,128)(2,1)}, u32[]{:S(2)}, u32[]{:S(2)}) collective-permute-start(bf16[2,128,1024]{2,1,0:T(8,128)(2,1)S(1)} %shard_map.103.refs_0_.refs_8_), channel_id=1, source_target_pairs={{0,1},{1,0},{2,3},{3,2},{4,5},{5,4},{6,7},{7,6},{8,9},{9,8},{10,11... | collective-permute-start | bytes 1572872 | tf_op jit(solution)/shard_map/ppermute | solution.py:21
  29.0 24.7 %collective-permute-start.12 = (bf16[256,1024]{1,0:T(8,128)(2,1)S(1)}, bf16[256,1024]{1,0:T(8,128)(2,1)}, u32[]{:S(2)}, u32[]{:S(2)}) collective-permute-start(bf16[256,1024]{1,0:T(8,128)(2,1)S(1)} %get-tuple-element.35), channel_id=1, source_target_pairs={{0,16},{16,0},{1,17},{17,1},{2,18},{18,2},{3,19},{19,3},{4,20},{20... | collective-permute-start | bytes 1572872 | tf_op jit(solution)/shard_map/ppermute | solution.py:21
  36.8 10.5 %collective-permute-start.8 = (bf16[2,128,1024]{2,1,0:T(8,128)(2,1)S(1)}, bf16[2,128,1024]{2,1,0:T(8,128)(2,1)}, u32[]{:S(2)}, u32[]{:S(2)}) collective-permute-start(bf16[2,128,1024]{2,1,0:T(8,128)(2,1)S(1)} %collective-permute-done.4.refs_2_.refs_10_), channel_id=1, source_target_pairs={{0,2},{1,7},{2,4},{3,1},{4,6},{5,3},{6,0},{7,5},{8,10},{9,15},{10,... | collective-permute-start | bytes 1572872 | tf_op jit(solution)/shard_map/ppermute | solution.py:27
  37.1 15.7 %collective-permute-start.5 = (bf16[2,128,1024]{2,1,0:T(8,128)(2,1)}, bf16[2,128,1024]{2,1,0:T(8,128)(2,1)}, u32[]{:S(2)}, u32[]{:S(2)}) collective-permute-start(bf16[2,128,1024]{2,1,0:T(8,128)(2,1)} %collective-permute-done.3.refs_1_.refs_9_), channel_id=1, source_target_pairs={{0,2},{1,7},{2,4},{3,1},{4,6},{5,3},{6,0},{7,5},{8,10},{9,15},{10,... | collective-permute-start | bytes 1572872 | tf_op jit(solution)/shard_map/ppermute | solution.py:27
  40.2 26.9 %collective-permute-start.11 = (bf16[512,1024]{1,0:T(8,128)(2,1)S(1)}, bf16[512,1024]{1,0:T(8,128)(2,1)}, u32[]{:S(2)}, u32[]{:S(2)}) collective-permute-start(bf16[512,1024]{1,0:T(8,128)(2,1)S(1)} %pad_maximum_fusion.refs_8_), channel_id=1, source_target_pairs={{0,1},{1,0},{2,3},{3,2},{4,5},{5,4},{6,7},{7,6},{8,9},{9,8},{10,11... | collective-permute-start | bytes 3145736 | tf_op jit(solution)/shard_map/ppermute | solution.py:21
  40.8 14.9 %collective-permute-start.7 = (bf16[2,128,1024]{2,1,0:T(8,128)(2,1)S(1)}, bf16[2,128,1024]{2,1,0:T(8,128)(2,1)}, u32[]{:S(2)}, u32[]{:S(2)}) collective-permute-start(bf16[2,128,1024]{2,1,0:T(8,128)(2,1)S(1)} %collective-permute-done.4.refs_2_.refs_10_), channel_id=1, source_target_pairs={{0,1},{1,0},{2,3},{3,2},{4,5},{5,4},{6,7},{7,6},{8,9},{9,8},{10,11... | collective-permute-start | bytes 1572872 | tf_op jit(solution)/shard_map/ppermute | solution.py:21
  53.7 13.3 %collective-permute-start.21 = (bf16[2,256,512]{2,1,0:T(8,128)(2,1)}, bf16[2,256,512]{2,1,0:T(8,128)(2,1)}, u32[]{:S(2)}, u32[]{:S(2)}) collective-permute-start(bf16[2,256,512]{2,1,0:T(8,128)(2,1)} %pad_maximum_fusion.1), channel_id=1, source_target_pairs={{0,32},{1,225},{32,64},{33,1},{64,96},{65,33},{96,128},{97,65},{12... | collective-permute-start | bytes 1572872 | tf_op jit(solution)/shard_map/ppermute | solution.py:27
  58.4 14.5 %collective-permute-start.13 = (bf16[256,512]{1,0:T(8,128)(2,1)}, bf16[256,512]{1,0:T(8,128)(2,1)}, u32[]{:S(2)}, u32[]{:S(2)}) collective-permute-start(bf16[256,512]{1,0:T(8,128)(2,1)} %shard_map.105), channel_id=1, source_target_pairs={{0,32},{1,225},{32,64},{33,1},{64,96},{65,33},{96,128},{97,65},{12... | collective-permute-start | bytes 786440 | tf_op jit(solution)/shard_map/ppermute | solution.py:27
  67.1 10.7 %collective-permute-start.22 = (bf16[2,256,512]{2,1,0:T(8,128)(2,1)}, bf16[2,256,512]{2,1,0:T(8,128)(2,1)}, u32[]{:S(2)}, u32[]{:S(2)}) collective-permute-start(bf16[2,256,512]{2,1,0:T(8,128)(2,1)} %collective-permute-done.21.refs_1_), channel_id=1, source_target_pairs={{0,32},{1,225},{32,64},{33,1},{64,96},{65,33},{96,128},{97,65},{12... | collective-permute-start | bytes 1572872 | tf_op jit(solution)/shard_map/ppermute | solution.py:27
  74.0 10.5 %collective-permute-start.14 = (bf16[2,256,512]{2,1,0:T(8,128)(2,1)S(1)}, bf16[2,256,512]{2,1,0:T(8,128)(2,1)S(1)}, u32[]{:S(2)}, u32[]{:S(2)}) collective-permute-start(bf16[2,256,512]{2,1,0:T(8,128)(2,1)S(1)} %shard_map.106), channel_id=1, source_target_pairs={{0,32},{1,225},{32,64},{33,1},{64,96},{65,33},{96,128},{97,65},{12... | collective-permute-start | bytes 1572872 | tf_op jit(solution)/shard_map/ppermute | solution.py:27
  77.8 12.4 %collective-permute-start.23 = (bf16[2,256,512]{2,1,0:T(8,128)(2,1)}, bf16[2,256,512]{2,1,0:T(8,128)(2,1)S(1)}, u32[]{:S(2)}, u32[]{:S(2)}) collective-permute-start(bf16[2,256,512]{2,1,0:T(8,128)(2,1)} %collective-permute-done.22.refs_2_), channel_id=1, source_target_pairs={{0,32},{1,225},{32,64},{33,1},{64,96},{65,33},{96,128},{97,65},{12... | collective-permute-start | bytes 1572872 | tf_op jit(solution)/shard_map/ppermute | solution.py:27
  84.7 11.1 %collective-permute-start.15 = (bf16[2,256,512]{2,1,0:T(8,128)(2,1)S(1)}, bf16[2,256,512]{2,1,0:T(8,128)(2,1)S(1)}, u32[]{:S(2)}, u32[]{:S(2)}) collective-permute-start(bf16[2,256,512]{2,1,0:T(8,128)(2,1)S(1)} %shard_map.107), channel_id=1, source_target_pairs={{0,32},{1,225},{32,64},{33,1},{64,96},{65,33},{96,128},{97,65},{12... | collective-permute-start | bytes 1572872 | tf_op jit(solution)/shard_map/ppermute | solution.py:27
  84.8 14.9 %collective-permute-start.19 = (bf16[256,1024]{1,0:T(8,128)(2,1)S(1)}, bf16[256,1024]{1,0:T(8,128)(2,1)}, u32[]{:S(2)}, u32[]{:S(2)}) collective-permute-start(bf16[256,1024]{1,0:T(8,128)(2,1)S(1)} %copy-done.12), channel_id=1, source_target_pairs={{0,16},{16,0},{1,17},{17,1},{2,18},{18,2},{3,19},{19,3},{4,20},{20... | collective-permute-start | bytes 1572872 | tf_op jit(solution)/shard_map/ppermute | solution.py:21
  86.6 14.1 %collective-permute-start.24 = (bf16[2,256,512]{2,1,0:T(8,128)(2,1)}, bf16[2,256,512]{2,1,0:T(8,128)(2,1)S(1)}, u32[]{:S(2)}, u32[]{:S(2)}) collective-permute-start(bf16[2,256,512]{2,1,0:T(8,128)(2,1)} %collective-permute-done.21.refs_1_), channel_id=1, source_target_pairs={{0,1},{1,0},{2,3},{3,2},{4,5},{5,4},{6,7},{7,6},{8,9},{9,8},{10,11... | collective-permute-start | bytes 1572872 | tf_op jit(solution)/shard_map/ppermute | solution.py:21
  87.3 14.2 %collective-permute-start.25 = (bf16[2,256,512]{2,1,0:T(8,128)(2,1)}, bf16[2,256,512]{2,1,0:T(8,128)(2,1)}, u32[]{:S(2)}, u32[]{:S(2)}) collective-permute-start(bf16[2,256,512]{2,1,0:T(8,128)(2,1)} %collective-permute-done.22.refs_2_), channel_id=1, source_target_pairs={{0,1},{1,0},{2,3},{3,2},{4,5},{5,4},{6,7},{7,6},{8,9},{9,8},{10,11... | collective-permute-start | bytes 1572872 | tf_op jit(solution)/shard_map/ppermute | solution.py:21
  90.2 13.5 %collective-permute-start.26 = (bf16[2,256,512]{2,1,0:T(8,128)(2,1)S(1)}, bf16[2,256,512]{2,1,0:T(8,128)(2,1)}, u32[]{:S(2)}, u32[]{:S(2)}) collective-permute-start(bf16[2,256,512]{2,1,0:T(8,128)(2,1)S(1)} %collective-permute-done.23.refs_3_), channel_id=1, source_target_pairs={{0,1},{1,0},{2,3},{3,2},{4,5},{5,4},{6,7},{7,6},{8,9},{9,8},{10,11... | collective-permute-start | bytes 1572872 | tf_op jit(solution)/shard_map/ppermute | solution.py:21
  99.7 12.7 %collective-permute-start.16 = (bf16[2,256,512]{2,1,0:T(8,128)(2,1)}, bf16[2,256,512]{2,1,0:T(8,128)(2,1)}, u32[]{:S(2)}, u32[]{:S(2)}) collective-permute-start(bf16[2,256,512]{2,1,0:T(8,128)(2,1)} %shard_map.108), channel_id=1, source_target_pairs={{0,32},{1,225},{32,64},{33,1},{64,96},{65,33},{96,128},{97,65},{12... | collective-permute-start | bytes 1572872 | tf_op jit(solution)/shard_map/ppermute | solution.py:27
  110.4 24.9 %collective-permute-start.28 = (bf16[512,1024]{1,0:T(8,128)(2,1)S(1)}, bf16[512,1024]{1,0:T(8,128)(2,1)}, u32[]{:S(2)}, u32[]{:S(2)}) collective-permute-start(bf16[512,1024]{1,0:T(8,128)(2,1)S(1)} %shard_map.110.grad.refs_0_), channel_id=1, source_target_pairs={{0,16},{16,0},{1,17},{17,1},{2,18},{18,2},{3,19},{19,3},{4,20},{20... | collective-permute-start | bytes 3145736 | tf_op jit(solution)/shard_map/ppermute | solution.py:21
  116.9 24.6 %collective-permute-start.18 = (bf16[128,512]{1,0:T(8,128)(2,1)S(1)}, bf16[128,512]{1,0:T(8,128)(2,1)S(1)}, u32[]{:S(2)}, u32[]{:S(2)}) collective-permute-start(bf16[128,512]{1,0:T(8,128)(2,1)S(1)} %get-tuple-element.26), channel_id=1, source_target_pairs={{0,16},{16,0},{1,17},{17,1},{2,18},{18,2},{3,19},{19,3},{4,20},{20... | collective-permute-start | bytes 393224 | tf_op jit(solution)/shard_map/ppermute | solution.py:21
  (19 other events, 141.8 us)

commit v3 on v2

v3 whole, which is shorter than its diff:
```python
import jax
import jax.numpy as jnp
from jax import lax
from jax.experimental import pallas as pl
from jax.experimental.pallas import tpu as pltpu
from jax.sharding import Mesh, PartitionSpec as P

F32 = jnp.float32
BF16 = jnp.bfloat16
VMEM = pl.BlockSpec(memory_space=pltpu.VMEM)
SMEM = pl.BlockSpec(memory_space=pltpu.SMEM)
ANY = pl.BlockSpec(memory_space=pl.ANY)
PARAMS = pltpu.CompilerParams(vmem_limit_bytes=40 * 1024 * 1024)


def after(value, *others):
    return lax.optimization_barrier((value, *others))[0]


def swap(value, axis):
    return lax.ppermute(value, axis, [(0, 1), (1, 0)])


def shift(value, axis, distance):
    n = lax.axis_size(axis)
    return lax.ppermute(value, axis, [(i, (i + distance) % n) for i in range(n)])


def cross(value):
    return lax.ppermute(value, ("xl", "xh"), [(0, 3), (3, 0), (1, 2), (2, 1)])


def half(value, index, dim):
    size = value.shape[dim] // 2
    return lax.dynamic_slice_in_dim(value, index * size, size, dim)


def dot(a, b, contract):
    return lax.dot_general(a, b, ((contract[:1], contract[1:]), ((), ())), preferred_element_type=F32)


def order(h, own, other, dim):
    low = jnp.where(h == 0, own, other)
    high = jnp.where(h == 0, other, own)
    return jnp.concatenate([low, high], axis=dim)


def hbm(value):
    return pltpu.with_memory_space_constraint(value, pltpu.HBM)


def call(kernel, shapes, *args, specs=None, outs=None, scratch=(), first=()):
    n = len(args)
    specs = specs or [VMEM] * (n - 1)
    args = [args[0]] + [hbm(a) if s is ANY else a for a, s in zip(args[1:], specs)]
    first = [hbm(a) for a in first]

    def body(*refs):
        kernel(*refs[:n], *refs[n + len(first) :])

    return pl.pallas_call(
        body,
        out_shape=[jax.ShapeDtypeStruct(s, t) for s, t in shapes],
        in_specs=[SMEM] + specs + [ANY] * len(first),
        out_specs=outs or [VMEM] * len(shapes),
        scratch_shapes=list(scratch),
        compiler_params=PARAMS,
        cost_estimate=pl.CostEstimate(flops=0, bytes_accessed=0, transcendentals=0),
    )(*args, *first)


def fetch(y_at, x_at, pieces, tokens, sems):
    tok = pieces[0].shape[1]
    for k in range(4):

        @pl.when(y_at == k)
        def _(k=k):
            for side in range(2):
                target = tokens.at[pl.ds(side * tok, tok)]
                pltpu.make_async_copy(pieces[2 * k + side].at[x_at], target, sems.at[side]).start()


def fetched(pieces, tokens, sems):
    tok = pieces[0].shape[1]
    for side in range(2):
        target = tokens.at[pl.ds(side * tok, tok)]
        pltpu.make_async_copy(pieces[side].at[0], target, sems.at[side]).wait()


def far_kernel(index, *refs):
    pieces, (weight, up, down, tokens, sems) = refs[:8], refs[8:]
    fetch(index[0], index[1], pieces, tokens, sems)
    fetched(pieces, tokens, sems)
    rows = up.shape[0]
    part = dot(tokens[...], weight[...], (1, 1)).astype(BF16)
    up[...] = part[:rows]
    down[...] = part[rows:]


def part_kernel(index, *refs):
    pieces, weight, outs, (tokens, sems) = refs[:8], refs[8], refs[9:13], refs[13:]
    for k in range(7):
        fetch(index[2 * k], index[2 * k + 1], pieces, tokens.at[k], sems.at[k])
    for k in range(7):
        fetched(pieces, tokens.at[k], sems.at[k])
        outs[k // 2][k % 2] = dot(tokens[k], weight[...], (1, 1))


def grad_kernel(index, *refs):
    acts, pieces, (out, rows, tokens, total, row_sems, sems) = refs[:8], refs[8:16], refs[16:]
    copies = []
    for k in range(8):
        copies.append(pltpu.make_async_copy(acts[k], rows.at[k], row_sems.at[k]))
        copies[k].start()
        fetch(index[2 * k], index[2 * k + 1], pieces, tokens.at[k], sems.at[k])
    for k in range(8):
        copies[k].wait()
        fetched(pieces, tokens.at[k], sems.at[k])
        product = dot(rows[k], tokens[k], (0, 0))
        if k == 0:
            total[...] = product
        elif k < 7:
            total[...] += product
        else:
            out[...] = (total[...] + product).astype(BF16)


def weight_kernel(index, own, other, out, sems):
    rows, d = out.shape[0], own.shape[1]
    at = pl.ds(pl.multiple_of(index[0] * rows, rows), rows)
    copies = [
        pltpu.make_async_copy(own.at[at], out.at[:, pl.ds(0, d)], sems.at[0]),
        pltpu.make_async_copy(other.at[pl.ds(0, rows)], out.at[:, pl.ds(d, d)], sems.at[1]),
    ]
    for c in copies:
        c.start()
    for c in copies:
        c.wait()


def own_kernel(index, grad, right_root, left_root, root_other, left_out, right_out, up_out):
    h = index[0]
    d = grad.shape[0]
    scale = 1.0 / (2 * d)
    at = pl.ds(pl.multiple_of(h * d, d), d)
    there = pl.ds(pl.multiple_of((1 - h) * d, d), d)
    left_out[...] = dot(grad[...], grad[...], (1, 1)) * scale
    right_out[...] = dot(grad[:, :d], grad[...], (0, 0)) * scale
    m = (dot(grad[:, :d], right_root[at], (1, 0)) + dot(grad[:, d:], right_root[there], (1, 0))).astype(BF16)
    up_out[:d] = dot(left_root[:, at], m, (1, 0))
    up_out[d:] = dot(root_other[pl.ds(pl.multiple_of((1 + h) * d, d), d)], m, (1, 0))


def other_kernel(index, *refs):
    (grad, other, right_root, left_root, root_other, left_own, right_own, up_own) = refs[:8]
    left_stats, right_stats, left_new, right_new, update = refs[8:13]
    left_in, right_in, left_buf, right_buf, up_buf, sems = refs[13:]
    h = index[0]
    d = grad.shape[0]
    scale = 1.0 / (2 * d)
    at = pl.ds(pl.multiple_of(h * d, d), d)
    there = pl.ds(pl.multiple_of((1 - h) * d, d), d)
    copy = pltpu.make_async_copy
    ins = [copy(left_stats, left_in, sems.at[0]), copy(right_stats, right_in, sems.at[1])]
    outs = [
        copy(up_buf, update, sems.at[2]),
        copy(left_buf, left_new, sems.at[3]),
        copy(right_buf, right_new, sems.at[4]),
    ]
    for c in ins:
        c.start()
    m = dot(other[:, d:], right_root[at], (1, 0)) + dot(other[:, :d], right_root[there], (1, 0))
    m = m.astype(BF16)
    up_buf[at] = (up_own[:d] + dot(left_root[:, there], m, (1, 0))).astype(BF16)
    part = up_own[d:] + dot(root_other[pl.ds(pl.multiple_of((2 - h) * d, d), d)], m, (1, 0))
    up_buf[there] = part.astype(BF16)
    outs[0].start()
    gram = dot(grad[:, :d], other[:, d:], (1, 1)) + dot(grad[:, d:], other[:, :d], (1, 1))
    ins[0].wait()
    left_buf[:, at] = left_in[:, at] + left_own[...]
    left_buf[:, there] = left_in[:, there] + gram * scale
    outs[1].start()
    mine = other[:, d:]
    gram = dot(mine, other[:, d:], (0, 0))
    ins[1].wait()
    right_buf[:, at] = right_in[:, at] + right_own[:, :d] + gram * scale
    gram = dot(mine, other[:, :d], (0, 0))
    right_buf[:, there] = right_in[:, there] + right_own[:, d:] + gram * scale
    outs[2].start()
    for c in outs:
        c.wait()


def cot_kernel(index, own, pair, far, cross_block, out):
    tok, d = own.shape
    out[0, :, :d] = own[...]
    out[0, :, d:] = pair[tok:]
    out[1, :, :d] = far[...]
    out[1, :, d:] = cross_block[...]


def add_kernel(index, part, up, down, up_out, down_out):
    if up.shape == up_out.shape:
        up_out[...] = (part[0] + up[...].astype(F32)).astype(BF16)
        down_out[...] = (part[1] + down[...].astype(F32)).astype(BF16)
    else:
        rows = up.shape[0]
        up_out[:rows] = (part[0, :rows] + up[...].astype(F32)).astype(BF16)
        up_out[rows:] = part[0, rows:].astype(BF16)
        down_out[:rows] = part[1, :rows].astype(BF16)
        down_out[rows:] = (part[1, rows:] + down[...].astype(F32)).astype(BF16)


def last_kernel(index, part, up, down, keep, send):
    rows = keep.shape[0]

    def total(k):
        at = pl.ds(pl.multiple_of(k * rows, rows), rows)
        return part[0, at] + up[at].astype(F32) + down[at].astype(F32)

    keep[...] = total(index[0]).astype(BF16)
    send[...] = total(1 - index[0]).astype(BF16)


def local(cotangent, activations, down_weight, left_stats, right_stats, left_root, right_root):
    z = lax.axis_index("z")
    h = lax.axis_index("xl")
    xh = lax.axis_index("xh")
    y = lax.axis_index("y")
    core = lax.axis_index("core")
    tok, d = cotangent.shape
    block = left_root.shape[2]
    left_stats, right_stats, left_root, right_root = (
        v[0] for v in (left_stats, right_stats, left_root, right_root)
    )

    nothing = jnp.zeros((1,), jnp.int32)
    sem = pltpu.SemaphoreType.DMA

    both = swap(jnp.concatenate([half(activations, 1 - h, 1), cotangent], 0), "xl")
    cot_cross = cross(cotangent)
    cot_far = swap(cotangent, "xh")
    act = order(h ^ core, half(activations, h, 1), both[:tok], 0)
    near = jnp.concatenate([cotangent, both[tok:]], 1)
    far = jnp.concatenate([cot_far, cot_cross], 1)

    up_1, down_1 = shift(act, "z", 1), shift(act, "z", -1)
    up_2, down_2 = shift(up_1, "z", 1), shift(down_1, "z", -1)
    up_3, down_3 = shift(up_2, "z", 1), shift(down_2, "z", -1)
    up_4 = shift(up_3, "z", 1)

    cot = jnp.stack([near, far])
    cot_s = swap(cot, "core")
    y_up, y_down = shift(cot, "y", 1), shift(cot, "y", -1)
    s_up, s_down = swap(y_up, "core"), swap(y_down, "core")
    y_2 = jnp.stack([shift(y_up[0], "y", 1), shift(y_down[1], "y", -1)])
    s_2 = swap(y_2, "core")
    pieces = (cot, cot_s, y_up, s_up, y_down, s_down, y_2, s_2)

    send = after(half(down_weight, 1 - h, 0), cot)
    weight_root = swap(jnp.concatenate([send, left_root[:, :d], left_root[:, d:]], 0), "xl")
    weight = call(
        weight_kernel,
        [((d, 2 * d), BF16)],
        h[None],
        down_weight,
        weight_root,
        specs=[ANY] * 2,
        scratch=[sem((2,))],
    )[0]

    def places(*ks):
        out = []
        for k in ks:
            target = (z + k) % 8
            offset = (target % 4 - y) % 4
            out += [jnp.where(offset % 2 == 0, offset // 2 * 3, (offset % 4 == 1) + 1), xh ^ (target // 4)]
        return jnp.stack(out)

    grad = call(
        grad_kernel,
        [((d, 2 * d), BF16)],
        places(0, -1, -2, -3, 1, 2, 3, 4),
        act, up_1, up_2, up_3, down_1, down_2, down_3, up_4,
        *pieces,
        specs=[ANY] * 16,
        scratch=[
            pltpu.VMEM((8, 2 * tok, d), BF16),
            pltpu.VMEM((8, 2 * tok, 2 * d), BF16),
            pltpu.VMEM((d, 2 * d), F32),
            sem((8,)),
            sem((8, 2)),
        ],
    )[0]
    other = swap(grad, "xl")

    small, full = ((tok, d), BF16), ((2 * tok, d), BF16)
    up, down = call(
        far_kernel,
        [small, small],
        places(4),
        *pieces,
        weight,
        specs=[ANY] * 8 + [VMEM],
        scratch=[pltpu.VMEM((2 * tok, 2 * d), BF16), sem((2,))],
        first=[up_3, down_3],
    )
    *parts, part_0 = call(
        part_kernel,
        [((2, 2 * tok, d), F32)] * 3 + [((1, 2 * tok, d), F32)],
        places(3, -3, 2, -2, 1, -1, 0),
        *pieces,
        weight,
        specs=[ANY] * 8 + [VMEM],
        scratch=[pltpu.VMEM((7, 2 * tok, 2 * d), BF16), sem((7, 2))],
    )
    up, down = shift(up, "z", 1), shift(down, "z", -1)
    for k, part in enumerate(parts):
        up, down = call(add_kernel, [full, full], nothing, part, up, down)
        up, down = shift(up, "z", 1), shift(down, "z", -1)
    keep, send = call(last_kernel, [small, small], (h ^ core)[None], part_0, up, down)
    input_grad = order(h, keep, swap(send, "xl"), 1)

    left_own, right_own, up_own = call(
        own_kernel,
        [((d, d), F32), ((d, 2 * d), F32), ((2 * d, d), F32)],
        h[None],
        grad,
        right_root,
        left_root,
        weight_root,
    )
    stats = ((d, 2 * d), F32)
    left_new, right_new, update = call(
        other_kernel,
        [stats, stats, ((2 * d, d), BF16)],
        h[None],
        grad,
        other,
        right_root,
        left_root,
        weight_root,
        left_own,
        right_own,
        up_own,
        left_stats,
        right_stats,
        specs=[VMEM] * 8 + [ANY] * 2,
        outs=[ANY] * 3,
        scratch=[pltpu.VMEM((d, 2 * d), F32)] * 4 + [pltpu.VMEM((2 * d, d), BF16), sem((5,))],
    )
    return input_grad, update, left_new[None], right_new[None]


def solution(mesh):
    fine = Mesh(mesh.devices.reshape(8, 2, 2, 4, 2), ("z", "xl", "xh", "y", "core"))
    row, col = ("z", "xl"), ("xh", "y", "core")
    in_specs = (
        P(col, row),
        P(row, col),
        P(col, row),
        P(col, row, None),
        P(col, row, None),
        P(col, row, None),
        P(col, None, row),
    )
    out_specs = (P(row, col), P(col, row), P(col, row, None), P(col, row, None))
    return jax.shard_map(local, mesh=fine, in_specs=in_specs, out_specs=out_specs, check_vma=False)
```

time: 143 us -> 123 us (0.86)
  waiting for transfers between devices: 80.2 us -> 40.2 us
  starting transfers between devices: 22.6 us -> 44.1 us
  local copies, waits for them, and re-layouts: 11.1 us -> 6.45 us
  Pallas kernels: 24.4 us -> 26.7 us
    ppermute x17 -> x9, waiting for transfers between devices: 35.7 us -> 4.18 us  [swap(): return lax.ppermute(value, axis, [(0, 1), (1, 0)])]
    ppermute x11 -> x19, starting transfers between devices: 8.72 us -> 33.6 us  [shift(): lax.ppermute(value, axis, [(i, (i + distance) % n) for i in range(n)])]
    ppermute x11 -> x19, waiting for transfers between devices: 44.4 us -> 36 us  [shift(): lax.ppermute(value, axis, [(i, (i + distance) % n) for i in range(n)])]
    unnamed x29 -> x30, local copies, waits for them, and re-layouts: 5.82 us -> 2.08 us
    ppermute x17 -> x9, starting transfers between devices: 12.3 us -> 8.92 us  [swap(): return lax.ppermute(value, axis, [(0, 1), (1, 0)])]
    pallas_call x11 -> x10, Pallas kernels: 24.4 us -> 26.7 us  [call(): pl.pallas_call(body, out_shape=[jax.ShapeDtypeStruct(s, t) for s, t in sh...]
  transfers between devices with their start and end apart: 29 -> 29, of which waited for: 13 -> 12; matrix products, arithmetic and copies ran while one was open for 4% -> 6% of each run, Pallas kernels for 17% -> 22%
where the time goes in v3:
time: 123 us; the launch traced here: 122 us
  starting transfers between devices  44.1 us (36%)
  waiting for transfers between devices  40.2 us (33%)
  Pallas kernels  26.7 us (22%)
  local copies, waits for them, and re-layouts  6.45 us (5%)
  other arithmetic  3.87 us (3%)
    ppermute x19, waiting for transfers between devices, shift(): lax.ppermute(value, axis, [(i, (i + distance) % n) for i in range(n)])  36 us
    ppermute x19, starting transfers between devices, shift(): lax.ppermute(value, axis, [(i, (i + distance) % n) for i in range(n)])  33.6 us
    pallas_call x10, Pallas kernels, call(): pl.pallas_call(body, out_shape=[jax.ShapeDtypeStruct(s, t) for s, t in sh...  26.7 us
    ppermute x9, starting transfers between devices, swap(): return lax.ppermute(value, axis, [(0, 1), (1, 0)])  8.92 us
    ppermute x9, waiting for transfers between devices, swap(): return lax.ppermute(value, axis, [(0, 1), (1, 0)])  4.18 us
  transfers between devices with their start and end apart: 29, of which 12 were waited for; matrix products, arithmetic and copies ran while one was open for 6% of the time, Pallas kernels for 22%

profile of v3, /device:TPU:2, one launch (start us, length us, event | category | flops | bytes accessed | tf_op | source)
XLA Modules:
  0.0 122.3 jit_solution(8526977835245050020)
XLA Ops:
  2.2 2.8 %collective-permute-start.1 = (bf16[128,512]{1,0:T(8,128)(2,1)}, bf16[128,512]{1,0:T(8,128)(2,1)}, u32[]{:S(2)}, u32[]{:S(2)}) collective-permute-start(bf16[128,512]{1,0:T(8,128)(2,1)} %param.7), channel_id=1, source_target_pairs={{0,8},{8,0},{1,9},{9,1},{2,10},{10,2},{3,11},{11,3},{4,12},{12,4},... | collective-permute-start | bytes 393224 | tf_op jit(solution)/shard_map/ppermute | solution.py:21
  10.3 3.4 %collective-permute-done = bf16[256,512]{1,0:T(8,128)(2,1)S(1)} collective-permute-done((bf16[256,512]{1,0:T(8,128)(2,1)S(1)}, bf16[256,512]{1,0:T(8,128)(2,1)S(1)}, u32[]{:S(2)}, u32[]{:S(2)}) %collective-permute-start) | collective-permute-done | bytes 262176 | tf_op jit(solution)/shard_map/ppermute | solution.py:21
  13.8 3.1 %collective-permute-start.6 = (bf16[2,128,1024]{2,1,0:T(8,128)(2,1)S(1)}, bf16[2,128,1024]{2,1,0:T(8,128)(2,1)}, u32[]{:S(2)}, u32[]{:S(2)}) collective-permute-start(bf16[2,128,1024]{2,1,0:T(8,128)(2,1)S(1)} %pad_maximum_fusion.1.refs_1_.refs_9_), channel_id=1, source_target_pairs={{0,6},{2,0},{4,2},{6,4},{1,7},{3,1},{5,3},{7,5},{8,14},{10,8},{12,... | collective-permute-start | bytes 1572872 | tf_op jit(solution)/shard_map/ppermute | solution.py:26
  19.8 4.0 %collective-permute-start.15 = (bf16[256,512]{1,0:T(8,128)(2,1)S(1)}, bf16[256,512]{1,0:T(8,128)(2,1)S(1)}, u32[]{:S(2)}, u32[]{:S(2)}) collective-permute-start(bf16[256,512]{1,0:T(8,128)(2,1)S(1)} %pad_maximum_fusion.4.refs_1_), channel_id=1, source_target_pairs={{0,224},{32,0},{64,32},{96,64},{128,96},{160,128},{192,160},{224,1... | collective-permute-start | bytes 786440 | tf_op jit(solution)/shard_map/ppermute | solution.py:26
  23.8 4.8 %collective-permute-done.12.refs_2_ = bf16[256,512]{1,0:T(8,128)(2,1)S(1)} collective-permute-done((bf16[256,512]{1,0:T(8,128)(2,1)S(1)}, bf16[256,512]{1,0:T(8,128)(2,1)S(1)}, u32[]{:S(2)}, u32[]{:S(2)}) %collective-permute-start.12) | collective-permute-done | bytes 262176 | tf_op jit(solution)/shard_map/ppermute | solution.py:26
  31.3 3.0 %collective-permute-start.9 = (bf16[128,1024]{1,0:T(8,128)(2,1)S(1)}, bf16[128,1024]{1,0:T(8,128)(2,1)S(1)}, u32[]{:S(2)}, u32[]{:S(2)}) collective-permute-start(bf16[128,1024]{1,0:T(8,128)(2,1)S(1)} %slice_bitcast_fusion), channel_id=1, source_target_pairs={{0,6},{2,0},{4,2},{6,4},{1,7},{3,1},{5,3},{7,5},{8,14},{10,8},{12,... | collective-permute-start | bytes 786440 | tf_op jit(solution)/shard_map/ppermute | solution.py:26
  35.3 3.2 %collective-permute-done.13.refs_3_ = bf16[256,512]{1,0:T(8,128)(2,1)S(1)} collective-permute-done((bf16[256,512]{1,0:T(8,128)(2,1)S(1)}, bf16[256,512]{1,0:T(8,128)(2,1)S(1)}, u32[]{:S(2)}, u32[]{:S(2)}) %collective-permute-start.13) | collective-permute-done | bytes 262176 | tf_op jit(solution)/shard_map/ppermute | solution.py:26
  40.2 3.1 %collective-permute-done.8 = bf16[128,1024]{1,0:T(8,128)(2,1)S(1)} collective-permute-done((bf16[128,1024]{1,0:T(8,128)(2,1)S(1)}, bf16[128,1024]{1,0:T(8,128)(2,1)S(1)}, u32[]{:S(2)}, u32[]{:S(2)}) %collective-permute-start.8) | collective-permute-done | bytes 262176 | tf_op jit(solution)/shard_map/ppermute | solution.py:26
  46.2 5.0 %collective-permute-done.14.refs_10_.refs_4_ = bf16[256,512]{1,0:T(8,128)(2,1)S(1)} collective-permute-done((bf16[256,512]{1,0:T(8,128)(2,1)S(1)}, bf16[256,512]{1,0:T(8,128)(2,1)S(1)}, u32[]{:S(2)}, u32[]{:S(2)}) %collective-permute-start.14) | collective-permute-done | bytes 262176 | tf_op jit(solution)/shard_map/ppermute | solution.py:26
  55.7 2.2 %collective-permute-done.17.refs_11_.refs_7_ = bf16[256,512]{1,0:T(8,128)(2,1)} collective-permute-done((bf16[256,512]{1,0:T(8,128)(2,1)}, bf16[256,512]{1,0:T(8,128)(2,1)}, u32[]{:S(2)}, u32[]{:S(2)}) %collective-permute-start.17) | collective-permute-done | bytes 262176 | tf_op jit(solution)/shard_map/ppermute | solution.py:26
  58.7 2.1 %shard_map.104 = (bf16[128,512]{1,0:T(8,128)(2,1)S(1)}, bf16[128,512]{1,0:T(8,128)(2,1)S(1)}) custom-call(s32[2]{0:T(128)S(1)} %pad_add_fusion.refs_0_, bf16[2,128,1024]{2,1,0:T(8,128)(2,1)} %copy-done.4, bf16[2,128,1024]{2,1,0:T(8,128)(2,1)} %copy-done.5, bf16[2,128,1024]{2,1,0:T(8,128)(2,1)} %collective-permute-done.4.refs_3_.refs_11_, ...), custom_call_target="tpu_custom_call" | custom-call | tf_op jit(solution)/shard_map/pallas_call | solution.py:61
  61.4 2.8 %collective-permute-start.19 = (bf16[128,512]{1,0:T(8,128)(2,1)S(1)}, bf16[128,512]{1,0:T(8,128)(2,1)S(1)}, u32[]{:S(2)}, u32[]{:S(2)}) collective-permute-start(bf16[128,512]{1,0:T(8,128)(2,1)S(1)} %get-tuple-element.31), channel_id=1, source_target_pairs={{0,224},{32,0},{64,32},{96,64},{128,96},{160,128},{192,160},{224,1... | collective-permute-start | bytes 393224 | tf_op jit(solution)/shard_map/ppermute | solution.py:26
  64.3 6.7 %shard_map.109.refs_1_ = bf16[512,1024]{1,0:T(8,128)(2,1)} custom-call(s32[16]{0:T(128)S(1)} %stack.115.refs_0_, bf16[256,512]{1,0:T(8,128)(2,1)} %copy-done.9, bf16[256,512]{1,0:T(8,128)(2,1)} %copy-done.12, bf16[256,512]{1,0:T(8,128)(2,1)} %copy-done.14, bf16[256,512]{1,0:T(8,128)(2,1)} %copy-done.8, bf16[256,512]{1,0:T(8,128)(2,1)} %copy-done.13, ...), custom_call_target="tpu_custom_call" | custom-call | tf_op jit(solution)/shard_map/pallas_call | solution.py:61
  71.0 2.8 %collective-permute-start.28 = (bf16[512,1024]{1,0:T(8,128)(2,1)}, bf16[512,1024]{1,0:T(8,128)(2,1)}, u32[]{:S(2)}, u32[]{:S(2)}) collective-permute-start(bf16[512,1024]{1,0:T(8,128)(2,1)} %shard_map.109.refs_1_), channel_id=1, source_target_pairs={{0,16},{16,0},{1,17},{17,1},{2,18},{18,2},{3,19},{19,3},{4,20},{20... | collective-permute-start | bytes 3145736 | tf_op jit(solution)/shard_map/ppermute | solution.py:21
  73.9 5.0 %shard_map.103 = (f32[2,256,512]{2,1,0:T(8,128)S(1)}, f32[2,256,512]{2,1,0:T(8,128)S(1)}, f32[2,256,512]{2,1,0:T(8,128)S(1)}, f32[1,256,512]{2,1,0:T(8,128)S(1)}) custom-call(s32[14]{0:T(128)S(1)} %stack.105.refs_0_, bf16[2,128,1024]{2,1,0:T(8,128)(2,1)} %copy-done.4, bf16[2,128,1024]{2,1,0:T(8,128)(2,1)} %copy-done.5, ...), custom_call_target="tpu_custom_call" | custom-call | tf_op jit(solution)/shard_map/pallas_call | solution.py:61
  79.1 3.2 %collective-permute-start.21 = (bf16[256,512]{1,0:T(8,128)(2,1)S(1)}, bf16[256,512]{1,0:T(8,128)(2,1)S(1)}, u32[]{:S(2)}, u32[]{:S(2)}) collective-permute-start(bf16[256,512]{1,0:T(8,128)(2,1)S(1)} %get-tuple-element.33), channel_id=1, source_target_pairs={{0,224},{32,0},{64,32},{96,64},{128,96},{160,128},{192,160},{224,1... | collective-permute-start | bytes 786440 | tf_op jit(solution)/shard_map/ppermute | solution.py:26
  82.3 4.8 %collective-permute-done.20.refs_2_ = bf16[256,512]{1,0:T(8,128)(2,1)S(1)} collective-permute-done((bf16[256,512]{1,0:T(8,128)(2,1)S(1)}, bf16[256,512]{1,0:T(8,128)(2,1)S(1)}, u32[]{:S(2)}, u32[]{:S(2)}) %collective-permute-start.20) | collective-permute-done | bytes 262176 | tf_op jit(solution)/shard_map/ppermute | solution.py:26
  87.3 3.5 %collective-permute-start.23 = (bf16[256,512]{1,0:T(8,128)(2,1)S(1)}, bf16[256,512]{1,0:T(8,128)(2,1)S(1)}, u32[]{:S(2)}, u32[]{:S(2)}) collective-permute-start(bf16[256,512]{1,0:T(8,128)(2,1)S(1)} %get-tuple-element.35), channel_id=1, source_target_pairs={{0,224},{32,0},{64,32},{96,64},{128,96},{160,128},{192,160},{224,1... | collective-permute-start | bytes 786440 | tf_op jit(solution)/shard_map/ppermute | solution.py:26
  90.8 5.5 %collective-permute-done.22.refs_2_ = bf16[256,512]{1,0:T(8,128)(2,1)S(1)} collective-permute-done((bf16[256,512]{1,0:T(8,128)(2,1)S(1)}, bf16[256,512]{1,0:T(8,128)(2,1)S(1)}, u32[]{:S(2)}, u32[]{:S(2)}) %collective-permute-start.22) | collective-permute-done | bytes 262176 | tf_op jit(solution)/shard_map/ppermute | solution.py:26
  96.4 4.0 %collective-permute-start.24 = (bf16[256,512]{1,0:T(8,128)(2,1)S(1)}, bf16[256,512]{1,0:T(8,128)(2,1)S(1)}, u32[]{:S(2)}, u32[]{:S(2)}) collective-permute-start(bf16[256,512]{1,0:T(8,128)(2,1)S(1)} %get-tuple-element.36), channel_id=1, source_target_pairs={{0,32},{32,64},{64,96},{96,128},{128,160},{160,192},{192,224},{224... | collective-permute-start | bytes 786440 | tf_op jit(solution)/shard_map/ppermute | solution.py:26
  100.4 4.3 %collective-permute-done.24.refs_2_ = bf16[256,512]{1,0:T(8,128)(2,1)S(1)} collective-permute-done((bf16[256,512]{1,0:T(8,128)(2,1)S(1)}, bf16[256,512]{1,0:T(8,128)(2,1)S(1)}, u32[]{:S(2)}, u32[]{:S(2)}) %collective-permute-start.24) | collective-permute-done | bytes 262176 | tf_op jit(solution)/shard_map/ppermute | solution.py:26
  104.7 2.3 %collective-permute-done.25.refs_3_ = bf16[256,512]{1,0:T(8,128)(2,1)S(1)} collective-permute-done((bf16[256,512]{1,0:T(8,128)(2,1)S(1)}, bf16[256,512]{1,0:T(8,128)(2,1)S(1)}, u32[]{:S(2)}, u32[]{:S(2)}) %collective-permute-start.25) | collective-permute-done | bytes 262176 | tf_op jit(solution)/shard_map/ppermute | solution.py:26
  110.2 3.7 %shard_map.110 = (f32[512,512]{1,0:T(8,128)S(1)}, f32[512,1024]{1,0:T(8,128)S(1)}, f32[1024,512]{1,0:T(8,128)S(1)}) custom-call(s32[1]{0:T(128)} %bitcast.21.refs_0_, bf16[512,1024]{1,0:T(8,128)(2,1)} %shard_map.109.refs_1_, bf16[1024,512]{1,0:T(8,128)(2,1)S(1)} %bitcast.37, bf16[512,1024]{1,0:T(8,128)(2,1)S(1)} %bitcast.35, bf16[1536,512]{1,0:T(8,128)(2,1)S(1)} %copy-done.1), custom_call_target="tpu_custom_call" | custom-call | tf_op jit(solution)/shard_map/pallas_call | solution.py:61
  113.9 7.6 %shard_map.111 = (f32[512,1024]{1,0:T(8,128)}, f32[512,1024]{1,0:T(8,128)}, bf16[1024,512]{1,0:T(8,128)(2,1)}) custom-call(s32[1]{0:T(128)} %bitcast.21.refs_0_, bf16[512,1024]{1,0:T(8,128)(2,1)} %shard_map.109.refs_1_, bf16[512,1024]{1,0:T(8,128)(2,1)} %collective-permute-done.28.refs_2_, bf16[1024,512]{1,0:T(8,128)(2,1)S(1)} %bitcast.38, ...), custom_call_target="tpu_custom_call" | custom-call | tf_op jit(solution)/shard_map/pallas_call | solution.py:61
  (92 shorter events, 28.5 us)
Async XLA Ops:
  0.6 7.8 %collective-permute-start.2 = (bf16[128,512]{1,0:T(8,128)(2,1)}, bf16[128,512]{1,0:T(8,128)(2,1)}, u32[]{:S(2)}, u32[]{:S(2)}) collective-permute-start(bf16[128,512]{1,0:T(8,128)(2,1)} %param.7), channel_id=1, source_target_pairs={{0,24},{24,0},{8,16},{16,8},{1,25},{25,1},{9,17},{17,9},{2,26},{26... | collective-permute-start | bytes 393224 | tf_op jit(solution)/shard_map/ppermute | solution.py:30
  13.8 14.8 %collective-permute-start.6 = (bf16[2,128,1024]{2,1,0:T(8,128)(2,1)S(1)}, bf16[2,128,1024]{2,1,0:T(8,128)(2,1)}, u32[]{:S(2)}, u32[]{:S(2)}) collective-permute-start(bf16[2,128,1024]{2,1,0:T(8,128)(2,1)S(1)} %pad_maximum_fusion.1.refs_1_.refs_9_), channel_id=1, source_target_pairs={{0,6},{2,0},{4,2},{6,4},{1,7},{3,1},{5,3},{7,5},{8,14},{10,8},{12,... | collective-permute-start | bytes 1572872 | tf_op jit(solution)/shard_map/ppermute | solution.py:26
  17.0 36.2 %collective-permute-start.11 = (bf16[1536,512]{1,0:T(8,128)(2,1)S(1)}, bf16[1536,512]{1,0:T(8,128)(2,1)S(1)}, u32[]{:S(2)}, u32[]{:S(2)}) collective-permute-start(bf16[1536,512]{1,0:T(8,128)(2,1)S(1)} %pad_maximum_fusion), channel_id=1, source_target_pairs={{0,16},{16,0},{1,17},{17,1},{2,18},{18,2},{3,19},{19,3},{4,20},{20... | collective-permute-start | bytes 4718600 | tf_op jit(solution)/shard_map/ppermute | solution.py:21
  17.7 13.5 %collective-permute-start.4 = (bf16[2,128,1024]{2,1,0:T(8,128)(2,1)S(1)}, bf16[2,128,1024]{2,1,0:T(8,128)(2,1)}, u32[]{:S(2)}, u32[]{:S(2)}) collective-permute-start(bf16[2,128,1024]{2,1,0:T(8,128)(2,1)S(1)} %pad_maximum_fusion.1.refs_1_.refs_9_), channel_id=1, source_target_pairs={{0,2},{2,4},{4,6},{6,0},{1,3},{3,5},{5,7},{7,1},{8,10},{10,12},{12... | collective-permute-start | bytes 1572872 | tf_op jit(solution)/shard_map/ppermute | solution.py:26
  18.2 10.4 %collective-permute-start.12 = (bf16[256,512]{1,0:T(8,128)(2,1)S(1)}, bf16[256,512]{1,0:T(8,128)(2,1)S(1)}, u32[]{:S(2)}, u32[]{:S(2)}) collective-permute-start(bf16[256,512]{1,0:T(8,128)(2,1)S(1)} %pad_maximum_fusion.4.refs_1_), channel_id=1, source_target_pairs={{0,32},{32,64},{64,96},{96,128},{128,160},{160,192},{192,224},{224... | collective-permute-start | bytes 786440 | tf_op jit(solution)/shard_map/ppermute | solution.py:26
  19.8 15.5 %collective-permute-start.15 = (bf16[256,512]{1,0:T(8,128)(2,1)S(1)}, bf16[256,512]{1,0:T(8,128)(2,1)S(1)}, u32[]{:S(2)}, u32[]{:S(2)}) collective-permute-start(bf16[256,512]{1,0:T(8,128)(2,1)S(1)} %pad_maximum_fusion.4.refs_1_), channel_id=1, source_target_pairs={{0,224},{32,0},{64,32},{96,64},{128,96},{160,128},{192,160},{224,1... | collective-permute-start | bytes 786440 | tf_op jit(solution)/shard_map/ppermute | solution.py:26
  28.6 17.1 %collective-permute-start.3 = (bf16[2,128,1024]{2,1,0:T(8,128)(2,1)S(1)}, bf16[2,128,1024]{2,1,0:T(8,128)(2,1)S(1)}, u32[]{:S(2)}, u32[]{:S(2)}) collective-permute-start(bf16[2,128,1024]{2,1,0:T(8,128)(2,1)S(1)} %pad_maximum_fusion.1.refs_1_.refs_9_), channel_id=1, source_target_pairs={{0,1},{1,0},{2,3},{3,2},{4,5},{5,4},{6,7},{7,6},{8,9},{9,8},{10,11... | collective-permute-start | bytes 1572872 | tf_op jit(solution)/shard_map/ppermute | solution.py:21
  28.6 9.9 %collective-permute-start.13 = (bf16[256,512]{1,0:T(8,128)(2,1)S(1)}, bf16[256,512]{1,0:T(8,128)(2,1)S(1)}, u32[]{:S(2)}, u32[]{:S(2)}) collective-permute-start(bf16[256,512]{1,0:T(8,128)(2,1)S(1)} %collective-permute-done.12.refs_2_), channel_id=1, source_target_pairs={{0,32},{32,64},{64,96},{96,128},{128,160},{160,192},{192,224},{224... | collective-permute-start | bytes 786440 | tf_op jit(solution)/shard_map/ppermute | solution.py:26
  31.3 9.0 %collective-permute-start.9 = (bf16[128,1024]{1,0:T(8,128)(2,1)S(1)}, bf16[128,1024]{1,0:T(8,128)(2,1)S(1)}, u32[]{:S(2)}, u32[]{:S(2)}) collective-permute-start(bf16[128,1024]{1,0:T(8,128)(2,1)S(1)} %slice_bitcast_fusion), channel_id=1, source_target_pairs={{0,6},{2,0},{4,2},{6,4},{1,7},{3,1},{5,3},{7,5},{8,14},{10,8},{12,... | collective-permute-start | bytes 786440 | tf_op jit(solution)/shard_map/ppermute | solution.py:26
  35.2 8.1 %collective-permute-start.8 = (bf16[128,1024]{1,0:T(8,128)(2,1)S(1)}, bf16[128,1024]{1,0:T(8,128)(2,1)S(1)}, u32[]{:S(2)}, u32[]{:S(2)}) collective-permute-start(bf16[128,1024]{1,0:T(8,128)(2,1)S(1)} %slice_bitcast_fusion.1), channel_id=1, source_target_pairs={{0,2},{2,4},{4,6},{6,0},{1,3},{3,5},{5,7},{7,1},{8,10},{10,12},{12... | collective-permute-start | bytes 786440 | tf_op jit(solution)/shard_map/ppermute | solution.py:26
  40.2 17.7 %collective-permute-start.7 = (bf16[2,128,1024]{2,1,0:T(8,128)(2,1)}, bf16[2,128,1024]{2,1,0:T(8,128)(2,1)}, u32[]{:S(2)}, u32[]{:S(2)}) collective-permute-start(bf16[2,128,1024]{2,1,0:T(8,128)(2,1)} %collective-permute-done.6.refs_5_.refs_13_), channel_id=1, source_target_pairs={{0,1},{1,0},{2,3},{3,2},{4,5},{5,4},{6,7},{7,6},{8,9},{9,8},{10,11... | collective-permute-start | bytes 1572872 | tf_op jit(solution)/shard_map/ppermute | solution.py:21
  43.3 7.9 %collective-permute-start.14 = (bf16[256,512]{1,0:T(8,128)(2,1)S(1)}, bf16[256,512]{1,0:T(8,128)(2,1)S(1)}, u32[]{:S(2)}, u32[]{:S(2)}) collective-permute-start(bf16[256,512]{1,0:T(8,128)(2,1)S(1)} %collective-permute-done.13.refs_3_), channel_id=1, source_target_pairs={{0,32},{32,64},{64,96},{96,128},{128,160},{160,192},{192,224},{224... | collective-permute-start | bytes 786440 | tf_op jit(solution)/shard_map/ppermute | solution.py:26
  45.7 12.2 %collective-permute-start.5 = (bf16[2,128,1024]{2,1,0:T(8,128)(2,1)}, bf16[2,128,1024]{2,1,0:T(8,128)(2,1)}, u32[]{:S(2)}, u32[]{:S(2)}) collective-permute-start(bf16[2,128,1024]{2,1,0:T(8,128)(2,1)} %collective-permute-done.4.refs_3_.refs_11_), channel_id=1, source_target_pairs={{0,1},{1,0},{2,3},{3,2},{4,5},{5,4},{6,7},{7,6},{8,9},{9,8},{10,11... | collective-permute-start | bytes 1572872 | tf_op jit(solution)/shard_map/ppermute | solution.py:21
  45.7 12.2 %collective-permute-start.10 = (bf16[2,128,1024]{2,1,0:T(8,128)(2,1)}, bf16[2,128,1024]{2,1,0:T(8,128)(2,1)S(1)}, u32[]{:S(2)}, u32[]{:S(2)}) collective-permute-start(bf16[2,128,1024]{2,1,0:T(8,128)(2,1)} %pad_maximum_fusion.2.refs_7_.refs_15_), channel_id=1, source_target_pairs={{0,1},{1,0},{2,3},{3,2},{4,5},{5,4},{6,7},{7,6},{8,9},{9,8},{10,11... | collective-permute-start | bytes 1572872 | tf_op jit(solution)/shard_map/ppermute | solution.py:21
  53.2 11.0 %collective-permute-start.27 = (bf16[256,512]{1,0:T(8,128)(2,1)S(1)}, bf16[256,512]{1,0:T(8,128)(2,1)}, u32[]{:S(2)}, u32[]{:S(2)}) collective-permute-start(bf16[256,512]{1,0:T(8,128)(2,1)S(1)} %collective-permute-done.14.refs_10_.refs_4_), channel_id=1, source_target_pairs={{0,32},{32,64},{64,96},{96,128},{128,160},{160,192},{192,224},{224... | collective-permute-start | bytes 786440 | tf_op jit(solution)/shard_map/ppermute | solution.py:26
  60.8 18.1 %collective-permute-start.18 = (bf16[128,512]{1,0:T(8,128)(2,1)S(1)}, bf16[128,512]{1,0:T(8,128)(2,1)S(1)}, u32[]{:S(2)}, u32[]{:S(2)}) collective-permute-start(bf16[128,512]{1,0:T(8,128)(2,1)S(1)} %get-tuple-element.30), channel_id=1, source_target_pairs={{0,32},{32,64},{64,96},{96,128},{128,160},{160,192},{192,224},{224... | collective-permute-start | bytes 393224 | tf_op jit(solution)/shard_map/ppermute | solution.py:26
  61.4 17.5 %collective-permute-start.19 = (bf16[128,512]{1,0:T(8,128)(2,1)S(1)}, bf16[128,512]{1,0:T(8,128)(2,1)S(1)}, u32[]{:S(2)}, u32[]{:S(2)}) collective-permute-start(bf16[128,512]{1,0:T(8,128)(2,1)S(1)} %get-tuple-element.31), channel_id=1, source_target_pairs={{0,224},{32,0},{64,32},{96,64},{128,96},{160,128},{192,160},{224,1... | collective-permute-start | bytes 393224 | tf_op jit(solution)/shard_map/ppermute | solution.py:26
  71.0 42.9 %collective-permute-start.28 = (bf16[512,1024]{1,0:T(8,128)(2,1)}, bf16[512,1024]{1,0:T(8,128)(2,1)}, u32[]{:S(2)}, u32[]{:S(2)}) collective-permute-start(bf16[512,1024]{1,0:T(8,128)(2,1)} %shard_map.109.refs_1_), channel_id=1, source_target_pairs={{0,16},{16,0},{1,17},{17,1},{2,18},{18,2},{3,19},{19,3},{4,20},{20... | collective-permute-start | bytes 3145736 | tf_op jit(solution)/shard_map/ppermute | solution.py:21
  79.0 8.1 %collective-permute-start.20 = (bf16[256,512]{1,0:T(8,128)(2,1)S(1)}, bf16[256,512]{1,0:T(8,128)(2,1)S(1)}, u32[]{:S(2)}, u32[]{:S(2)}) collective-permute-start(bf16[256,512]{1,0:T(8,128)(2,1)S(1)} %get-tuple-element.32), channel_id=1, source_target_pairs={{0,32},{32,64},{64,96},{96,128},{128,160},{160,192},{192,224},{224... | collective-permute-start | bytes 786440 | tf_op jit(solution)/shard_map/ppermute | solution.py:26
  79.1 8.0 %collective-permute-start.21 = (bf16[256,512]{1,0:T(8,128)(2,1)S(1)}, bf16[256,512]{1,0:T(8,128)(2,1)S(1)}, u32[]{:S(2)}, u32[]{:S(2)}) collective-permute-start(bf16[256,512]{1,0:T(8,128)(2,1)S(1)} %get-tuple-element.33), channel_id=1, source_target_pairs={{0,224},{32,0},{64,32},{96,64},{128,96},{160,128},{192,160},{224,1... | collective-permute-start | bytes 786440 | tf_op jit(solution)/shard_map/ppermute | solution.py:26
  87.2 9.1 %collective-permute-start.22 = (bf16[256,512]{1,0:T(8,128)(2,1)S(1)}, bf16[256,512]{1,0:T(8,128)(2,1)S(1)}, u32[]{:S(2)}, u32[]{:S(2)}) collective-permute-start(bf16[256,512]{1,0:T(8,128)(2,1)S(1)} %get-tuple-element.34), channel_id=1, source_target_pairs={{0,32},{32,64},{64,96},{96,128},{128,160},{160,192},{192,224},{224... | collective-permute-start | bytes 786440 | tf_op jit(solution)/shard_map/ppermute | solution.py:26
  87.3 9.0 %collective-permute-start.23 = (bf16[256,512]{1,0:T(8,128)(2,1)S(1)}, bf16[256,512]{1,0:T(8,128)(2,1)S(1)}, u32[]{:S(2)}, u32[]{:S(2)}) collective-permute-start(bf16[256,512]{1,0:T(8,128)(2,1)S(1)} %get-tuple-element.35), channel_id=1, source_target_pairs={{0,224},{32,0},{64,32},{96,64},{128,96},{160,128},{192,160},{224,1... | collective-permute-start | bytes 786440 | tf_op jit(solution)/shard_map/ppermute | solution.py:26
  96.4 8.3 %collective-permute-start.24 = (bf16[256,512]{1,0:T(8,128)(2,1)S(1)}, bf16[256,512]{1,0:T(8,128)(2,1)S(1)}, u32[]{:S(2)}, u32[]{:S(2)}) collective-permute-start(bf16[256,512]{1,0:T(8,128)(2,1)S(1)} %get-tuple-element.36), channel_id=1, source_target_pairs={{0,32},{32,64},{64,96},{96,128},{128,160},{160,192},{192,224},{224... | collective-permute-start | bytes 786440 | tf_op jit(solution)/shard_map/ppermute | solution.py:26
  107.0 14.5 %collective-permute-start.26 = (bf16[128,512]{1,0:T(8,128)(2,1)S(1)}, bf16[128,512]{1,0:T(8,128)(2,1)S(1)}, u32[]{:S(2)}, u32[]{:S(2)}) collective-permute-start(bf16[128,512]{1,0:T(8,128)(2,1)S(1)} %get-tuple-element.39), channel_id=1, source_target_pairs={{0,16},{16,0},{1,17},{17,1},{2,18},{18,2},{3,19},{19,3},{4,20},{20... | collective-permute-start | bytes 393224 | tf_op jit(solution)/shard_map/ppermute | solution.py:21
  (20 other events, 216.9 us)

commit v4 on v3

--- a/solution.py
+++ b/solution.py
@@ -53,7 +53,6 @@
     n = len(args)
     specs = specs or [VMEM] * (n - 1)
     args = [args[0]] + [hbm(a) if s is ANY else a for a, s in zip(args[1:], specs)]
-    first = [hbm(a) for a in first]
 
     def body(*refs):
         kernel(*refs[:n], *refs[n + len(first) :])
@@ -87,23 +86,19 @@
         pltpu.make_async_copy(pieces[side].at[0], target, sems.at[side]).wait()
 
 
-def far_kernel(index, *refs):
-    pieces, (weight, up, down, tokens, sems) = refs[:8], refs[8:]
-    fetch(index[0], index[1], pieces, tokens, sems)
-    fetched(pieces, tokens, sems)
-    rows = up.shape[0]
-    part = dot(tokens[...], weight[...], (1, 1)).astype(BF16)
-    up[...] = part[:rows]
-    down[...] = part[rows:]
-
-
 def part_kernel(index, *refs):
-    pieces, weight, outs, (tokens, sems) = refs[:8], refs[8], refs[9:13], refs[13:]
-    for k in range(7):
+    pieces, weight, up, down, outs, (tokens, sems) = refs[:8], refs[8], refs[9], refs[10], refs[11:15], refs[15:]
+    for k in range(8):
         fetch(index[2 * k], index[2 * k + 1], pieces, tokens.at[k], sems.at[k])
-    for k in range(7):
+    for k in range(8):
         fetched(pieces, tokens.at[k], sems.at[k])
-        outs[k // 2][k % 2] = dot(tokens[k], weight[...], (1, 1))
+        part = dot(tokens[k], weight[...], (1, 1))
+        if k == 0:
+            rows = up.shape[0]
+            up[...] = part[:rows].astype(BF16)
+            down[...] = part[rows:].astype(BF16)
+        else:
+            outs[(k - 1) // 2][(k - 1) % 2] = part
 
 
 def grad_kernel(index, *refs):
@@ -148,7 +143,7 @@
     right_out[...] = dot(grad[:, :d], grad[...], (0, 0)) * scale
     m = (dot(grad[:, :d], right_root[at], (1, 0)) + dot(grad[:, d:], right_root[there], (1, 0))).astype(BF16)
     up_out[:d] = dot(left_root[:, at], m, (1, 0))
-    up_out[d:] = dot(root_other[pl.ds(pl.multiple_of((1 + h) * d, d), d)], m, (1, 0))
+    up_out[d:] = dot(root_other[:, at], m, (1, 0))
 
 
 def other_kernel(index, *refs):
@@ -172,7 +167,7 @@
     m = dot(other[:, d:], right_root[at], (1, 0)) + dot(other[:, :d], right_root[there], (1, 0))
     m = m.astype(BF16)
     up_buf[at] = (up_own[:d] + dot(left_root[:, there], m, (1, 0))).astype(BF16)
-    part = up_own[d:] + dot(root_other[pl.ds(pl.multiple_of((2 - h) * d, d), d)], m, (1, 0))
+    part = up_own[d:] + dot(root_other[:, there], m, (1, 0))
     up_buf[there] = part.astype(BF16)
     outs[0].start()
     gram = dot(grad[:, :d], other[:, d:], (1, 1)) + dot(grad[:, d:], other[:, :d], (1, 1))
@@ -257,14 +252,14 @@
     s_2 = swap(y_2, "core")
     pieces = (cot, cot_s, y_up, s_up, y_down, s_down, y_2, s_2)
 
-    send = after(half(down_weight, 1 - h, 0), cot)
-    weight_root = swap(jnp.concatenate([send, left_root[:, :d], left_root[:, d:]], 0), "xl")
+    weight_other = swap(after(half(down_weight, 1 - h, 0), cot), "xl")
+    root_other = swap(after(left_root, weight_other), "xl")
     weight = call(
         weight_kernel,
         [((d, 2 * d), BF16)],
         h[None],
         down_weight,
-        weight_root,
+        weight_other,
         specs=[ANY] * 2,
         scratch=[sem((2,))],
     )[0]
@@ -276,6 +271,18 @@
             offset = (target % 4 - y) % 4
             out += [jnp.where(offset % 2 == 0, offset // 2 * 3, (offset % 4 == 1) + 1), xh ^ (target // 4)]
         return jnp.stack(out)
+
+    small, full = ((tok, d), BF16), ((2 * tok, d), BF16)
+    up, down, *parts, part_0 = call(
+        part_kernel,
+        [small, small] + [((2, 2 * tok, d), F32)] * 3 + [((1, 2 * tok, d), F32)],
+        places(4, 3, -3, 2, -2, 1, -1, 0),
+        *pieces,
+        weight,
+        specs=[ANY] * 8 + [VMEM],
+        scratch=[pltpu.VMEM((8, 2 * tok, 2 * d), BF16), sem((8, 2))],
+        first=[up_3, down_3],
+    )
 
     grad = call(
         grad_kernel,
@@ -291,35 +298,9 @@
             sem((8,)),
             sem((8, 2)),
         ],
+        first=[up],
     )[0]
     other = swap(grad, "xl")
-
-    small, full = ((tok, d), BF16), ((2 * tok, d), BF16)
-    up, down = call(
-        far_kernel,
-        [small, small],
-        places(4),
-        *pieces,
-        weight,
-        specs=[ANY] * 8 + [VMEM],
-        scratch=[pltpu.VMEM((2 * tok, 2 * d), BF16), sem((2,))],
-        first=[up_3, down_3],
-    )
-    *parts, part_0 = call(
-        part_kernel,
-        [((2, 2 * tok, d), F32)] * 3 + [((1, 2 * tok, d), F32)],
-        places(3, -3, 2, -2, 1, -1, 0),
-        *pieces,
-        weight,
-        specs=[ANY] * 8 + [VMEM],
-        scratch=[pltpu.VMEM((7, 2 * tok, 2 * d), BF16), sem((7, 2))],
-    )
-    up, down = shift(up, "z", 1), shift(down, "z", -1)
-    for k, part in enumerate(parts):
-        up, down = call(add_kernel, [full, full], nothing, part, up, down)
-        up, down = shift(up, "z", 1), shift(down, "z", -1)
-    keep, send = call(last_kernel, [small, small], (h ^ core)[None], part_0, up, down)
-    input_grad = order(h, keep, swap(send, "xl"), 1)
 
     left_own, right_own, up_own = call(
         own_kernel,
@@ -328,8 +309,12 @@
         grad,
         right_root,
         left_root,
-        weight_root,
-    )
+        root_other,
+    )
+    up, down = shift(up, "z", 1), shift(down, "z", -1)
+    for k, part in enumerate(parts):
+        up, down = call(add_kernel, [full, full], nothing, part, up, down, first=[left_own] if k == 1 else [])
+        up, down = shift(up, "z", 1), shift(down, "z", -1)
     stats = ((d, 2 * d), F32)
     left_new, right_new, update = call(
         other_kernel,
@@ -339,7 +324,7 @@
         other,
         right_root,
         left_root,
-        weight_root,
+        root_other,
         left_own,
         right_own,
         up_own,
@@ -349,6 +334,9 @@
         outs=[ANY] * 3,
         scratch=[pltpu.VMEM((d, 2 * d), F32)] * 4 + [pltpu.VMEM((2 * d, d), BF16), sem((5,))],
     )
+    keep, send = call(last_kernel, [small, small], (h ^ core)[None], part_0, up, down, first=[update])
+    input_grad = order(h, keep, swap(send, "xl"), 1)
+
     return input_grad, update, left_new[None], right_new[None]
 
 

time: 123 us -> 115 us (0.935)
  Pallas kernels: 26.7 us -> 21.6 us
  starting transfers between devices: 44.1 us -> 39.2 us
  waiting for transfers between devices: 40.2 us -> 43.7 us
  local copies, waits for them, and re-layouts: 6.45 us -> 4.46 us
    ppermute x9 -> x10, waiting for transfers between devices: 4.18 us -> 14.1 us  [swap(): return lax.ppermute(value, axis, [(0, 1), (1, 0)])]
    ppermute x19, waiting for transfers between devices: 36 us -> 26.5 us  [shift(): lax.ppermute(value, axis, [(i, (i + distance) % n) for i in range(n)])]
    ppermute x19, starting transfers between devices: 33.6 us -> 28.4 us  [shift(): lax.ppermute(value, axis, [(i, (i + distance) % n) for i in range(n)])]
    pallas_call x10 -> x9, Pallas kernels: 26.7 us -> 21.6 us  [call(): pl.pallas_call(body, out_shape=[jax.ShapeDtypeStruct(s, t) for s, t in sh...]
    ppermute x1, waiting for transfers between devices: 0.01 us -> 3.01 us  [cross(): return lax.ppermute(value, ('xl', 'xh'), [(0, 3), (3, 0), (1, 2), (2, 1)])]
    ppermute x9 -> x10, starting transfers between devices: 8.92 us -> 10.4 us  [swap(): return lax.ppermute(value, axis, [(0, 1), (1, 0)])]
    slice x1 -> x0, local copies, waits for them, and re-layouts: 1.31 us -> none  [local(): left_root[:, :d]]
  transfers between devices with their start and end apart: 29 -> 30, of which waited for: 12 -> 14; matrix products, arithmetic and copies ran while one was open for 6% -> 3% of each run, Pallas kernels for 22% -> 19%
where the time goes in v4:
time: 115 us
  waiting for transfers between devices  43.7 us (38%)
  starting transfers between devices  39.2 us (34%)
  Pallas kernels  21.6 us (19%)
  local copies, waits for them, and re-layouts  4.46 us (4%)
  other arithmetic  3.58 us (3%)
  between operations  2.04 us (2%)
    ppermute x19, starting transfers between devices, shift(): lax.ppermute(value, axis, [(i, (i + distance) % n) for i in range(n)])  28.4 us
    ppermute x19, waiting for transfers between devices, shift(): lax.ppermute(value, axis, [(i, (i + distance) % n) for i in range(n)])  26.5 us
    pallas_call x9, Pallas kernels, call(): pl.pallas_call(body, out_shape=[jax.ShapeDtypeStruct(s, t) for s, t in sh...  21.6 us
    ppermute x10, waiting for transfers between devices, swap(): return lax.ppermute(value, axis, [(0, 1), (1, 0)])  14.1 us
    ppermute x10, starting transfers between devices, swap(): return lax.ppermute(value, axis, [(0, 1), (1, 0)])  10.4 us
    ppermute x1, waiting for transfers between devices, cross(): return lax.ppermute(value, ('xl', 'xh'), [(0, 3), (3, 0), (1, 2), (2, 1)])  3.01 us
  transfers between devices with their start and end apart: 30, of which 14 were waited for; matrix products, arithmetic and copies ran while one was open for 3% of the time, Pallas kernels for 19%

profile of v4, /device:TPU:2, one launch (start us, length us, event | category | flops | bytes accessed | tf_op | source)
XLA Modules:
  0.0 114.6 jit_solution(14524367479429347292)
XLA Ops:
  2.6 2.4 %collective-permute-start = (bf16[256,512]{1,0:T(8,128)(2,1)S(1)}, bf16[256,512]{1,0:T(8,128)(2,1)S(1)}, u32[]{:S(2)}, u32[]{:S(2)}) collective-permute-start(bf16[256,512]{1,0:T(8,128)(2,1)S(1)} %pad_maximum_fusion.2), channel_id=1, source_target_pairs={{0,16},{16,0},{1,17},{17,1},{2,18},{18,2},{3,19},{19,3},{4,20},{20... | collective-permute-start | bytes 786440 | tf_op jit(solution)/shard_map/ppermute | solution.py:21
  7.1 3.0 %collective-permute-done.2 = bf16[128,512]{1,0:T(8,128)(2,1)S(1)} collective-permute-done((bf16[128,512]{1,0:T(8,128)(2,1)}, bf16[128,512]{1,0:T(8,128)(2,1)S(1)}, u32[]{:S(2)}, u32[]{:S(2)}) %collective-permute-start.2) | collective-permute-done | bytes 131104 | tf_op jit(solution)/shard_map/ppermute | solution.py:30
  10.1 4.3 %collective-permute-done.1 = bf16[128,512]{1,0:T(8,128)(2,1)S(1)} collective-permute-done((bf16[128,512]{1,0:T(8,128)(2,1)}, bf16[128,512]{1,0:T(8,128)(2,1)S(1)}, u32[]{:S(2)}, u32[]{:S(2)}) %collective-permute-start.1) | collective-permute-done | bytes 131104 | tf_op jit(solution)/shard_map/ppermute | solution.py:21
  15.6 3.1 %collective-permute-start.6 = (bf16[2,128,1024]{2,1,0:T(8,128)(2,1)S(1)}, bf16[2,128,1024]{2,1,0:T(8,128)(2,1)}, u32[]{:S(2)}, u32[]{:S(2)}) collective-permute-start(bf16[2,128,1024]{2,1,0:T(8,128)(2,1)S(1)} %pad_maximum_fusion.refs_1_.refs_9_), channel_id=1, source_target_pairs={{0,6},{2,0},{4,2},{6,4},{1,7},{3,1},{5,3},{7,5},{8,14},{10,8},{12,... | collective-permute-start | bytes 1572872 | tf_op jit(solution)/shard_map/ppermute | solution.py:26
  18.7 2.0 %collective-permute-start.12 = (bf16[256,512]{1,0:T(8,128)(2,1)S(1)}, bf16[256,512]{1,0:T(8,128)(2,1)S(1)}, u32[]{:S(2)}, u32[]{:S(2)}) collective-permute-start(bf16[256,512]{1,0:T(8,128)(2,1)S(1)} %pad_maximum_fusion.3.refs_1_), channel_id=1, source_target_pairs={{0,32},{32,64},{64,96},{96,128},{128,160},{160,192},{192,224},{224... | collective-permute-start | bytes 786440 | tf_op jit(solution)/shard_map/ppermute | solution.py:26
  20.9 4.0 %collective-permute-start.15 = (bf16[256,512]{1,0:T(8,128)(2,1)S(1)}, bf16[256,512]{1,0:T(8,128)(2,1)S(1)}, u32[]{:S(2)}, u32[]{:S(2)}) collective-permute-start(bf16[256,512]{1,0:T(8,128)(2,1)S(1)} %pad_maximum_fusion.3.refs_1_), channel_id=1, source_target_pairs={{0,224},{32,0},{64,32},{96,64},{128,96},{160,128},{192,160},{224,1... | collective-permute-start | bytes 786440 | tf_op jit(solution)/shard_map/ppermute | solution.py:26
  24.9 4.9 %collective-permute-done.12.refs_2_ = bf16[256,512]{1,0:T(8,128)(2,1)S(1)} collective-permute-done((bf16[256,512]{1,0:T(8,128)(2,1)S(1)}, bf16[256,512]{1,0:T(8,128)(2,1)S(1)}, u32[]{:S(2)}, u32[]{:S(2)}) %collective-permute-start.12) | collective-permute-done | bytes 262176 | tf_op jit(solution)/shard_map/ppermute | solution.py:26
  32.6 3.2 %collective-permute-start.9 = (bf16[128,1024]{1,0:T(8,128)(2,1)S(1)}, bf16[128,1024]{1,0:T(8,128)(2,1)S(1)}, u32[]{:S(2)}, u32[]{:S(2)}) collective-permute-start(bf16[128,1024]{1,0:T(8,128)(2,1)S(1)} %slice_bitcast_fusion), channel_id=1, source_target_pairs={{0,6},{2,0},{4,2},{6,4},{1,7},{3,1},{5,3},{7,5},{8,14},{10,8},{12,... | collective-permute-start | bytes 786440 | tf_op jit(solution)/shard_map/ppermute | solution.py:26
  36.9 5.0 %collective-permute-done.11.refs_2_ = bf16[512,512]{1,0:T(8,128)(2,1)S(1)} collective-permute-done((bf16[512,512]{1,0:T(8,128)(2,1)S(1)}, bf16[512,512]{1,0:T(8,128)(2,1)S(1)}, u32[]{:S(2)}, u32[]{:S(2)}) %collective-permute-start.11) | collective-permute-done | bytes 524320 | tf_op jit(solution)/shard_map/ppermute | solution.py:21
  43.9 1.8 %collective-permute-start.23 = (bf16[512,1024]{1,0:T(8,128)(2,1)S(1)}, bf16[512,1024]{1,0:T(8,128)(2,1)S(1)}, u32[]{:S(2)}, u32[]{:S(2)}) collective-permute-start(bf16[512,1024]{1,0:T(8,128)(2,1)S(1)} %bitcast.36), channel_id=1, source_target_pairs={{0,16},{16,0},{1,17},{17,1},{2,18},{18,2},{3,19},{19,3},{4,20},{20... | collective-permute-start | bytes 3145736 | tf_op jit(solution)/shard_map/ppermute | solution.py:21
  48.2 2.7 %collective-permute-done.14.refs_10_.refs_4_ = bf16[256,512]{1,0:T(8,128)(2,1)S(1)} collective-permute-done((bf16[256,512]{1,0:T(8,128)(2,1)S(1)}, bf16[256,512]{1,0:T(8,128)(2,1)S(1)}, u32[]{:S(2)}, u32[]{:S(2)}) %collective-permute-start.14) | collective-permute-done | bytes 262176 | tf_op jit(solution)/shard_map/ppermute | solution.py:26
  51.0 6.3 %collective-permute-done.17.refs_11_.refs_7_ = bf16[256,512]{1,0:T(8,128)(2,1)S(1)} collective-permute-done((bf16[256,512]{1,0:T(8,128)(2,1)S(1)}, bf16[256,512]{1,0:T(8,128)(2,1)S(1)}, u32[]{:S(2)}, u32[]{:S(2)}) %collective-permute-start.17) | collective-permute-done | bytes 262176 | tf_op jit(solution)/shard_map/ppermute | solution.py:26
  59.9 5.5 %shard_map.103 = (bf16[128,512]{1,0:T(8,128)(2,1)S(1)}, bf16[128,512]{1,0:T(8,128)(2,1)S(1)}, f32[2,256,512]{2,1,0:T(8,128)S(1)}, f32[2,256,512]{2,1,0:T(8,128)S...) custom-call(s32[16]{0:T(128)S(1)} %stack.104.refs_0_, bf16[2,128,1024]{2,1,0:T(8,128)(2,1)} %copy-done.5, ...), custom_call_target="tpu_custom_call" | custom-call | tf_op jit(solution)/shard_map/pallas_call | solution.py:60
  67.2 5.7 %shard_map.105.refs_1_ = bf16[512,1024]{1,0:T(8,128)(2,1)S(1)} custom-call(s32[16]{0:T(128)S(1)} %stack.111.refs_0_, bf16[256,512]{1,0:T(8,128)(2,1)} %copy-done.8, bf16[256,512]{1,0:T(8,128)(2,1)} %copy-done.11, bf16[256,512]{1,0:T(8,128)(2,1)} %copy-done.13, bf16[256,512]{1,0:T(8,128)(2,1)} %copy-done.3, bf16[256,512]{1,0:T(8,128)(2,1)} %copy-done.12, ...), custom_call_target="tpu_custom_call" | custom-call | tf_op jit(solution)/shard_map/pallas_call | solution.py:60
  72.9 1.8 %collective-permute-start.28 = (bf16[512,1024]{1,0:T(8,128)(2,1)S(1)}, bf16[512,1024]{1,0:T(8,128)(2,1)S(1)}, u32[]{:S(2)}, u32[]{:S(2)}) collective-permute-start(bf16[512,1024]{1,0:T(8,128)(2,1)S(1)} %shard_map.105.refs_1_), channel_id=1, source_target_pairs={{0,16},{16,0},{1,17},{17,1},{2,18},{18,2},{3,19},{19,3},{4,20},{20... | collective-permute-start | bytes 3145736 | tf_op jit(solution)/shard_map/ppermute | solution.py:21
  74.7 3.2 %collective-permute-start.19 = (bf16[128,512]{1,0:T(8,128)(2,1)S(1)}, bf16[128,512]{1,0:T(8,128)(2,1)S(1)}, u32[]{:S(2)}, u32[]{:S(2)}) collective-permute-start(bf16[128,512]{1,0:T(8,128)(2,1)S(1)} %get-tuple-element.32), channel_id=1, source_target_pairs={{0,224},{32,0},{64,32},{96,64},{128,96},{160,128},{192,160},{224,1... | collective-permute-start | bytes 393224 | tf_op jit(solution)/shard_map/ppermute | solution.py:26
  78.0 2.9 %collective-permute-done.18.refs_2_ = bf16[128,512]{1,0:T(8,128)(2,1)S(1)} collective-permute-done((bf16[128,512]{1,0:T(8,128)(2,1)S(1)}, bf16[128,512]{1,0:T(8,128)(2,1)S(1)}, u32[]{:S(2)}, u32[]{:S(2)}) %collective-permute-start.18) | collective-permute-done | bytes 131104 | tf_op jit(solution)/shard_map/ppermute | solution.py:26
  82.6 2.1 %collective-permute-start.21 = (bf16[256,512]{1,0:T(8,128)(2,1)S(1)}, bf16[256,512]{1,0:T(8,128)(2,1)S(1)}, u32[]{:S(2)}, u32[]{:S(2)}) collective-permute-start(bf16[256,512]{1,0:T(8,128)(2,1)S(1)} %get-tuple-element.34), channel_id=1, source_target_pairs={{0,224},{32,0},{64,32},{96,64},{128,96},{160,128},{192,160},{224,1... | collective-permute-start | bytes 786440 | tf_op jit(solution)/shard_map/ppermute | solution.py:26
  84.6 2.5 %shard_map.106 = (f32[512,512]{1,0:T(8,128)S(1)}, f32[512,1024]{1,0:T(8,128)S(1)}, f32[1024,512]{1,0:T(8,128)S(1)}) custom-call(s32[1]{0:T(128)} %bitcast.23.refs_0_, bf16[512,1024]{1,0:T(8,128)(2,1)S(1)} %shard_map.105.refs_1_, bf16[1024,512]{1,0:T(8,128)(2,1)S(1)} %bitcast.34, bf16[512,1024]{1,0:T(8,128)(2,1)S(1)} %bitcast.37, ...), custom_call_target="tpu_custom_call" | custom-call | tf_op jit(solution)/shard_map/pallas_call | solution.py:60
  90.5 2.0 %collective-permute-start.25 = (bf16[256,512]{1,0:T(8,128)(2,1)S(1)}, bf16[256,512]{1,0:T(8,128)(2,1)S(1)}, u32[]{:S(2)}, u32[]{:S(2)}) collective-permute-start(bf16[256,512]{1,0:T(8,128)(2,1)S(1)} %get-tuple-element.38), channel_id=1, source_target_pairs={{0,224},{32,0},{64,32},{96,64},{128,96},{160,128},{192,160},{224,1... | collective-permute-start | bytes 786440 | tf_op jit(solution)/shard_map/ppermute | solution.py:26
  92.5 4.6 %collective-permute-done.24.refs_2_ = bf16[256,512]{1,0:T(8,128)(2,1)S(1)} collective-permute-done((bf16[256,512]{1,0:T(8,128)(2,1)S(1)}, bf16[256,512]{1,0:T(8,128)(2,1)S(1)}, u32[]{:S(2)}, u32[]{:S(2)}) %collective-permute-start.24) | collective-permute-done | bytes 262176 | tf_op jit(solution)/shard_map/ppermute | solution.py:26
  97.6 2.5 %collective-permute-start.26 = (bf16[256,512]{1,0:T(8,128)(2,1)S(1)}, bf16[256,512]{1,0:T(8,128)(2,1)S(1)}, u32[]{:S(2)}, u32[]{:S(2)}) collective-permute-start(bf16[256,512]{1,0:T(8,128)(2,1)S(1)} %get-tuple-element.39), channel_id=1, source_target_pairs={{0,32},{32,64},{64,96},{96,128},{128,160},{160,192},{192,224},{224... | collective-permute-start | bytes 786440 | tf_op jit(solution)/shard_map/ppermute | solution.py:26
  101.1 6.4 %shard_map.109 = (f32[512,1024]{1,0:T(8,128)}, f32[512,1024]{1,0:T(8,128)}, bf16[1024,512]{1,0:T(8,128)(2,1)}) custom-call(s32[1]{0:T(128)} %bitcast.23.refs_0_, bf16[512,1024]{1,0:T(8,128)(2,1)S(1)} %shard_map.105.refs_1_, bf16[512,1024]{1,0:T(8,128)(2,1)S(1)} %collective-permute-done.28.refs_2_, bf16[1024,512]{1,0:T(8,128)(2,1)S(1)} %bitcast.35, ...), custom_call_target="tpu_custom_call" | custom-call | tf_op jit(solution)/shard_map/pallas_call | solution.py:60
  109.1 4.8 %collective-permute-done.29 = bf16[128,512]{1,0:T(8,128)(2,1)S(1)} collective-permute-done((bf16[128,512]{1,0:T(8,128)(2,1)S(1)}, bf16[128,512]{1,0:T(8,128)(2,1)S(1)}, u32[]{:S(2)}, u32[]{:S(2)}) %collective-permute-start.29) | collective-permute-done | bytes 131104 | tf_op jit(solution)/shard_map/ppermute | solution.py:21
  (90 shorter events, 25.8 us)
Async XLA Ops:
  2.6 11.9 %collective-permute-start = (bf16[256,512]{1,0:T(8,128)(2,1)S(1)}, bf16[256,512]{1,0:T(8,128)(2,1)S(1)}, u32[]{:S(2)}, u32[]{:S(2)}) collective-permute-start(bf16[256,512]{1,0:T(8,128)(2,1)S(1)} %pad_maximum_fusion.2), channel_id=1, source_target_pairs={{0,16},{16,0},{1,17},{17,1},{2,18},{18,2},{3,19},{19,3},{4,20},{20... | collective-permute-start | bytes 786440 | tf_op jit(solution)/shard_map/ppermute | solution.py:21
  5.4 9.1 %collective-permute-start.1 = (bf16[128,512]{1,0:T(8,128)(2,1)}, bf16[128,512]{1,0:T(8,128)(2,1)S(1)}, u32[]{:S(2)}, u32[]{:S(2)}) collective-permute-start(bf16[128,512]{1,0:T(8,128)(2,1)} %param.7), channel_id=1, source_target_pairs={{0,8},{8,0},{1,9},{9,1},{2,10},{10,2},{3,11},{11,3},{4,12},{12,4},... | collective-permute-start | bytes 393224 | tf_op jit(solution)/shard_map/ppermute | solution.py:21
  15.6 16.0 %collective-permute-start.6 = (bf16[2,128,1024]{2,1,0:T(8,128)(2,1)S(1)}, bf16[2,128,1024]{2,1,0:T(8,128)(2,1)}, u32[]{:S(2)}, u32[]{:S(2)}) collective-permute-start(bf16[2,128,1024]{2,1,0:T(8,128)(2,1)S(1)} %pad_maximum_fusion.refs_1_.refs_9_), channel_id=1, source_target_pairs={{0,6},{2,0},{4,2},{6,4},{1,7},{3,1},{5,3},{7,5},{8,14},{10,8},{12,... | collective-permute-start | bytes 1572872 | tf_op jit(solution)/shard_map/ppermute | solution.py:26
  18.7 13.9 %collective-permute-start.4 = (bf16[2,128,1024]{2,1,0:T(8,128)(2,1)S(1)}, bf16[2,128,1024]{2,1,0:T(8,128)(2,1)}, u32[]{:S(2)}, u32[]{:S(2)}) collective-permute-start(bf16[2,128,1024]{2,1,0:T(8,128)(2,1)S(1)} %pad_maximum_fusion.refs_1_.refs_9_), channel_id=1, source_target_pairs={{0,2},{2,4},{4,6},{6,0},{1,3},{3,5},{5,7},{7,1},{8,10},{10,12},{12... | collective-permute-start | bytes 1572872 | tf_op jit(solution)/shard_map/ppermute | solution.py:26
  18.7 11.1 %collective-permute-start.12 = (bf16[256,512]{1,0:T(8,128)(2,1)S(1)}, bf16[256,512]{1,0:T(8,128)(2,1)S(1)}, u32[]{:S(2)}, u32[]{:S(2)}) collective-permute-start(bf16[256,512]{1,0:T(8,128)(2,1)S(1)} %pad_maximum_fusion.3.refs_1_), channel_id=1, source_target_pairs={{0,32},{32,64},{64,96},{96,128},{128,160},{160,192},{192,224},{224... | collective-permute-start | bytes 786440 | tf_op jit(solution)/shard_map/ppermute | solution.py:26
  20.8 25.8 %collective-permute-start.3 = (bf16[2,128,1024]{2,1,0:T(8,128)(2,1)S(1)}, bf16[2,128,1024]{2,1,0:T(8,128)(2,1)S(1)}, u32[]{:S(2)}, u32[]{:S(2)}) collective-permute-start(bf16[2,128,1024]{2,1,0:T(8,128)(2,1)S(1)} %pad_maximum_fusion.refs_1_.refs_9_), channel_id=1, source_target_pairs={{0,1},{1,0},{2,3},{3,2},{4,5},{5,4},{6,7},{7,6},{8,9},{9,8},{10,11... | collective-permute-start | bytes 1572872 | tf_op jit(solution)/shard_map/ppermute | solution.py:21
  20.9 15.9 %collective-permute-start.15 = (bf16[256,512]{1,0:T(8,128)(2,1)S(1)}, bf16[256,512]{1,0:T(8,128)(2,1)S(1)}, u32[]{:S(2)}, u32[]{:S(2)}) collective-permute-start(bf16[256,512]{1,0:T(8,128)(2,1)S(1)} %pad_maximum_fusion.3.refs_1_), channel_id=1, source_target_pairs={{0,224},{32,0},{64,32},{96,64},{128,96},{160,128},{192,160},{224,1... | collective-permute-start | bytes 786440 | tf_op jit(solution)/shard_map/ppermute | solution.py:26
  29.8 12.0 %collective-permute-start.11 = (bf16[512,512]{1,0:T(8,128)(2,1)S(1)}, bf16[512,512]{1,0:T(8,128)(2,1)S(1)}, u32[]{:S(2)}, u32[]{:S(2)}) collective-permute-start(bf16[512,512]{1,0:T(8,128)(2,1)S(1)} %constant_dynamic-slice_fusion), channel_id=1, source_target_pairs={{0,16},{16,0},{1,17},{17,1},{2,18},{18,2},{3,19},{19,3},{4,20},{20... | collective-permute-start | bytes 1572872 | tf_op jit(solution)/shard_map/ppermute | solution.py:21
  31.6 11.7 %collective-permute-start.13 = (bf16[256,512]{1,0:T(8,128)(2,1)S(1)}, bf16[256,512]{1,0:T(8,128)(2,1)S(1)}, u32[]{:S(2)}, u32[]{:S(2)}) collective-permute-start(bf16[256,512]{1,0:T(8,128)(2,1)S(1)} %collective-permute-done.12.refs_2_), channel_id=1, source_target_pairs={{0,32},{32,64},{64,96},{96,128},{128,160},{160,192},{192,224},{224... | collective-permute-start | bytes 786440 | tf_op jit(solution)/shard_map/ppermute | solution.py:26
  32.6 11.3 %collective-permute-start.9 = (bf16[128,1024]{1,0:T(8,128)(2,1)S(1)}, bf16[128,1024]{1,0:T(8,128)(2,1)S(1)}, u32[]{:S(2)}, u32[]{:S(2)}) collective-permute-start(bf16[128,1024]{1,0:T(8,128)(2,1)S(1)} %slice_bitcast_fusion), channel_id=1, source_target_pairs={{0,6},{2,0},{4,2},{6,4},{1,7},{3,1},{5,3},{7,5},{8,14},{10,8},{12,... | collective-permute-start | bytes 786440 | tf_op jit(solution)/shard_map/ppermute | solution.py:26
  36.8 9.0 %collective-permute-start.8 = (bf16[128,1024]{1,0:T(8,128)(2,1)S(1)}, bf16[128,1024]{1,0:T(8,128)(2,1)S(1)}, u32[]{:S(2)}, u32[]{:S(2)}) collective-permute-start(bf16[128,1024]{1,0:T(8,128)(2,1)S(1)} %slice_bitcast_fusion.1), channel_id=1, source_target_pairs={{0,2},{2,4},{4,6},{6,0},{1,3},{3,5},{5,7},{7,1},{8,10},{10,12},{12... | collective-permute-start | bytes 786440 | tf_op jit(solution)/shard_map/ppermute | solution.py:26
  43.3 7.6 %collective-permute-start.14 = (bf16[256,512]{1,0:T(8,128)(2,1)S(1)}, bf16[256,512]{1,0:T(8,128)(2,1)S(1)}, u32[]{:S(2)}, u32[]{:S(2)}) collective-permute-start(bf16[256,512]{1,0:T(8,128)(2,1)S(1)} %collective-permute-done.13.refs_3_), channel_id=1, source_target_pairs={{0,32},{32,64},{64,96},{96,128},{128,160},{160,192},{192,224},{224... | collective-permute-start | bytes 786440 | tf_op jit(solution)/shard_map/ppermute | solution.py:26
  43.9 40.7 %collective-permute-start.23 = (bf16[512,1024]{1,0:T(8,128)(2,1)S(1)}, bf16[512,1024]{1,0:T(8,128)(2,1)S(1)}, u32[]{:S(2)}, u32[]{:S(2)}) collective-permute-start(bf16[512,1024]{1,0:T(8,128)(2,1)S(1)} %bitcast.36), channel_id=1, source_target_pairs={{0,16},{16,0},{1,17},{17,1},{2,18},{18,2},{3,19},{19,3},{4,20},{20... | collective-permute-start | bytes 3145736 | tf_op jit(solution)/shard_map/ppermute | solution.py:21
  45.7 14.2 %collective-permute-start.5 = (bf16[2,128,1024]{2,1,0:T(8,128)(2,1)}, bf16[2,128,1024]{2,1,0:T(8,128)(2,1)}, u32[]{:S(2)}, u32[]{:S(2)}) collective-permute-start(bf16[2,128,1024]{2,1,0:T(8,128)(2,1)} %collective-permute-done.4.refs_3_.refs_11_), channel_id=1, source_target_pairs={{0,1},{1,0},{2,3},{3,2},{4,5},{5,4},{6,7},{7,6},{8,9},{9,8},{10,11... | collective-permute-start | bytes 1572872 | tf_op jit(solution)/shard_map/ppermute | solution.py:21
  46.6 13.3 %collective-permute-start.7 = (bf16[2,128,1024]{2,1,0:T(8,128)(2,1)}, bf16[2,128,1024]{2,1,0:T(8,128)(2,1)}, u32[]{:S(2)}, u32[]{:S(2)}) collective-permute-start(bf16[2,128,1024]{2,1,0:T(8,128)(2,1)} %collective-permute-done.6.refs_5_.refs_13_), channel_id=1, source_target_pairs={{0,1},{1,0},{2,3},{3,2},{4,5},{5,4},{6,7},{7,6},{8,9},{9,8},{10,11... | collective-permute-start | bytes 1572872 | tf_op jit(solution)/shard_map/ppermute | solution.py:21
  48.2 11.7 %collective-permute-start.10 = (bf16[2,128,1024]{2,1,0:T(8,128)(2,1)}, bf16[2,128,1024]{2,1,0:T(8,128)(2,1)}, u32[]{:S(2)}, u32[]{:S(2)}) collective-permute-start(bf16[2,128,1024]{2,1,0:T(8,128)(2,1)} %pad_maximum_fusion.1.refs_7_.refs_15_), channel_id=1, source_target_pairs={{0,1},{1,0},{2,3},{3,2},{4,5},{5,4},{6,7},{7,6},{8,9},{9,8},{10,11... | collective-permute-start | bytes 1572872 | tf_op jit(solution)/shard_map/ppermute | solution.py:21
  57.3 9.9 %collective-permute-start.22 = (bf16[256,512]{1,0:T(8,128)(2,1)S(1)}, bf16[256,512]{1,0:T(8,128)(2,1)}, u32[]{:S(2)}, u32[]{:S(2)}) collective-permute-start(bf16[256,512]{1,0:T(8,128)(2,1)S(1)} %collective-permute-done.14.refs_10_.refs_4_), channel_id=1, source_target_pairs={{0,32},{32,64},{64,96},{96,128},{128,160},{160,192},{192,224},{224... | collective-permute-start | bytes 786440 | tf_op jit(solution)/shard_map/ppermute | solution.py:26
  72.9 28.2 %collective-permute-start.28 = (bf16[512,1024]{1,0:T(8,128)(2,1)S(1)}, bf16[512,1024]{1,0:T(8,128)(2,1)S(1)}, u32[]{:S(2)}, u32[]{:S(2)}) collective-permute-start(bf16[512,1024]{1,0:T(8,128)(2,1)S(1)} %shard_map.105.refs_1_), channel_id=1, source_target_pairs={{0,16},{16,0},{1,17},{17,1},{2,18},{18,2},{3,19},{19,3},{4,20},{20... | collective-permute-start | bytes 3145736 | tf_op jit(solution)/shard_map/ppermute | solution.py:21
  81.0 7.7 %collective-permute-start.20 = (bf16[256,512]{1,0:T(8,128)(2,1)S(1)}, bf16[256,512]{1,0:T(8,128)(2,1)S(1)}, u32[]{:S(2)}, u32[]{:S(2)}) collective-permute-start(bf16[256,512]{1,0:T(8,128)(2,1)S(1)} %get-tuple-element.33), channel_id=1, source_target_pairs={{0,32},{32,64},{64,96},{96,128},{128,160},{160,192},{192,224},{224... | collective-permute-start | bytes 786440 | tf_op jit(solution)/shard_map/ppermute | solution.py:26
  82.6 6.4 %collective-permute-start.21 = (bf16[256,512]{1,0:T(8,128)(2,1)S(1)}, bf16[256,512]{1,0:T(8,128)(2,1)S(1)}, u32[]{:S(2)}, u32[]{:S(2)}) collective-permute-start(bf16[256,512]{1,0:T(8,128)(2,1)S(1)} %get-tuple-element.34), channel_id=1, source_target_pairs={{0,224},{32,0},{64,32},{96,64},{128,96},{160,128},{192,160},{224,1... | collective-permute-start | bytes 786440 | tf_op jit(solution)/shard_map/ppermute | solution.py:26
  89.0 8.1 %collective-permute-start.24 = (bf16[256,512]{1,0:T(8,128)(2,1)S(1)}, bf16[256,512]{1,0:T(8,128)(2,1)S(1)}, u32[]{:S(2)}, u32[]{:S(2)}) collective-permute-start(bf16[256,512]{1,0:T(8,128)(2,1)S(1)} %get-tuple-element.37), channel_id=1, source_target_pairs={{0,32},{32,64},{64,96},{96,128},{128,160},{160,192},{192,224},{224... | collective-permute-start | bytes 786440 | tf_op jit(solution)/shard_map/ppermute | solution.py:26
  90.5 7.0 %collective-permute-start.25 = (bf16[256,512]{1,0:T(8,128)(2,1)S(1)}, bf16[256,512]{1,0:T(8,128)(2,1)S(1)}, u32[]{:S(2)}, u32[]{:S(2)}) collective-permute-start(bf16[256,512]{1,0:T(8,128)(2,1)S(1)} %get-tuple-element.38), channel_id=1, source_target_pairs={{0,224},{32,0},{64,32},{96,64},{128,96},{160,128},{192,160},{224,1... | collective-permute-start | bytes 786440 | tf_op jit(solution)/shard_map/ppermute | solution.py:26
  97.6 9.9 %collective-permute-start.26 = (bf16[256,512]{1,0:T(8,128)(2,1)S(1)}, bf16[256,512]{1,0:T(8,128)(2,1)S(1)}, u32[]{:S(2)}, u32[]{:S(2)}) collective-permute-start(bf16[256,512]{1,0:T(8,128)(2,1)S(1)} %get-tuple-element.39), channel_id=1, source_target_pairs={{0,32},{32,64},{64,96},{96,128},{128,160},{160,192},{192,224},{224... | collective-permute-start | bytes 786440 | tf_op jit(solution)/shard_map/ppermute | solution.py:26
  100.1 7.3 %collective-permute-start.27 = (bf16[256,512]{1,0:T(8,128)(2,1)S(1)}, bf16[256,512]{1,0:T(8,128)(2,1)S(1)}, u32[]{:S(2)}, u32[]{:S(2)}) collective-permute-start(bf16[256,512]{1,0:T(8,128)(2,1)S(1)} %get-tuple-element.40), channel_id=1, source_target_pairs={{0,224},{32,0},{64,32},{96,64},{128,96},{160,128},{192,160},{224,1... | collective-permute-start | bytes 786440 | tf_op jit(solution)/shard_map/ppermute | solution.py:26
  (21 other events, 305.4 us)

commit v5 on v4

--- a/solution.py
+++ b/solution.py
@@ -68,31 +68,27 @@
     )(*args, *first)
 
 
-def fetch(y_at, x_at, pieces, tokens, sems):
+def block(k):
+    return pl.ds(pl.multiple_of(k * 256, 256), 256)
+
+
+def fetch(pieces, tokens, sems):
     tok = pieces[0].shape[1]
-    for k in range(4):
-
-        @pl.when(y_at == k)
-        def _(k=k):
-            for side in range(2):
-                target = tokens.at[pl.ds(side * tok, tok)]
-                pltpu.make_async_copy(pieces[2 * k + side].at[x_at], target, sems.at[side]).start()
-
-
-def fetched(pieces, tokens, sems):
-    tok = pieces[0].shape[1]
-    for side in range(2):
-        target = tokens.at[pl.ds(side * tok, tok)]
-        pltpu.make_async_copy(pieces[side].at[0], target, sems.at[side]).wait()
+    copies = []
+    for k, piece in enumerate(pieces):
+        for i in range(2):
+            at = pl.ds((k // 2 * 2 + i) * 2 * tok + k % 2 * tok, tok)
+            copies.append(pltpu.make_async_copy(piece.at[i], tokens.at[at], sems.at[2 * k + i]))
+            copies[-1].start()
+    return copies
 
 
 def part_kernel(index, *refs):
     pieces, weight, up, down, outs, (tokens, sems) = refs[:8], refs[8], refs[9], refs[10], refs[11:15], refs[15:]
+    for c in fetch(pieces, tokens, sems):
+        c.wait()
     for k in range(8):
-        fetch(index[2 * k], index[2 * k + 1], pieces, tokens.at[k], sems.at[k])
-    for k in range(8):
-        fetched(pieces, tokens.at[k], sems.at[k])
-        part = dot(tokens[k], weight[...], (1, 1))
+        part = dot(tokens[block(2 * index[2 * k] + index[2 * k + 1])], weight[...], (1, 1))
         if k == 0:
             rows = up.shape[0]
             up[...] = part[:rows].astype(BF16)
@@ -105,19 +101,26 @@
     acts, pieces, (out, rows, tokens, total, row_sems, sems) = refs[:8], refs[8:16], refs[16:]
     copies = []
     for k in range(8):
-        copies.append(pltpu.make_async_copy(acts[k], rows.at[k], row_sems.at[k]))
-        copies[k].start()
-        fetch(index[2 * k], index[2 * k + 1], pieces, tokens.at[k], sems.at[k])
-    for k in range(8):
-        copies[k].wait()
-        fetched(pieces, tokens.at[k], sems.at[k])
-        product = dot(rows[k], tokens[k], (0, 0))
-        if k == 0:
-            total[...] = product
-        elif k < 7:
-            total[...] += product
-        else:
-            out[...] = (total[...] + product).astype(BF16)
+        at = block(2 * index[2 * k] + index[2 * k + 1])
+        copies.append(pltpu.make_async_copy(acts[k], rows.at[at], row_sems.at[k]))
+        copies[-1].start()
+    copies += fetch(pieces, tokens, sems)
+    for c in copies:
+        c.wait()
+    out[...] = dot(rows[...], tokens[...], (0, 0)).astype(BF16)
+
+
+def send_kernel(index, act, own, out, sems):
+    tok, d = own.shape
+    at = pl.ds(pl.multiple_of(index[0] * d, d), d)
+    copies = [
+        pltpu.make_async_copy(act.at[:, at], out.at[pl.ds(0, tok)], sems.at[0]),
+        pltpu.make_async_copy(own, out.at[pl.ds(tok, tok)], sems.at[1]),
+    ]
+    for c in copies:
+        c.start()
+    for c in copies:
+        c.wait()
 
 
 def weight_kernel(index, own, other, out, sems):
@@ -232,7 +235,16 @@
     nothing = jnp.zeros((1,), jnp.int32)
     sem = pltpu.SemaphoreType.DMA
 
-    both = swap(jnp.concatenate([half(activations, 1 - h, 1), cotangent], 0), "xl")
+    both = call(
+        send_kernel,
+        [((2 * tok, d), BF16)],
+        (1 - h)[None],
+        activations,
+        cotangent,
+        specs=[ANY] * 2,
+        scratch=[sem((2,))],
+    )[0]
+    both = swap(both, "xl")
     cot_cross = cross(cotangent)
     cot_far = swap(cotangent, "xh")
     act = order(h ^ core, half(activations, h, 1), both[:tok], 0)
@@ -280,7 +292,7 @@
         *pieces,
         weight,
         specs=[ANY] * 8 + [VMEM],
-        scratch=[pltpu.VMEM((8, 2 * tok, 2 * d), BF16), sem((8, 2))],
+        scratch=[pltpu.VMEM((16 * tok, 2 * d), BF16), sem((16,))],
         first=[up_3, down_3],
     )
 
@@ -292,11 +304,11 @@
         *pieces,
         specs=[ANY] * 16,
         scratch=[
-            pltpu.VMEM((8, 2 * tok, d), BF16),
-            pltpu.VMEM((8, 2 * tok, 2 * d), BF16),
+            pltpu.VMEM((16 * tok, d), BF16),
+            pltpu.VMEM((16 * tok, 2 * d), BF16),
             pltpu.VMEM((d, 2 * d), F32),
             sem((8,)),
-            sem((8, 2)),
+            sem((16,)),
         ],
         first=[up],
     )[0]
@@ -334,7 +346,7 @@
         outs=[ANY] * 3,
         scratch=[pltpu.VMEM((d, 2 * d), F32)] * 4 + [pltpu.VMEM((2 * d, d), BF16), sem((5,))],
     )
-    keep, send = call(last_kernel, [small, small], (h ^ core)[None], part_0, up, down, first=[update])
+    keep, send = call(last_kernel, [small, small], (h ^ core)[None], part_0, up, down, first=[hbm(update)])
     input_grad = order(h, keep, swap(send, "xl"), 1)
 
     return input_grad, update, left_new[None], right_new[None]

time: 115 us -> 114 us (level)
  local copies, waits for them, and re-layouts: 4.46 us -> 1.36 us
  waiting for transfers between devices: 43.7 us -> 45.8 us
    squeeze x2, local copies, waits for them, and re-layouts: 1.94 us -> 0.04 us  [local(): y_2 = jnp.stack([shift(y_up[0], 'y', 1), shift(y_down[1], 'y', -1)])]
    ppermute x10, waiting for transfers between devices: 14.1 us -> 16 us  [swap(): return lax.ppermute(value, axis, [(0, 1), (1, 0)])]
    unnamed x30 -> x26, local copies, waits for them, and re-layouts: 1.29 us -> 0.06 us
    pallas_call x9 -> x10, Pallas kernels: 21.6 us -> 22.4 us  [call(): pl.pallas_call(body, out_shape=[jax.ShapeDtypeStruct(s, t) for s, t in sh...]
  transfers between devices with their start and end apart: 30 -> 30, of which waited for: 14 -> 14; matrix products, arithmetic and copies ran while one was open for 3% -> 2% of each run, Pallas kernels for 19% -> 19%
where the time goes in v5:
time: 114 us
  waiting for transfers between devices  45.8 us (40%)
  starting transfers between devices  38.4 us (34%)
  Pallas kernels  22.4 us (20%)
  other arithmetic  3.66 us (3%)
  between operations  2.02 us (2%)
  local copies, waits for them, and re-layouts  1.36 us (1%)
    ppermute x19, starting transfers between devices, shift(): lax.ppermute(value, axis, [(i, (i + distance) % n) for i in range(n)])  27.5 us
    ppermute x19, waiting for transfers between devices, shift(): lax.ppermute(value, axis, [(i, (i + distance) % n) for i in range(n)])  26.7 us
    pallas_call x10, Pallas kernels, call(): pl.pallas_call(body, out_shape=[jax.ShapeDtypeStruct(s, t) for s, t in sh...  22.4 us
    ppermute x10, waiting for transfers between devices, swap(): return lax.ppermute(value, axis, [(0, 1), (1, 0)])  16 us
    ppermute x10, starting transfers between devices, swap(): return lax.ppermute(value, axis, [(0, 1), (1, 0)])  10.5 us
    ppermute x1, waiting for transfers between devices, cross(): return lax.ppermute(value, ('xl', 'xh'), [(0, 3), (3, 0), (1, 2), (2, 1)])  3.01 us
  transfers between devices with their start and end apart: 30, of which 14 were waited for; matrix products, arithmetic and copies ran while one was open for 2% of the time, Pallas kernels for 19%

profile of v5, /device:TPU:2, one launch (start us, length us, event | category | flops | bytes accessed | tf_op | source)
XLA Modules:
  0.0 113.5 jit_solution(2073384511515249697)
XLA Ops:
  1.6 2.4 %collective-permute-start = (bf16[256,512]{1,0:T(8,128)(2,1)S(1)}, bf16[256,512]{1,0:T(8,128)(2,1)S(1)}, u32[]{:S(2)}, u32[]{:S(2)}) collective-permute-start(bf16[256,512]{1,0:T(8,128)(2,1)S(1)} %shard_map.102), channel_id=1, source_target_pairs={{0,16},{16,0},{1,17},{17,1},{2,18},{18,2},{3,19},{19,3},{4,20},{20... | collective-permute-start | bytes 786440 | tf_op jit(solution)/shard_map/ppermute | solution.py:21
  6.2 3.0 %collective-permute-done.2 = bf16[128,512]{1,0:T(8,128)(2,1)S(1)} collective-permute-done((bf16[128,512]{1,0:T(8,128)(2,1)}, bf16[128,512]{1,0:T(8,128)(2,1)S(1)}, u32[]{:S(2)}, u32[]{:S(2)}) %collective-permute-start.2) | collective-permute-done | bytes 131104 | tf_op jit(solution)/shard_map/ppermute | solution.py:30
  9.2 4.3 %collective-permute-done.1 = bf16[128,512]{1,0:T(8,128)(2,1)S(1)} collective-permute-done((bf16[128,512]{1,0:T(8,128)(2,1)}, bf16[128,512]{1,0:T(8,128)(2,1)S(1)}, u32[]{:S(2)}, u32[]{:S(2)}) %collective-permute-start.1) | collective-permute-done | bytes 131104 | tf_op jit(solution)/shard_map/ppermute | solution.py:21
  15.6 3.1 %collective-permute-start.6 = (bf16[2,128,1024]{2,1,0:T(8,128)(2,1)S(1)}, bf16[2,128,1024]{2,1,0:T(8,128)(2,1)S(1)}, u32[]{:S(2)}, u32[]{:S(2)}) collective-permute-start(bf16[2,128,1024]{2,1,0:T(8,128)(2,1)S(1)} %pad_maximum_fusion.refs_1_.refs_9_), channel_id=1, source_target_pairs={{0,6},{2,0},{4,2},{6,4},{1,7},{3,1},{5,3},{7,5},{8,14},{10,8},{12,... | collective-permute-start | bytes 1572872 | tf_op jit(solution)/shard_map/ppermute | solution.py:26
  18.7 2.0 %collective-permute-start.12 = (bf16[256,512]{1,0:T(8,128)(2,1)S(1)}, bf16[256,512]{1,0:T(8,128)(2,1)}, u32[]{:S(2)}, u32[]{:S(2)}) collective-permute-start(bf16[256,512]{1,0:T(8,128)(2,1)S(1)} %pad_maximum_fusion.2.refs_1_), channel_id=1, source_target_pairs={{0,32},{32,64},{64,96},{96,128},{128,160},{160,192},{192,224},{224... | collective-permute-start | bytes 786440 | tf_op jit(solution)/shard_map/ppermute | solution.py:26
  21.9 4.0 %collective-permute-start.15 = (bf16[256,512]{1,0:T(8,128)(2,1)S(1)}, bf16[256,512]{1,0:T(8,128)(2,1)S(1)}, u32[]{:S(2)}, u32[]{:S(2)}) collective-permute-start(bf16[256,512]{1,0:T(8,128)(2,1)S(1)} %pad_maximum_fusion.2.refs_1_), channel_id=1, source_target_pairs={{0,224},{32,0},{64,32},{96,64},{128,96},{160,128},{192,160},{224,1... | collective-permute-start | bytes 786440 | tf_op jit(solution)/shard_map/ppermute | solution.py:26
  25.9 4.0 %collective-permute-done.12.refs_2_ = bf16[256,512]{1,0:T(8,128)(2,1)} collective-permute-done((bf16[256,512]{1,0:T(8,128)(2,1)S(1)}, bf16[256,512]{1,0:T(8,128)(2,1)}, u32[]{:S(2)}, u32[]{:S(2)}) %collective-permute-start.12) | collective-permute-done | bytes 262176 | tf_op jit(solution)/shard_map/ppermute | solution.py:26
  32.4 2.4 %collective-permute-start.9 = (bf16[128,1024]{1,0:T(8,128)(2,1)S(1)}, bf16[128,1024]{1,0:T(8,128)(2,1)S(1)}, u32[]{:S(2)}, u32[]{:S(2)}) collective-permute-start(bf16[128,1024]{1,0:T(8,128)(2,1)S(1)} %slice_bitcast_fusion), channel_id=1, source_target_pairs={{0,6},{2,0},{4,2},{6,4},{1,7},{3,1},{5,3},{7,5},{8,14},{10,8},{12,... | collective-permute-start | bytes 786440 | tf_op jit(solution)/shard_map/ppermute | solution.py:26
  35.0 6.9 %collective-permute-done.11.refs_2_ = bf16[512,512]{1,0:T(8,128)(2,1)S(1)} collective-permute-done((bf16[512,512]{1,0:T(8,128)(2,1)S(1)}, bf16[512,512]{1,0:T(8,128)(2,1)S(1)}, u32[]{:S(2)}, u32[]{:S(2)}) %collective-permute-start.11) | collective-permute-done | bytes 524320 | tf_op jit(solution)/shard_map/ppermute | solution.py:21
  48.2 2.7 %collective-permute-done.14.refs_10_.refs_4_ = bf16[256,512]{1,0:T(8,128)(2,1)S(1)} collective-permute-done((bf16[256,512]{1,0:T(8,128)(2,1)S(1)}, bf16[256,512]{1,0:T(8,128)(2,1)S(1)}, u32[]{:S(2)}, u32[]{:S(2)}) %collective-permute-start.14) | collective-permute-done | bytes 262176 | tf_op jit(solution)/shard_map/ppermute | solution.py:26
  51.0 6.3 %collective-permute-done.17.refs_11_.refs_7_ = bf16[256,512]{1,0:T(8,128)(2,1)S(1)} collective-permute-done((bf16[256,512]{1,0:T(8,128)(2,1)S(1)}, bf16[256,512]{1,0:T(8,128)(2,1)S(1)}, u32[]{:S(2)}, u32[]{:S(2)}) %collective-permute-start.17) | collective-permute-done | bytes 262176 | tf_op jit(solution)/shard_map/ppermute | solution.py:26
  59.9 5.2 %shard_map.104 = (bf16[128,512]{1,0:T(8,128)(2,1)S(1)}, bf16[128,512]{1,0:T(8,128)(2,1)S(1)}, f32[2,256,512]{2,1,0:T(8,128)S(1)}, f32[2,256,512]{2,1,0:T(8,128)S...) custom-call(s32[16]{0:T(128)S(1)} %stack.104.refs_0_, bf16[2,128,1024]{2,1,0:T(8,128)(2,1)} %copy-done.4, ...), custom_call_target="tpu_custom_call" | custom-call | tf_op jit(solution)/shard_map/pallas_call | solution.py:60
  65.1 2.0 %collective-permute-done.22.refs_8_ = bf16[256,512]{1,0:T(8,128)(2,1)} collective-permute-done((bf16[256,512]{1,0:T(8,128)(2,1)S(1)}, bf16[256,512]{1,0:T(8,128)(2,1)}, u32[]{:S(2)}, u32[]{:S(2)}) %collective-permute-start.22) | collective-permute-done | bytes 262176 | tf_op jit(solution)/shard_map/ppermute | solution.py:26
  67.2 5.9 %shard_map.106.refs_1_ = bf16[512,1024]{1,0:T(8,128)(2,1)S(1)} custom-call(s32[16]{0:T(128)S(1)} %stack.111.refs_0_, bf16[256,512]{1,0:T(8,128)(2,1)} %copy-done.8, bf16[256,512]{1,0:T(8,128)(2,1)} %collective-permute-done.12.refs_2_, bf16[256,512]{1,0:T(8,128)(2,1)} %copy-done.11, bf16[256,512]{1,0:T(8,128)(2,1)} %copy-done.2, bf16[256,512]{1,0:T(8,128)(2,1)} %copy-done.10, ...), custom_call_target="tpu_custom_call" | custom-call | tf_op jit(solution)/shard_map/pallas_call | solution.py:60
  73.1 1.8 %collective-permute-start.28 = (bf16[512,1024]{1,0:T(8,128)(2,1)S(1)}, bf16[512,1024]{1,0:T(8,128)(2,1)S(1)}, u32[]{:S(2)}, u32[]{:S(2)}) collective-permute-start(bf16[512,1024]{1,0:T(8,128)(2,1)S(1)} %shard_map.106.refs_1_), channel_id=1, source_target_pairs={{0,16},{16,0},{1,17},{17,1},{2,18},{18,2},{3,19},{19,3},{4,20},{20... | collective-permute-start | bytes 3145736 | tf_op jit(solution)/shard_map/ppermute | solution.py:21
  74.9 3.2 %collective-permute-start.19 = (bf16[128,512]{1,0:T(8,128)(2,1)S(1)}, bf16[128,512]{1,0:T(8,128)(2,1)S(1)}, u32[]{:S(2)}, u32[]{:S(2)}) collective-permute-start(bf16[128,512]{1,0:T(8,128)(2,1)S(1)} %get-tuple-element.32), channel_id=1, source_target_pairs={{0,224},{32,0},{64,32},{96,64},{128,96},{160,128},{192,160},{224,1... | collective-permute-start | bytes 393224 | tf_op jit(solution)/shard_map/ppermute | solution.py:26
  78.2 2.9 %collective-permute-done.18.refs_2_ = bf16[128,512]{1,0:T(8,128)(2,1)S(1)} collective-permute-done((bf16[128,512]{1,0:T(8,128)(2,1)S(1)}, bf16[128,512]{1,0:T(8,128)(2,1)S(1)}, u32[]{:S(2)}, u32[]{:S(2)}) %collective-permute-start.18) | collective-permute-done | bytes 131104 | tf_op jit(solution)/shard_map/ppermute | solution.py:26
  81.5 3.0 %collective-permute-start.21 = (bf16[256,512]{1,0:T(8,128)(2,1)S(1)}, bf16[256,512]{1,0:T(8,128)(2,1)S(1)}, u32[]{:S(2)}, u32[]{:S(2)}) collective-permute-start(bf16[256,512]{1,0:T(8,128)(2,1)S(1)} %get-tuple-element.34), channel_id=1, source_target_pairs={{0,224},{32,0},{64,32},{96,64},{128,96},{160,128},{192,160},{224,1... | collective-permute-start | bytes 786440 | tf_op jit(solution)/shard_map/ppermute | solution.py:26
  84.6 2.4 %shard_map.107 = (f32[512,512]{1,0:T(8,128)S(1)}, f32[512,1024]{1,0:T(8,128)S(1)}, f32[1024,512]{1,0:T(8,128)S(1)}) custom-call(s32[1]{0:T(128)} %bitcast.24.refs_0_, bf16[512,1024]{1,0:T(8,128)(2,1)S(1)} %shard_map.106.refs_1_, bf16[1024,512]{1,0:T(8,128)(2,1)S(1)} %bitcast.35, bf16[512,1024]{1,0:T(8,128)(2,1)S(1)} %bitcast.38, ...), custom_call_target="tpu_custom_call" | custom-call | tf_op jit(solution)/shard_map/pallas_call | solution.py:60
  90.2 2.4 %collective-permute-start.25 = (bf16[256,512]{1,0:T(8,128)(2,1)S(1)}, bf16[256,512]{1,0:T(8,128)(2,1)S(1)}, u32[]{:S(2)}, u32[]{:S(2)}) collective-permute-start(bf16[256,512]{1,0:T(8,128)(2,1)S(1)} %get-tuple-element.38), channel_id=1, source_target_pairs={{0,224},{32,0},{64,32},{96,64},{128,96},{160,128},{192,160},{224,1... | collective-permute-start | bytes 786440 | tf_op jit(solution)/shard_map/ppermute | solution.py:26
  92.6 4.8 %collective-permute-done.24.refs_2_ = bf16[256,512]{1,0:T(8,128)(2,1)S(1)} collective-permute-done((bf16[256,512]{1,0:T(8,128)(2,1)S(1)}, bf16[256,512]{1,0:T(8,128)(2,1)S(1)}, u32[]{:S(2)}, u32[]{:S(2)}) %collective-permute-start.24) | collective-permute-done | bytes 262176 | tf_op jit(solution)/shard_map/ppermute | solution.py:26
  97.9 2.4 %collective-permute-start.26 = (bf16[256,512]{1,0:T(8,128)(2,1)S(1)}, bf16[256,512]{1,0:T(8,128)(2,1)S(1)}, u32[]{:S(2)}, u32[]{:S(2)}) collective-permute-start(bf16[256,512]{1,0:T(8,128)(2,1)S(1)} %get-tuple-element.39), channel_id=1, source_target_pairs={{0,32},{32,64},{64,96},{96,128},{128,160},{160,192},{192,224},{224... | collective-permute-start | bytes 786440 | tf_op jit(solution)/shard_map/ppermute | solution.py:26
  101.3 6.3 %shard_map.110 = (f32[512,1024]{1,0:T(8,128)}, f32[512,1024]{1,0:T(8,128)}, bf16[1024,512]{1,0:T(8,128)(2,1)}) custom-call(s32[1]{0:T(128)} %bitcast.24.refs_0_, bf16[512,1024]{1,0:T(8,128)(2,1)S(1)} %shard_map.106.refs_1_, bf16[512,1024]{1,0:T(8,128)(2,1)S(1)} %collective-permute-done.28.refs_2_, bf16[1024,512]{1,0:T(8,128)(2,1)S(1)} %bitcast.36, ...), custom_call_target="tpu_custom_call" | custom-call | tf_op jit(solution)/shard_map/pallas_call | solution.py:60
  108.0 4.8 %collective-permute-done.29 = bf16[128,512]{1,0:T(8,128)(2,1)S(1)} collective-permute-done((bf16[128,512]{1,0:T(8,128)(2,1)S(1)}, bf16[128,512]{1,0:T(8,128)(2,1)S(1)}, u32[]{:S(2)}, u32[]{:S(2)}) %collective-permute-start.29) | collective-permute-done | bytes 131104 | tf_op jit(solution)/shard_map/ppermute | solution.py:21
  (85 shorter events, 23.2 us)
Async XLA Ops:
  1.6 11.9 %collective-permute-start = (bf16[256,512]{1,0:T(8,128)(2,1)S(1)}, bf16[256,512]{1,0:T(8,128)(2,1)S(1)}, u32[]{:S(2)}, u32[]{:S(2)}) collective-permute-start(bf16[256,512]{1,0:T(8,128)(2,1)S(1)} %shard_map.102), channel_id=1, source_target_pairs={{0,16},{16,0},{1,17},{17,1},{2,18},{18,2},{3,19},{19,3},{4,20},{20... | collective-permute-start | bytes 786440 | tf_op jit(solution)/shard_map/ppermute | solution.py:21
  4.4 9.1 %collective-permute-start.1 = (bf16[128,512]{1,0:T(8,128)(2,1)}, bf16[128,512]{1,0:T(8,128)(2,1)S(1)}, u32[]{:S(2)}, u32[]{:S(2)}) collective-permute-start(bf16[128,512]{1,0:T(8,128)(2,1)} %refs_2_.1), channel_id=1, source_target_pairs={{0,8},{8,0},{1,9},{9,1},{2,10},{10,2},{3,11},{11,3},{4,12},{12,4},... | collective-permute-start | bytes 393224 | tf_op jit(solution)/shard_map/ppermute | solution.py:21
  15.6 16.1 %collective-permute-start.6 = (bf16[2,128,1024]{2,1,0:T(8,128)(2,1)S(1)}, bf16[2,128,1024]{2,1,0:T(8,128)(2,1)S(1)}, u32[]{:S(2)}, u32[]{:S(2)}) collective-permute-start(bf16[2,128,1024]{2,1,0:T(8,128)(2,1)S(1)} %pad_maximum_fusion.refs_1_.refs_9_), channel_id=1, source_target_pairs={{0,6},{2,0},{4,2},{6,4},{1,7},{3,1},{5,3},{7,5},{8,14},{10,8},{12,... | collective-permute-start | bytes 1572872 | tf_op jit(solution)/shard_map/ppermute | solution.py:26
  18.7 13.7 %collective-permute-start.4 = (bf16[2,128,1024]{2,1,0:T(8,128)(2,1)S(1)}, bf16[2,128,1024]{2,1,0:T(8,128)(2,1)S(1)}, u32[]{:S(2)}, u32[]{:S(2)}) collective-permute-start(bf16[2,128,1024]{2,1,0:T(8,128)(2,1)S(1)} %pad_maximum_fusion.refs_1_.refs_9_), channel_id=1, source_target_pairs={{0,2},{2,4},{4,6},{6,0},{1,3},{3,5},{5,7},{7,1},{8,10},{10,12},{12... | collective-permute-start | bytes 1572872 | tf_op jit(solution)/shard_map/ppermute | solution.py:26
  18.7 11.2 %collective-permute-start.12 = (bf16[256,512]{1,0:T(8,128)(2,1)S(1)}, bf16[256,512]{1,0:T(8,128)(2,1)}, u32[]{:S(2)}, u32[]{:S(2)}) collective-permute-start(bf16[256,512]{1,0:T(8,128)(2,1)S(1)} %pad_maximum_fusion.2.refs_1_), channel_id=1, source_target_pairs={{0,32},{32,64},{64,96},{96,128},{128,160},{160,192},{192,224},{224... | collective-permute-start | bytes 786440 | tf_op jit(solution)/shard_map/ppermute | solution.py:26
  21.8 24.8 %collective-permute-start.3 = (bf16[2,128,1024]{2,1,0:T(8,128)(2,1)S(1)}, bf16[2,128,1024]{2,1,0:T(8,128)(2,1)S(1)}, u32[]{:S(2)}, u32[]{:S(2)}) collective-permute-start(bf16[2,128,1024]{2,1,0:T(8,128)(2,1)S(1)} %pad_maximum_fusion.refs_1_.refs_9_), channel_id=1, source_target_pairs={{0,1},{1,0},{2,3},{3,2},{4,5},{5,4},{6,7},{7,6},{8,9},{9,8},{10,11... | collective-permute-start | bytes 1572872 | tf_op jit(solution)/shard_map/ppermute | solution.py:21
  21.9 12.9 %collective-permute-start.15 = (bf16[256,512]{1,0:T(8,128)(2,1)S(1)}, bf16[256,512]{1,0:T(8,128)(2,1)S(1)}, u32[]{:S(2)}, u32[]{:S(2)}) collective-permute-start(bf16[256,512]{1,0:T(8,128)(2,1)S(1)} %pad_maximum_fusion.2.refs_1_), channel_id=1, source_target_pairs={{0,224},{32,0},{64,32},{96,64},{128,96},{160,128},{192,160},{224,1... | collective-permute-start | bytes 786440 | tf_op jit(solution)/shard_map/ppermute | solution.py:26
  29.9 11.9 %collective-permute-start.11 = (bf16[512,512]{1,0:T(8,128)(2,1)S(1)}, bf16[512,512]{1,0:T(8,128)(2,1)S(1)}, u32[]{:S(2)}, u32[]{:S(2)}) collective-permute-start(bf16[512,512]{1,0:T(8,128)(2,1)S(1)} %constant_dynamic-slice_fusion), channel_id=1, source_target_pairs={{0,16},{16,0},{1,17},{17,1},{2,18},{18,2},{3,19},{19,3},{4,20},{20... | collective-permute-start | bytes 1572872 | tf_op jit(solution)/shard_map/ppermute | solution.py:21
  31.7 11.6 %collective-permute-start.13 = (bf16[256,512]{1,0:T(8,128)(2,1)}, bf16[256,512]{1,0:T(8,128)(2,1)S(1)}, u32[]{:S(2)}, u32[]{:S(2)}) collective-permute-start(bf16[256,512]{1,0:T(8,128)(2,1)} %collective-permute-done.12.refs_2_), channel_id=1, source_target_pairs={{0,32},{32,64},{64,96},{96,128},{128,160},{160,192},{192,224},{224... | collective-permute-start | bytes 786440 | tf_op jit(solution)/shard_map/ppermute | solution.py:26
  32.4 11.5 %collective-permute-start.9 = (bf16[128,1024]{1,0:T(8,128)(2,1)S(1)}, bf16[128,1024]{1,0:T(8,128)(2,1)S(1)}, u32[]{:S(2)}, u32[]{:S(2)}) collective-permute-start(bf16[128,1024]{1,0:T(8,128)(2,1)S(1)} %slice_bitcast_fusion), channel_id=1, source_target_pairs={{0,6},{2,0},{4,2},{6,4},{1,7},{3,1},{5,3},{7,5},{8,14},{10,8},{12,... | collective-permute-start | bytes 786440 | tf_op jit(solution)/shard_map/ppermute | solution.py:26
  34.9 10.9 %collective-permute-start.8 = (bf16[128,1024]{1,0:T(8,128)(2,1)S(1)}, bf16[128,1024]{1,0:T(8,128)(2,1)S(1)}, u32[]{:S(2)}, u32[]{:S(2)}) collective-permute-start(bf16[128,1024]{1,0:T(8,128)(2,1)S(1)} %slice_bitcast_fusion.1), channel_id=1, source_target_pairs={{0,2},{2,4},{4,6},{6,0},{1,3},{3,5},{5,7},{7,1},{8,10},{10,12},{12... | collective-permute-start | bytes 786440 | tf_op jit(solution)/shard_map/ppermute | solution.py:26
  43.3 7.6 %collective-permute-start.14 = (bf16[256,512]{1,0:T(8,128)(2,1)S(1)}, bf16[256,512]{1,0:T(8,128)(2,1)S(1)}, u32[]{:S(2)}, u32[]{:S(2)}) collective-permute-start(bf16[256,512]{1,0:T(8,128)(2,1)S(1)} %collective-permute-done.13.refs_3_), channel_id=1, source_target_pairs={{0,32},{32,64},{64,96},{96,128},{128,160},{160,192},{192,224},{224... | collective-permute-start | bytes 786440 | tf_op jit(solution)/shard_map/ppermute | solution.py:26
  43.9 40.6 %collective-permute-start.23 = (bf16[512,1024]{1,0:T(8,128)(2,1)S(1)}, bf16[512,1024]{1,0:T(8,128)(2,1)S(1)}, u32[]{:S(2)}, u32[]{:S(2)}) collective-permute-start(bf16[512,1024]{1,0:T(8,128)(2,1)S(1)} %bitcast.37), channel_id=1, source_target_pairs={{0,16},{16,0},{1,17},{17,1},{2,18},{18,2},{3,19},{19,3},{4,20},{20... | collective-permute-start | bytes 3145736 | tf_op jit(solution)/shard_map/ppermute | solution.py:21
  45.8 14.1 %collective-permute-start.5 = (bf16[2,128,1024]{2,1,0:T(8,128)(2,1)}, bf16[2,128,1024]{2,1,0:T(8,128)(2,1)}, u32[]{:S(2)}, u32[]{:S(2)}) collective-permute-start(bf16[2,128,1024]{2,1,0:T(8,128)(2,1)} %copy-done.6), channel_id=1, source_target_pairs={{0,1},{1,0},{2,3},{3,2},{4,5},{5,4},{6,7},{7,6},{8,9},{9,8},{10,11... | collective-permute-start | bytes 1572872 | tf_op jit(solution)/shard_map/ppermute | solution.py:21
  46.6 13.3 %collective-permute-start.7 = (bf16[2,128,1024]{2,1,0:T(8,128)(2,1)}, bf16[2,128,1024]{2,1,0:T(8,128)(2,1)}, u32[]{:S(2)}, u32[]{:S(2)}) collective-permute-start(bf16[2,128,1024]{2,1,0:T(8,128)(2,1)} %copy-done.5), channel_id=1, source_target_pairs={{0,1},{1,0},{2,3},{3,2},{4,5},{5,4},{6,7},{7,6},{8,9},{9,8},{10,11... | collective-permute-start | bytes 1572872 | tf_op jit(solution)/shard_map/ppermute | solution.py:21
  48.2 11.7 %collective-permute-start.10 = (bf16[2,128,1024]{2,1,0:T(8,128)(2,1)}, bf16[2,128,1024]{2,1,0:T(8,128)(2,1)}, u32[]{:S(2)}, u32[]{:S(2)}) collective-permute-start(bf16[2,128,1024]{2,1,0:T(8,128)(2,1)} %pad_maximum_fusion.1.refs_7_.refs_15_), channel_id=1, source_target_pairs={{0,1},{1,0},{2,3},{3,2},{4,5},{5,4},{6,7},{7,6},{8,9},{9,8},{10,11... | collective-permute-start | bytes 1572872 | tf_op jit(solution)/shard_map/ppermute | solution.py:21
  57.3 9.9 %collective-permute-start.22 = (bf16[256,512]{1,0:T(8,128)(2,1)S(1)}, bf16[256,512]{1,0:T(8,128)(2,1)}, u32[]{:S(2)}, u32[]{:S(2)}) collective-permute-start(bf16[256,512]{1,0:T(8,128)(2,1)S(1)} %collective-permute-done.14.refs_10_.refs_4_), channel_id=1, source_target_pairs={{0,32},{32,64},{64,96},{96,128},{128,160},{160,192},{192,224},{224... | collective-permute-start | bytes 786440 | tf_op jit(solution)/shard_map/ppermute | solution.py:26
  73.1 28.2 %collective-permute-start.28 = (bf16[512,1024]{1,0:T(8,128)(2,1)S(1)}, bf16[512,1024]{1,0:T(8,128)(2,1)S(1)}, u32[]{:S(2)}, u32[]{:S(2)}) collective-permute-start(bf16[512,1024]{1,0:T(8,128)(2,1)S(1)} %shard_map.106.refs_1_), channel_id=1, source_target_pairs={{0,16},{16,0},{1,17},{17,1},{2,18},{18,2},{3,19},{19,3},{4,20},{20... | collective-permute-start | bytes 3145736 | tf_op jit(solution)/shard_map/ppermute | solution.py:21
  81.2 7.7 %collective-permute-start.20 = (bf16[256,512]{1,0:T(8,128)(2,1)S(1)}, bf16[256,512]{1,0:T(8,128)(2,1)S(1)}, u32[]{:S(2)}, u32[]{:S(2)}) collective-permute-start(bf16[256,512]{1,0:T(8,128)(2,1)S(1)} %get-tuple-element.33), channel_id=1, source_target_pairs={{0,32},{32,64},{64,96},{96,128},{128,160},{160,192},{192,224},{224... | collective-permute-start | bytes 786440 | tf_op jit(solution)/shard_map/ppermute | solution.py:26
  81.5 7.3 %collective-permute-start.21 = (bf16[256,512]{1,0:T(8,128)(2,1)S(1)}, bf16[256,512]{1,0:T(8,128)(2,1)S(1)}, u32[]{:S(2)}, u32[]{:S(2)}) collective-permute-start(bf16[256,512]{1,0:T(8,128)(2,1)S(1)} %get-tuple-element.34), channel_id=1, source_target_pairs={{0,224},{32,0},{64,32},{96,64},{128,96},{160,128},{192,160},{224,1... | collective-permute-start | bytes 786440 | tf_op jit(solution)/shard_map/ppermute | solution.py:26
  88.9 8.5 %collective-permute-start.24 = (bf16[256,512]{1,0:T(8,128)(2,1)S(1)}, bf16[256,512]{1,0:T(8,128)(2,1)S(1)}, u32[]{:S(2)}, u32[]{:S(2)}) collective-permute-start(bf16[256,512]{1,0:T(8,128)(2,1)S(1)} %get-tuple-element.37), channel_id=1, source_target_pairs={{0,32},{32,64},{64,96},{96,128},{128,160},{160,192},{192,224},{224... | collective-permute-start | bytes 786440 | tf_op jit(solution)/shard_map/ppermute | solution.py:26
  90.2 7.6 %collective-permute-start.25 = (bf16[256,512]{1,0:T(8,128)(2,1)S(1)}, bf16[256,512]{1,0:T(8,128)(2,1)S(1)}, u32[]{:S(2)}, u32[]{:S(2)}) collective-permute-start(bf16[256,512]{1,0:T(8,128)(2,1)S(1)} %get-tuple-element.38), channel_id=1, source_target_pairs={{0,224},{32,0},{64,32},{96,64},{128,96},{160,128},{192,160},{224,1... | collective-permute-start | bytes 786440 | tf_op jit(solution)/shard_map/ppermute | solution.py:26
  97.9 9.7 %collective-permute-start.26 = (bf16[256,512]{1,0:T(8,128)(2,1)S(1)}, bf16[256,512]{1,0:T(8,128)(2,1)S(1)}, u32[]{:S(2)}, u32[]{:S(2)}) collective-permute-start(bf16[256,512]{1,0:T(8,128)(2,1)S(1)} %get-tuple-element.39), channel_id=1, source_target_pairs={{0,32},{32,64},{64,96},{96,128},{128,160},{160,192},{192,224},{224... | collective-permute-start | bytes 786440 | tf_op jit(solution)/shard_map/ppermute | solution.py:26
  100.3 7.3 %collective-permute-start.27 = (bf16[256,512]{1,0:T(8,128)(2,1)S(1)}, bf16[256,512]{1,0:T(8,128)(2,1)S(1)}, u32[]{:S(2)}, u32[]{:S(2)}) collective-permute-start(bf16[256,512]{1,0:T(8,128)(2,1)S(1)} %get-tuple-element.40), channel_id=1, source_target_pairs={{0,224},{32,0},{64,32},{96,64},{128,96},{160,128},{192,160},{224,1... | collective-permute-start | bytes 786440 | tf_op jit(solution)/shard_map/ppermute | solution.py:26
  (19 other events, 267.6 us)

commit v6 on v5

--- a/solution.py
+++ b/solution.py
@@ -94,7 +94,7 @@
             up[...] = part[:rows].astype(BF16)
             down[...] = part[rows:].astype(BF16)
         else:
-            outs[(k - 1) // 2][(k - 1) % 2] = part
+            outs[(k - 1) // 2][(k - 1) % 2] = part.astype(BF16)
 
 
 def grad_kernel(index, *refs):
@@ -287,7 +287,7 @@
     small, full = ((tok, d), BF16), ((2 * tok, d), BF16)
     up, down, *parts, part_0 = call(
         part_kernel,
-        [small, small] + [((2, 2 * tok, d), F32)] * 3 + [((1, 2 * tok, d), F32)],
+        [small, small] + [((2, 2 * tok, d), BF16)] * 3 + [((1, 2 * tok, d), BF16)],
         places(4, 3, -3, 2, -2, 1, -1, 0),
         *pieces,
         weight,

time: 114 us -> 114 us (level)
  no operation moved by 1% of the time
where the time goes in v6:
time: 114 us
  waiting for transfers between devices  45.7 us (40%)
  starting transfers between devices  38.4 us (34%)
  Pallas kernels  22.5 us (20%)
  other arithmetic  3.66 us (3%)
  between operations  2.01 us (2%)
  local copies, waits for them, and re-layouts  1.36 us (1%)
    ppermute x19, starting transfers between devices, shift(): lax.ppermute(value, axis, [(i, (i + distance) % n) for i in range(n)])  27.5 us
    ppermute x19, waiting for transfers between devices, shift(): lax.ppermute(value, axis, [(i, (i + distance) % n) for i in range(n)])  26.7 us
    pallas_call x10, Pallas kernels, call(): pl.pallas_call(body, out_shape=[jax.ShapeDtypeStruct(s, t) for s, t in sh...  22.5 us
    ppermute x10, waiting for transfers between devices, swap(): return lax.ppermute(value, axis, [(0, 1), (1, 0)])  16 us
    ppermute x10, starting transfers between devices, swap(): return lax.ppermute(value, axis, [(0, 1), (1, 0)])  10.5 us
    ppermute x1, waiting for transfers between devices, cross(): return lax.ppermute(value, ('xl', 'xh'), [(0, 3), (3, 0), (1, 2), (2, 1)])  3.01 us
  transfers between devices with their start and end apart: 30, of which 14 were waited for; matrix products, arithmetic and copies ran while one was open for 2% of the time, Pallas kernels for 19%

profile of v6, /device:TPU:2, one launch (start us, length us, event | category | flops | bytes accessed | tf_op | source)
XLA Modules:
  0.0 113.6 jit_solution(13870594787047042624)
XLA Ops:
  1.6 2.4 %collective-permute-start = (bf16[256,512]{1,0:T(8,128)(2,1)S(1)}, bf16[256,512]{1,0:T(8,128)(2,1)S(1)}, u32[]{:S(2)}, u32[]{:S(2)}) collective-permute-start(bf16[256,512]{1,0:T(8,128)(2,1)S(1)} %shard_map.102), channel_id=1, source_target_pairs={{0,16},{16,0},{1,17},{17,1},{2,18},{18,2},{3,19},{19,3},{4,20},{20... | collective-permute-start | bytes 786440 | tf_op jit(solution)/shard_map/ppermute | solution.py:21
  6.2 3.0 %collective-permute-done.2 = bf16[128,512]{1,0:T(8,128)(2,1)S(1)} collective-permute-done((bf16[128,512]{1,0:T(8,128)(2,1)}, bf16[128,512]{1,0:T(8,128)(2,1)S(1)}, u32[]{:S(2)}, u32[]{:S(2)}) %collective-permute-start.2) | collective-permute-done | bytes 131104 | tf_op jit(solution)/shard_map/ppermute | solution.py:30
  9.2 4.3 %collective-permute-done.1 = bf16[128,512]{1,0:T(8,128)(2,1)S(1)} collective-permute-done((bf16[128,512]{1,0:T(8,128)(2,1)}, bf16[128,512]{1,0:T(8,128)(2,1)S(1)}, u32[]{:S(2)}, u32[]{:S(2)}) %collective-permute-start.1) | collective-permute-done | bytes 131104 | tf_op jit(solution)/shard_map/ppermute | solution.py:21
  15.6 3.1 %collective-permute-start.6 = (bf16[2,128,1024]{2,1,0:T(8,128)(2,1)S(1)}, bf16[2,128,1024]{2,1,0:T(8,128)(2,1)S(1)}, u32[]{:S(2)}, u32[]{:S(2)}) collective-permute-start(bf16[2,128,1024]{2,1,0:T(8,128)(2,1)S(1)} %pad_maximum_fusion.refs_1_.refs_9_), channel_id=1, source_target_pairs={{0,6},{2,0},{4,2},{6,4},{1,7},{3,1},{5,3},{7,5},{8,14},{10,8},{12,... | collective-permute-start | bytes 1572872 | tf_op jit(solution)/shard_map/ppermute | solution.py:26
  18.7 2.0 %collective-permute-start.12 = (bf16[256,512]{1,0:T(8,128)(2,1)S(1)}, bf16[256,512]{1,0:T(8,128)(2,1)}, u32[]{:S(2)}, u32[]{:S(2)}) collective-permute-start(bf16[256,512]{1,0:T(8,128)(2,1)S(1)} %pad_maximum_fusion.2.refs_1_), channel_id=1, source_target_pairs={{0,32},{32,64},{64,96},{96,128},{128,160},{160,192},{192,224},{224... | collective-permute-start | bytes 786440 | tf_op jit(solution)/shard_map/ppermute | solution.py:26
  21.9 4.0 %collective-permute-start.15 = (bf16[256,512]{1,0:T(8,128)(2,1)S(1)}, bf16[256,512]{1,0:T(8,128)(2,1)S(1)}, u32[]{:S(2)}, u32[]{:S(2)}) collective-permute-start(bf16[256,512]{1,0:T(8,128)(2,1)S(1)} %pad_maximum_fusion.2.refs_1_), channel_id=1, source_target_pairs={{0,224},{32,0},{64,32},{96,64},{128,96},{160,128},{192,160},{224,1... | collective-permute-start | bytes 786440 | tf_op jit(solution)/shard_map/ppermute | solution.py:26
  25.9 4.0 %collective-permute-done.12.refs_2_ = bf16[256,512]{1,0:T(8,128)(2,1)} collective-permute-done((bf16[256,512]{1,0:T(8,128)(2,1)S(1)}, bf16[256,512]{1,0:T(8,128)(2,1)}, u32[]{:S(2)}, u32[]{:S(2)}) %collective-permute-start.12) | collective-permute-done | bytes 262176 | tf_op jit(solution)/shard_map/ppermute | solution.py:26
  32.4 2.4 %collective-permute-start.9 = (bf16[128,1024]{1,0:T(8,128)(2,1)S(1)}, bf16[128,1024]{1,0:T(8,128)(2,1)S(1)}, u32[]{:S(2)}, u32[]{:S(2)}) collective-permute-start(bf16[128,1024]{1,0:T(8,128)(2,1)S(1)} %slice_bitcast_fusion), channel_id=1, source_target_pairs={{0,6},{2,0},{4,2},{6,4},{1,7},{3,1},{5,3},{7,5},{8,14},{10,8},{12,... | collective-permute-start | bytes 786440 | tf_op jit(solution)/shard_map/ppermute | solution.py:26
  35.0 6.9 %collective-permute-done.11.refs_2_ = bf16[512,512]{1,0:T(8,128)(2,1)S(1)} collective-permute-done((bf16[512,512]{1,0:T(8,128)(2,1)S(1)}, bf16[512,512]{1,0:T(8,128)(2,1)S(1)}, u32[]{:S(2)}, u32[]{:S(2)}) %collective-permute-start.11) | collective-permute-done | bytes 524320 | tf_op jit(solution)/shard_map/ppermute | solution.py:21
  48.2 2.7 %collective-permute-done.14.refs_10_.refs_4_ = bf16[256,512]{1,0:T(8,128)(2,1)S(1)} collective-permute-done((bf16[256,512]{1,0:T(8,128)(2,1)S(1)}, bf16[256,512]{1,0:T(8,128)(2,1)S(1)}, u32[]{:S(2)}, u32[]{:S(2)}) %collective-permute-start.14) | collective-permute-done | bytes 262176 | tf_op jit(solution)/shard_map/ppermute | solution.py:26
  51.0 6.3 %collective-permute-done.17.refs_11_.refs_7_ = bf16[256,512]{1,0:T(8,128)(2,1)S(1)} collective-permute-done((bf16[256,512]{1,0:T(8,128)(2,1)S(1)}, bf16[256,512]{1,0:T(8,128)(2,1)S(1)}, u32[]{:S(2)}, u32[]{:S(2)}) %collective-permute-start.17) | collective-permute-done | bytes 262176 | tf_op jit(solution)/shard_map/ppermute | solution.py:26
  59.9 5.2 %shard_map.104 = (bf16[128,512]{1,0:T(8,128)(2,1)S(1)}, bf16[128,512]{1,0:T(8,128)(2,1)S(1)}, bf16[2,256,512]{2,1,0:T(8,128)(2,1)S(1)}, bf16[2,256,512]{2,1,0:T(...) custom-call(s32[16]{0:T(128)S(1)} %stack.104.refs_0_, ...), custom_call_target="tpu_custom_call" | custom-call | tf_op jit(solution)/shard_map/pallas_call | solution.py:60
  65.1 2.0 %collective-permute-done.22.refs_8_ = bf16[256,512]{1,0:T(8,128)(2,1)} collective-permute-done((bf16[256,512]{1,0:T(8,128)(2,1)S(1)}, bf16[256,512]{1,0:T(8,128)(2,1)}, u32[]{:S(2)}, u32[]{:S(2)}) %collective-permute-start.22) | collective-permute-done | bytes 262176 | tf_op jit(solution)/shard_map/ppermute | solution.py:26
  67.2 5.9 %shard_map.106.refs_1_ = bf16[512,1024]{1,0:T(8,128)(2,1)S(1)} custom-call(s32[16]{0:T(128)S(1)} %stack.111.refs_0_, bf16[256,512]{1,0:T(8,128)(2,1)} %copy-done.8, bf16[256,512]{1,0:T(8,128)(2,1)} %collective-permute-done.12.refs_2_, bf16[256,512]{1,0:T(8,128)(2,1)} %copy-done.11, bf16[256,512]{1,0:T(8,128)(2,1)} %copy-done.2, bf16[256,512]{1,0:T(8,128)(2,1)} %copy-done.10, ...), custom_call_target="tpu_custom_call" | custom-call | tf_op jit(solution)/shard_map/pallas_call | solution.py:60
  73.1 1.8 %collective-permute-start.28 = (bf16[512,1024]{1,0:T(8,128)(2,1)S(1)}, bf16[512,1024]{1,0:T(8,128)(2,1)S(1)}, u32[]{:S(2)}, u32[]{:S(2)}) collective-permute-start(bf16[512,1024]{1,0:T(8,128)(2,1)S(1)} %shard_map.106.refs_1_), channel_id=1, source_target_pairs={{0,16},{16,0},{1,17},{17,1},{2,18},{18,2},{3,19},{19,3},{4,20},{20... | collective-permute-start | bytes 3145736 | tf_op jit(solution)/shard_map/ppermute | solution.py:21
  74.9 3.2 %collective-permute-start.19 = (bf16[128,512]{1,0:T(8,128)(2,1)S(1)}, bf16[128,512]{1,0:T(8,128)(2,1)S(1)}, u32[]{:S(2)}, u32[]{:S(2)}) collective-permute-start(bf16[128,512]{1,0:T(8,128)(2,1)S(1)} %get-tuple-element.32), channel_id=1, source_target_pairs={{0,224},{32,0},{64,32},{96,64},{128,96},{160,128},{192,160},{224,1... | collective-permute-start | bytes 393224 | tf_op jit(solution)/shard_map/ppermute | solution.py:26
  78.2 2.9 %collective-permute-done.18.refs_2_ = bf16[128,512]{1,0:T(8,128)(2,1)S(1)} collective-permute-done((bf16[128,512]{1,0:T(8,128)(2,1)S(1)}, bf16[128,512]{1,0:T(8,128)(2,1)S(1)}, u32[]{:S(2)}, u32[]{:S(2)}) %collective-permute-start.18) | collective-permute-done | bytes 131104 | tf_op jit(solution)/shard_map/ppermute | solution.py:26
  81.5 3.0 %collective-permute-start.21 = (bf16[256,512]{1,0:T(8,128)(2,1)S(1)}, bf16[256,512]{1,0:T(8,128)(2,1)S(1)}, u32[]{:S(2)}, u32[]{:S(2)}) collective-permute-start(bf16[256,512]{1,0:T(8,128)(2,1)S(1)} %get-tuple-element.34), channel_id=1, source_target_pairs={{0,224},{32,0},{64,32},{96,64},{128,96},{160,128},{192,160},{224,1... | collective-permute-start | bytes 786440 | tf_op jit(solution)/shard_map/ppermute | solution.py:26
  84.6 2.4 %shard_map.107 = (f32[512,512]{1,0:T(8,128)S(1)}, f32[512,1024]{1,0:T(8,128)S(1)}, f32[1024,512]{1,0:T(8,128)S(1)}) custom-call(s32[1]{0:T(128)} %bitcast.24.refs_0_, bf16[512,1024]{1,0:T(8,128)(2,1)S(1)} %shard_map.106.refs_1_, bf16[1024,512]{1,0:T(8,128)(2,1)S(1)} %bitcast.35, bf16[512,1024]{1,0:T(8,128)(2,1)S(1)} %bitcast.38, ...), custom_call_target="tpu_custom_call" | custom-call | tf_op jit(solution)/shard_map/pallas_call | solution.py:60
  90.3 2.4 %collective-permute-start.25 = (bf16[256,512]{1,0:T(8,128)(2,1)S(1)}, bf16[256,512]{1,0:T(8,128)(2,1)S(1)}, u32[]{:S(2)}, u32[]{:S(2)}) collective-permute-start(bf16[256,512]{1,0:T(8,128)(2,1)S(1)} %get-tuple-element.38), channel_id=1, source_target_pairs={{0,224},{32,0},{64,32},{96,64},{128,96},{160,128},{192,160},{224,1... | collective-permute-start | bytes 786440 | tf_op jit(solution)/shard_map/ppermute | solution.py:26
  92.7 4.8 %collective-permute-done.24.refs_2_ = bf16[256,512]{1,0:T(8,128)(2,1)S(1)} collective-permute-done((bf16[256,512]{1,0:T(8,128)(2,1)S(1)}, bf16[256,512]{1,0:T(8,128)(2,1)S(1)}, u32[]{:S(2)}, u32[]{:S(2)}) %collective-permute-start.24) | collective-permute-done | bytes 262176 | tf_op jit(solution)/shard_map/ppermute | solution.py:26
  97.9 2.4 %collective-permute-start.26 = (bf16[256,512]{1,0:T(8,128)(2,1)S(1)}, bf16[256,512]{1,0:T(8,128)(2,1)S(1)}, u32[]{:S(2)}, u32[]{:S(2)}) collective-permute-start(bf16[256,512]{1,0:T(8,128)(2,1)S(1)} %get-tuple-element.39), channel_id=1, source_target_pairs={{0,32},{32,64},{64,96},{96,128},{128,160},{160,192},{192,224},{224... | collective-permute-start | bytes 786440 | tf_op jit(solution)/shard_map/ppermute | solution.py:26
  101.3 6.3 %shard_map.110 = (f32[512,1024]{1,0:T(8,128)}, f32[512,1024]{1,0:T(8,128)}, bf16[1024,512]{1,0:T(8,128)(2,1)}) custom-call(s32[1]{0:T(128)} %bitcast.24.refs_0_, bf16[512,1024]{1,0:T(8,128)(2,1)S(1)} %shard_map.106.refs_1_, bf16[512,1024]{1,0:T(8,128)(2,1)S(1)} %collective-permute-done.28.refs_2_, bf16[1024,512]{1,0:T(8,128)(2,1)S(1)} %bitcast.36, ...), custom_call_target="tpu_custom_call" | custom-call | tf_op jit(solution)/shard_map/pallas_call | solution.py:60
  108.1 4.8 %collective-permute-done.29 = bf16[128,512]{1,0:T(8,128)(2,1)S(1)} collective-permute-done((bf16[128,512]{1,0:T(8,128)(2,1)S(1)}, bf16[128,512]{1,0:T(8,128)(2,1)S(1)}, u32[]{:S(2)}, u32[]{:S(2)}) %collective-permute-start.29) | collective-permute-done | bytes 131104 | tf_op jit(solution)/shard_map/ppermute | solution.py:21
  (85 shorter events, 23.3 us)
Async XLA Ops:
  1.6 11.9 %collective-permute-start = (bf16[256,512]{1,0:T(8,128)(2,1)S(1)}, bf16[256,512]{1,0:T(8,128)(2,1)S(1)}, u32[]{:S(2)}, u32[]{:S(2)}) collective-permute-start(bf16[256,512]{1,0:T(8,128)(2,1)S(1)} %shard_map.102), channel_id=1, source_target_pairs={{0,16},{16,0},{1,17},{17,1},{2,18},{18,2},{3,19},{19,3},{4,20},{20... | collective-permute-start | bytes 786440 | tf_op jit(solution)/shard_map/ppermute | solution.py:21
  4.4 9.1 %collective-permute-start.1 = (bf16[128,512]{1,0:T(8,128)(2,1)}, bf16[128,512]{1,0:T(8,128)(2,1)S(1)}, u32[]{:S(2)}, u32[]{:S(2)}) collective-permute-start(bf16[128,512]{1,0:T(8,128)(2,1)} %refs_2_.1), channel_id=1, source_target_pairs={{0,8},{8,0},{1,9},{9,1},{2,10},{10,2},{3,11},{11,3},{4,12},{12,4},... | collective-permute-start | bytes 393224 | tf_op jit(solution)/shard_map/ppermute | solution.py:21
  15.6 16.1 %collective-permute-start.6 = (bf16[2,128,1024]{2,1,0:T(8,128)(2,1)S(1)}, bf16[2,128,1024]{2,1,0:T(8,128)(2,1)S(1)}, u32[]{:S(2)}, u32[]{:S(2)}) collective-permute-start(bf16[2,128,1024]{2,1,0:T(8,128)(2,1)S(1)} %pad_maximum_fusion.refs_1_.refs_9_), channel_id=1, source_target_pairs={{0,6},{2,0},{4,2},{6,4},{1,7},{3,1},{5,3},{7,5},{8,14},{10,8},{12,... | collective-permute-start | bytes 1572872 | tf_op jit(solution)/shard_map/ppermute | solution.py:26
  18.7 13.7 %collective-permute-start.4 = (bf16[2,128,1024]{2,1,0:T(8,128)(2,1)S(1)}, bf16[2,128,1024]{2,1,0:T(8,128)(2,1)S(1)}, u32[]{:S(2)}, u32[]{:S(2)}) collective-permute-start(bf16[2,128,1024]{2,1,0:T(8,128)(2,1)S(1)} %pad_maximum_fusion.refs_1_.refs_9_), channel_id=1, source_target_pairs={{0,2},{2,4},{4,6},{6,0},{1,3},{3,5},{5,7},{7,1},{8,10},{10,12},{12... | collective-permute-start | bytes 1572872 | tf_op jit(solution)/shard_map/ppermute | solution.py:26
  18.7 11.2 %collective-permute-start.12 = (bf16[256,512]{1,0:T(8,128)(2,1)S(1)}, bf16[256,512]{1,0:T(8,128)(2,1)}, u32[]{:S(2)}, u32[]{:S(2)}) collective-permute-start(bf16[256,512]{1,0:T(8,128)(2,1)S(1)} %pad_maximum_fusion.2.refs_1_), channel_id=1, source_target_pairs={{0,32},{32,64},{64,96},{96,128},{128,160},{160,192},{192,224},{224... | collective-permute-start | bytes 786440 | tf_op jit(solution)/shard_map/ppermute | solution.py:26
  21.8 24.8 %collective-permute-start.3 = (bf16[2,128,1024]{2,1,0:T(8,128)(2,1)S(1)}, bf16[2,128,1024]{2,1,0:T(8,128)(2,1)S(1)}, u32[]{:S(2)}, u32[]{:S(2)}) collective-permute-start(bf16[2,128,1024]{2,1,0:T(8,128)(2,1)S(1)} %pad_maximum_fusion.refs_1_.refs_9_), channel_id=1, source_target_pairs={{0,1},{1,0},{2,3},{3,2},{4,5},{5,4},{6,7},{7,6},{8,9},{9,8},{10,11... | collective-permute-start | bytes 1572872 | tf_op jit(solution)/shard_map/ppermute | solution.py:21
  21.9 12.9 %collective-permute-start.15 = (bf16[256,512]{1,0:T(8,128)(2,1)S(1)}, bf16[256,512]{1,0:T(8,128)(2,1)S(1)}, u32[]{:S(2)}, u32[]{:S(2)}) collective-permute-start(bf16[256,512]{1,0:T(8,128)(2,1)S(1)} %pad_maximum_fusion.2.refs_1_), channel_id=1, source_target_pairs={{0,224},{32,0},{64,32},{96,64},{128,96},{160,128},{192,160},{224,1... | collective-permute-start | bytes 786440 | tf_op jit(solution)/shard_map/ppermute | solution.py:26
  29.9 11.9 %collective-permute-start.11 = (bf16[512,512]{1,0:T(8,128)(2,1)S(1)}, bf16[512,512]{1,0:T(8,128)(2,1)S(1)}, u32[]{:S(2)}, u32[]{:S(2)}) collective-permute-start(bf16[512,512]{1,0:T(8,128)(2,1)S(1)} %constant_dynamic-slice_fusion), channel_id=1, source_target_pairs={{0,16},{16,0},{1,17},{17,1},{2,18},{18,2},{3,19},{19,3},{4,20},{20... | collective-permute-start | bytes 1572872 | tf_op jit(solution)/shard_map/ppermute | solution.py:21
  31.7 11.6 %collective-permute-start.13 = (bf16[256,512]{1,0:T(8,128)(2,1)}, bf16[256,512]{1,0:T(8,128)(2,1)S(1)}, u32[]{:S(2)}, u32[]{:S(2)}) collective-permute-start(bf16[256,512]{1,0:T(8,128)(2,1)} %collective-permute-done.12.refs_2_), channel_id=1, source_target_pairs={{0,32},{32,64},{64,96},{96,128},{128,160},{160,192},{192,224},{224... | collective-permute-start | bytes 786440 | tf_op jit(solution)/shard_map/ppermute | solution.py:26
  32.4 11.5 %collective-permute-start.9 = (bf16[128,1024]{1,0:T(8,128)(2,1)S(1)}, bf16[128,1024]{1,0:T(8,128)(2,1)S(1)}, u32[]{:S(2)}, u32[]{:S(2)}) collective-permute-start(bf16[128,1024]{1,0:T(8,128)(2,1)S(1)} %slice_bitcast_fusion), channel_id=1, source_target_pairs={{0,6},{2,0},{4,2},{6,4},{1,7},{3,1},{5,3},{7,5},{8,14},{10,8},{12,... | collective-permute-start | bytes 786440 | tf_op jit(solution)/shard_map/ppermute | solution.py:26
  34.9 10.9 %collective-permute-start.8 = (bf16[128,1024]{1,0:T(8,128)(2,1)S(1)}, bf16[128,1024]{1,0:T(8,128)(2,1)S(1)}, u32[]{:S(2)}, u32[]{:S(2)}) collective-permute-start(bf16[128,1024]{1,0:T(8,128)(2,1)S(1)} %slice_bitcast_fusion.1), channel_id=1, source_target_pairs={{0,2},{2,4},{4,6},{6,0},{1,3},{3,5},{5,7},{7,1},{8,10},{10,12},{12... | collective-permute-start | bytes 786440 | tf_op jit(solution)/shard_map/ppermute | solution.py:26
  43.3 7.6 %collective-permute-start.14 = (bf16[256,512]{1,0:T(8,128)(2,1)S(1)}, bf16[256,512]{1,0:T(8,128)(2,1)S(1)}, u32[]{:S(2)}, u32[]{:S(2)}) collective-permute-start(bf16[256,512]{1,0:T(8,128)(2,1)S(1)} %collective-permute-done.13.refs_3_), channel_id=1, source_target_pairs={{0,32},{32,64},{64,96},{96,128},{128,160},{160,192},{192,224},{224... | collective-permute-start | bytes 786440 | tf_op jit(solution)/shard_map/ppermute | solution.py:26
  43.9 40.6 %collective-permute-start.23 = (bf16[512,1024]{1,0:T(8,128)(2,1)S(1)}, bf16[512,1024]{1,0:T(8,128)(2,1)S(1)}, u32[]{:S(2)}, u32[]{:S(2)}) collective-permute-start(bf16[512,1024]{1,0:T(8,128)(2,1)S(1)} %bitcast.37), channel_id=1, source_target_pairs={{0,16},{16,0},{1,17},{17,1},{2,18},{18,2},{3,19},{19,3},{4,20},{20... | collective-permute-start | bytes 3145736 | tf_op jit(solution)/shard_map/ppermute | solution.py:21
  45.8 14.1 %collective-permute-start.5 = (bf16[2,128,1024]{2,1,0:T(8,128)(2,1)}, bf16[2,128,1024]{2,1,0:T(8,128)(2,1)}, u32[]{:S(2)}, u32[]{:S(2)}) collective-permute-start(bf16[2,128,1024]{2,1,0:T(8,128)(2,1)} %copy-done.6), channel_id=1, source_target_pairs={{0,1},{1,0},{2,3},{3,2},{4,5},{5,4},{6,7},{7,6},{8,9},{9,8},{10,11... | collective-permute-start | bytes 1572872 | tf_op jit(solution)/shard_map/ppermute | solution.py:21
  46.6 13.3 %collective-permute-start.7 = (bf16[2,128,1024]{2,1,0:T(8,128)(2,1)}, bf16[2,128,1024]{2,1,0:T(8,128)(2,1)}, u32[]{:S(2)}, u32[]{:S(2)}) collective-permute-start(bf16[2,128,1024]{2,1,0:T(8,128)(2,1)} %copy-done.5), channel_id=1, source_target_pairs={{0,1},{1,0},{2,3},{3,2},{4,5},{5,4},{6,7},{7,6},{8,9},{9,8},{10,11... | collective-permute-start | bytes 1572872 | tf_op jit(solution)/shard_map/ppermute | solution.py:21
  48.2 11.7 %collective-permute-start.10 = (bf16[2,128,1024]{2,1,0:T(8,128)(2,1)}, bf16[2,128,1024]{2,1,0:T(8,128)(2,1)}, u32[]{:S(2)}, u32[]{:S(2)}) collective-permute-start(bf16[2,128,1024]{2,1,0:T(8,128)(2,1)} %pad_maximum_fusion.1.refs_7_.refs_15_), channel_id=1, source_target_pairs={{0,1},{1,0},{2,3},{3,2},{4,5},{5,4},{6,7},{7,6},{8,9},{9,8},{10,11... | collective-permute-start | bytes 1572872 | tf_op jit(solution)/shard_map/ppermute | solution.py:21
  57.3 9.9 %collective-permute-start.22 = (bf16[256,512]{1,0:T(8,128)(2,1)S(1)}, bf16[256,512]{1,0:T(8,128)(2,1)}, u32[]{:S(2)}, u32[]{:S(2)}) collective-permute-start(bf16[256,512]{1,0:T(8,128)(2,1)S(1)} %collective-permute-done.14.refs_10_.refs_4_), channel_id=1, source_target_pairs={{0,32},{32,64},{64,96},{96,128},{128,160},{160,192},{192,224},{224... | collective-permute-start | bytes 786440 | tf_op jit(solution)/shard_map/ppermute | solution.py:26
  73.1 28.2 %collective-permute-start.28 = (bf16[512,1024]{1,0:T(8,128)(2,1)S(1)}, bf16[512,1024]{1,0:T(8,128)(2,1)S(1)}, u32[]{:S(2)}, u32[]{:S(2)}) collective-permute-start(bf16[512,1024]{1,0:T(8,128)(2,1)S(1)} %shard_map.106.refs_1_), channel_id=1, source_target_pairs={{0,16},{16,0},{1,17},{17,1},{2,18},{18,2},{3,19},{19,3},{4,20},{20... | collective-permute-start | bytes 3145736 | tf_op jit(solution)/shard_map/ppermute | solution.py:21
  81.2 7.7 %collective-permute-start.20 = (bf16[256,512]{1,0:T(8,128)(2,1)S(1)}, bf16[256,512]{1,0:T(8,128)(2,1)S(1)}, u32[]{:S(2)}, u32[]{:S(2)}) collective-permute-start(bf16[256,512]{1,0:T(8,128)(2,1)S(1)} %get-tuple-element.33), channel_id=1, source_target_pairs={{0,32},{32,64},{64,96},{96,128},{128,160},{160,192},{192,224},{224... | collective-permute-start | bytes 786440 | tf_op jit(solution)/shard_map/ppermute | solution.py:26
  81.5 7.3 %collective-permute-start.21 = (bf16[256,512]{1,0:T(8,128)(2,1)S(1)}, bf16[256,512]{1,0:T(8,128)(2,1)S(1)}, u32[]{:S(2)}, u32[]{:S(2)}) collective-permute-start(bf16[256,512]{1,0:T(8,128)(2,1)S(1)} %get-tuple-element.34), channel_id=1, source_target_pairs={{0,224},{32,0},{64,32},{96,64},{128,96},{160,128},{192,160},{224,1... | collective-permute-start | bytes 786440 | tf_op jit(solution)/shard_map/ppermute | solution.py:26
  89.0 8.5 %collective-permute-start.24 = (bf16[256,512]{1,0:T(8,128)(2,1)S(1)}, bf16[256,512]{1,0:T(8,128)(2,1)S(1)}, u32[]{:S(2)}, u32[]{:S(2)}) collective-permute-start(bf16[256,512]{1,0:T(8,128)(2,1)S(1)} %get-tuple-element.37), channel_id=1, source_target_pairs={{0,32},{32,64},{64,96},{96,128},{128,160},{160,192},{192,224},{224... | collective-permute-start | bytes 786440 | tf_op jit(solution)/shard_map/ppermute | solution.py:26
  90.3 7.6 %collective-permute-start.25 = (bf16[256,512]{1,0:T(8,128)(2,1)S(1)}, bf16[256,512]{1,0:T(8,128)(2,1)S(1)}, u32[]{:S(2)}, u32[]{:S(2)}) collective-permute-start(bf16[256,512]{1,0:T(8,128)(2,1)S(1)} %get-tuple-element.38), channel_id=1, source_target_pairs={{0,224},{32,0},{64,32},{96,64},{128,96},{160,128},{192,160},{224,1... | collective-permute-start | bytes 786440 | tf_op jit(solution)/shard_map/ppermute | solution.py:26
  97.9 9.7 %collective-permute-start.26 = (bf16[256,512]{1,0:T(8,128)(2,1)S(1)}, bf16[256,512]{1,0:T(8,128)(2,1)S(1)}, u32[]{:S(2)}, u32[]{:S(2)}) collective-permute-start(bf16[256,512]{1,0:T(8,128)(2,1)S(1)} %get-tuple-element.39), channel_id=1, source_target_pairs={{0,32},{32,64},{64,96},{96,128},{128,160},{160,192},{192,224},{224... | collective-permute-start | bytes 786440 | tf_op jit(solution)/shard_map/ppermute | solution.py:26
  100.3 7.3 %collective-permute-start.27 = (bf16[256,512]{1,0:T(8,128)(2,1)S(1)}, bf16[256,512]{1,0:T(8,128)(2,1)S(1)}, u32[]{:S(2)}, u32[]{:S(2)}) collective-permute-start(bf16[256,512]{1,0:T(8,128)(2,1)S(1)} %get-tuple-element.40), channel_id=1, source_target_pairs={{0,224},{32,0},{64,32},{96,64},{128,96},{160,128},{192,160},{224,1... | collective-permute-start | bytes 786440 | tf_op jit(solution)/shard_map/ppermute | solution.py:26
  (19 other events, 267.6 us)
